TPU v7x, 32 devices: a whole 2x2x4 slice. The times are simulated.
32 devices in a mesh: dp: 8 (over y, x, core), feat: 4 (over z).
Axes of the slice: x: 2, y: 2, z: 4, core: 2. Of those that a mesh axis runs over, the one named last changes fastest.
Arguments:
- inputs: float32 [4096, 2048], P('dp', 'feat'), may hold values from -6 to 6
- partner_bits: int32 [4, 2], P('feat'), may hold values from 0 to 1, each once within a row
- block_weights: float32 [4, 512, 3, 512], P('feat', 'dp'), may hold values from -0.15625 to 0.15625
- low_left: float32 [4, 512, 256], P('feat', 'dp'), may hold values from -0.125 to 0.125
- low_right: float32 [4, 256, 512], P('feat', 'dp'), may hold values from -0.375 to 0.375
- cotangent: float32 [4096, 2048], P('dp', 'feat'), may hold values from -6 to 6
Outputs:
- outputs: float32 [4096, 2048], P('dp', 'feat')
- input_grad: float32 [4096, 2048], P('dp', 'feat')
- block_grads: float32 [4, 512, 3, 512], P('feat', 'dp')
- left_grads: float32 [4, 512, 256], P('feat', 'dp')
- right_grads: float32 [4, 256, 512], P('feat', 'dp')
Inputs may be any that keep to these rules, and one draw needn't show every extreme that they name: `partner_bits`: each row holds every bit number 0 .. 1 once.
All inputs are finite; a program needn't handle non-finite values.
Results may differ from a plain program's by a relative error of at most 0.000086.
Values sent between devices are 32-bit elements; how exact they have to be, the bound alone decides.
No kernel may reach another device: no remote copies, remote signals or barrier semaphores. Data moves between devices by JAX's collectives and lax.ppermute only.
A program may use at most 128 MiB of HBM per device.

v0:
```python
import math

import jax
import jax.numpy as jnp
from jax import lax
from jax.sharding import PartitionSpec as P


def swapped(block, axis, apart):
    count = lax.axis_size(axis)
    route = []
    for low in range(count):
        high = low | 1 << apart
        if high != low and high < count:
            route += [(low, high), (high, low)]
    return lax.ppermute(block, axis, route)


def on_device(inputs, partner_bits, block_weights, low_left, low_right, cotangent):
    highest = lax.Precision.HIGHEST
    row_count, block = inputs.shape
    sections = partner_bits.shape[1]
    my_bits = partner_bits[0]
    arrived = []
    for level in range(sections):
        arrived.append(swapped(inputs, "feat", level))
    by_bit = jnp.stack(arrived)
    sources = jnp.concatenate([inputs[None], by_bit[my_bits]], axis=0)
    bit_numbers = jnp.arange(sections, dtype=jnp.int32)
    matches = (my_bits[:, None] == bit_numbers[None, :]).astype(jnp.int32)
    slot_of_bit = jnp.sum(matches * bit_numbers[:, None], axis=0)
    left_full, right_full = (
        lax.all_gather(low_left, "dp", axis=1, tiled=True),
        lax.all_gather(low_right, "dp", axis=1, tiled=True),
    )
    left_full = left_full[0]
    right_full = right_full[0]
    code_part = jnp.dot(inputs, left_full, precision=highest, preferred_element_type=jnp.float32)
    code_grad_part = jnp.dot(
        cotangent, right_full.T, precision=highest, preferred_element_type=jnp.float32
    )
    codes = lax.psum(code_part, "feat")
    full_weights = lax.all_gather(block_weights, "dp", axis=1, tiled=True)[0]
    sparse = jnp.einsum("sri,iso->ro", sources, full_weights, precision=highest)
    outputs = sparse + jnp.dot(
        codes, right_full, precision=highest, preferred_element_type=jnp.float32
    )
    code_grads = lax.psum(code_grad_part, "feat")
    weights_back = lax.all_gather(block_weights, "dp", axis=1, tiled=True)[0]
    products = jnp.einsum("ro,iso->sri", cotangent, weights_back, precision=highest)
    grad_scale = 1.0 / math.sqrt(row_count * lax.axis_size("dp"))
    block_grad = jnp.einsum("sri,ro->iso", sources, cotangent, precision=highest) * grad_scale
    right_grad = (
        jnp.dot(codes.T, cotangent, precision=highest, preferred_element_type=jnp.float32)
        * grad_scale
    )
    left_grad = (
        jnp.dot(inputs.T, code_grads, precision=highest, preferred_element_type=jnp.float32)
        * grad_scale
    )
    input_grad = products[0] + jnp.dot(
        code_grads, left_full.T, precision=highest, preferred_element_type=jnp.float32
    )
    for level in range(sections):
        outgoing = products[1 + slot_of_bit[level]]
        input_grad = input_grad + swapped(outgoing, "feat", level)
    block_grads, left_grads, right_grads = (
        lax.psum_scatter(block_grad[None], "dp", scatter_dimension=1, tiled=True),
        lax.psum_scatter(left_grad[None], "dp", scatter_dimension=1, tiled=True),
        lax.psum_scatter(right_grad[None], "dp", scatter_dimension=1, tiled=True),
    )
    return (outputs, input_grad, block_grads, left_grads, right_grads)


def solution(mesh):
    in_specs = (
        P("dp", "feat"),
        P("feat", None),
        P("feat", "dp", None, None),
        P("feat", "dp", None),
        P("feat", "dp", None),
        P("dp", "feat"),
    )
    out_specs = (
        P("dp", "feat"),
        P("dp", "feat"),
        P("feat", "dp", None, None),
        P("feat", "dp", None),
        P("feat", "dp", None),
    )
    return jax.shard_map(
        on_device, mesh=mesh, in_specs=in_specs, out_specs=out_specs, check_vma=False
    )
```

profile of v0, /device:TPU:0, one launch (start us, length us, event | category | flops | bytes accessed | tf_op | source)
XLA Modules:
  0.0 277.6 jit_solution(13523292206942892220)
XLA Ops:
  8.0 0.0 copy-start
  8.0 0.0 copy-start.1
  8.0 0.0 all-reduce.7.cloned.1.call-start
  8.1 11.7 %all_gather.11 = f32[1,512,256]{2,1,0:T(8,128)S(1)} all-gather(f32[1,64,256]{2,1,0:T(8,128)} %param.9), channel_id=1, replica_groups=mesh['dp'=8,'feat'=4] {'dp'}, dimensions={1}, use_global_device_ids=true | all-gather | bytes 589824 | tf_op jit(solution)/shard_map/all_gather | solution.py:33
  19.8 9.5 %all_gather.12 = f32[1,256,512]{2,1,0:T(8,128)S(1)} all-gather(f32[1,32,512]{2,1,0:T(8,128)} %param.10), channel_id=1, replica_groups=mesh['dp'=8,'feat'=4] {'dp'}, dimensions={1}, use_global_device_ids=true | all-gather | bytes 589824 | tf_op jit(solution)/shard_map/all_gather | solution.py:34
  29.3 0.8 copy-done.5
  30.2 1.8 fusion.17
  32.0 1.8 fusion.22
  33.8 0.0 all-reduce.7.cloned.1.call-update
  33.8 0.0 all-gather.2.cloned.1.call-start
  33.9 0.5 all-gather.2.cloned.1.call-update
  34.4 0.0 all-reduce.5.cloned.1.call-start
  34.4 2.7 collective-permute-start.1
  37.1 1.6 collective-permute-start
  38.7 87.0 %all-reduce.7.cloned.1.call-done = (f32[512,256]{1,0:T(8,128)}, f32[512,256]{1,0:T(8,128)}) async-done(((f32[512,256]{1,0:T(8,128)}, f32[512,256]{1,0:T(8,128)}), (f32[512,256]{1,0:T(8,128)}, f32[512,256]{1,0:T(8,128)})) %all-reduce.7.cloned.1.call-update) | async-done | bytes 1048592 | tf_op jit(solution)/shard_map/psum | solution.py:42
  125.6 2.2 fusion.14
  127.8 1.0 copy.22
  128.8 0.0 all-reduce.5.cloned.1.call-update
  128.9 0.0 reduce-scatter.5.cloned.1.call-start
  128.9 1.9 fusion.13
  130.8 0.0 reduce-scatter.5.cloned.1.call-update
  130.8 0.2 reduce-scatter.3.cloned.1.call-start
  131.1 0.0 collective-permute-done.1
  131.1 0.0 collective-permute-done
  131.1 3.1 %pad_maximum_fusion.3 = f32[2,512,512]{2,1,0:T(8,128)} fusion(f32[1,512,512]{2,1,0:T(8,128)} %bitcast.2, f32[1,512,512]{2,1,0:T(8,128)} %bitcast.1), kind=kLoop, calls=%fused_computation.8 | loop fusion | flops 524288 | bytes 4194304 | tf_op jit(solution)/shard_map/stack | solution.py:27
  134.2 2.3 gather_fusion
  136.5 8.0 %multiply_bitcast_fusion = f32[1,512,3,512]{3,1,2,0:T(8,128)} fusion(f32[2,512,512]{2,1,0:T(8,128)S(1)} %gather_fusion, f32[1,512,512]{2,1,0:T(8,128)} %bitcast.72, f32[512,512]{1,0:T(8,128)S(1)} %copy-done), kind=kOutput, calls=%fused_computation.6 | convolution fusion | flops 4833411072 | bytes 7340032 | tf_op jit(solution)/shard_map/sri,ro->iso/dot_general | solution.py:52
  144.5 0.0 reduce-scatter.3.cloned.1.call-update
  144.5 0.1 fusion.24
  144.6 0.6 fusion.28
  147.8 0.0 all-gather.2.cloned.1.call-done
  147.8 7.4 %fusion = f32[512,3,512]{2,0,1:T(8,128)S(1)} fusion(f32[1,512,3,512]{3,1,2,0:T(8,128)} %all-gather.2.cloned.1.call-done, f32[512,512]{1,0:T(8,128)S(1)} %copy-done), kind=kOutput, calls=%fused_computation.2 | convolution fusion | flops 4831838208 | bytes 7340032 | tf_op jit(solution)/shard_map/ro,iso->sri/dot_general | solution.py:50
  155.2 1.7 copy-done.2
  156.9 1.6 dynamic-slice_bitcast_fusion.1
  158.5 1.3 collective-permute-start.2
  159.8 1.0 collective-permute-start.3
  160.8 0.6 dynamic-slice.8
  162.1 3.4 %fusion.19 = f32[512,512]{1,0:T(8,128)} fusion(f32[512,256]{1,0:T(8,128)} %get-tuple-element.20, f32[1,256,512]{2,1,0:T(8,128)} %copy-done.5), kind=kOutput, calls=%fused_computation.25 | convolution fusion | flops 805306368 | bytes 2097152 | tf_op jit(solution)/shard_map/dot_general | solution.py:45
  165.5 16.9 %all-reduce.5.cloned.1.call-done = f32[1,512,256]{2,0,1:T(1,128)} async-done(((f32[1,512,256]{2,0,1:T(1,128)}), f32[1,512,256]{2,0,1:T(1,128)}) %all-reduce.5.cloned.1.call-update) | async-done | bytes 524304
  182.4 0.8 constant_dynamic-slice_fusion
  183.2 0.6 copy.24
  183.9 8.0 %fusion.10 = f32[512,512]{1,0:T(8,128)} fusion(f32[512,512]{1,0:T(8,128)} %fusion.19, f32[1,512,3,512]{3,1,2,0:T(8,128)} %all-gather.2.cloned.1.call-done, f32[2,512,512]{2,1,0:T(8,128)S(1)} %gather_fusion, f32[1,512,512]{2,1,0:T(8,128)} %bitcast.73), kind=kOutput, calls=%fused_computation.13 | convolution fusion | flops 4832886784 | bytes 8388608 | tf_op jit(solution)/shard_map/sri,iso->ro/dot_general | solution.py:44
  191.9 14.2 %collective-permute-done.2 = f32[512,512]{0,1:T(8,128)} collective-permute-done((f32[512,512]{0,1:T(8,128)}, f32[512,512]{0,1:T(8,128)}, u32[]{:S(2)}, u32[]{:S(2)}) %collective-permute-start.2) | collective-permute-done | bytes 1048608 | tf_op jit(solution)/shard_map/ppermute | solution.py:16
  206.0 1.9 collective-permute-done.3
  208.0 3.0 %fusion.9 = f32[512,512]{0,1:T(8,128)S(1)} fusion(f32[512,512]{0,1:T(8,128)} %collective-permute-done.3, f32[512,512]{0,1:T(8,128)} %collective-permute-done.2, f32[512,256]{1,0:T(8,128)S(1)} %copy-done.6, f32[3,512,512]{1,2,0:T(8,128)} %bitcast.74, f32[1,512,256]{2,1,0:T(8,128)S(1)} %copy-done.4), kind=kOutput, calls=%fused_computation.12 | convolution fusion | flops 806092800 | bytes 5242880 | tf_op jit(solution)/shard_map/dot_general | solution.py:61
  211.0 1.3 copy.23
  212.3 7.3 %reduce-scatter.5.cloned.1.call-done = f32[1,32,512]{2,1,0:T(8,128)} async-done(((f32[1,256,512]{2,1,0:T(8,128)}), f32[1,32,512]{2,1,0:T(8,128)}) %reduce-scatter.5.cloned.1.call-update) | async-done | bytes 65552 | tf_op jit(solution)/shard_map/reduce_scatter | solution.py:70
  219.5 50.5 %reduce-scatter.3.cloned.1.call-done = f32[1,64,3,512]{3,1,2,0:T(8,128)} async-done(((f32[1,512,3,512]{3,1,2,0:T(8,128)}), f32[1,64,3,512]{3,1,2,0:T(8,128)}) %reduce-scatter.3.cloned.1.call-update) | async-done | bytes 393232 | tf_op jit(solution)/shard_map/reduce_scatter | solution.py:68
  (18 shorter events, 0.0 us)
Async XLA Ops:
  8.0 22.2 %copy-start = (f32[512,512]{1,0:T(8,128)S(1)}, f32[512,512]{1,0:T(8,128)}, u32[]{:S(2)}) copy-start(f32[512,512]{1,0:T(8,128)} %param.11) | copy-start | bytes 3145732
  8.0 24.0 %copy-start.1 = (f32[512,512]{1,0:T(8,128)S(1)}, f32[512,512]{1,0:T(8,128)}, u32[]{:S(2)}) copy-start(f32[512,512]{1,0:T(8,128)} %param.6) | copy-start | bytes 3145732
  8.0 117.6 %all-reduce.7.cloned.1.call-start = ((), (), s32[]{:S(2)}) async-start(), calls=%async_computation.6 | async-start | bytes 2097152 | tf_op jit(solution)/shard_map/psum | solution.py:42
  19.8 12.2 %copy-start.3 = (f32[1,512,256]{2,1,0:T(8,128)}, f32[1,512,256]{2,1,0:T(8,128)S(1)}, u32[]{:S(2)}) copy-start(f32[1,512,256]{2,1,0:T(8,128)S(1)} %all_gather.11) | copy-start | bytes 1572868
  29.3 0.8 copy-start.5
  33.8 114.0 %all-gather.2.cloned.1.call-start = ((), (), s32[]{:S(2)}) async-start(), calls=%async_computation.2 | async-start | bytes 3538944 | tf_op jit(solution)/shard_map/all_gather | solution.py:43
  34.4 148.0 %all-reduce.5.cloned.1.call-start = ((), (), s32[]{:S(2)}) async-start(), calls=%async_computation.5 | async-start | bytes 1048576
  34.4 96.7 %collective-permute-start.1 = (f32[512,512]{1,0:T(8,128)S(1)}, f32[512,512]{1,0:T(8,128)}, u32[]{:S(2)}, u32[]{:S(2)}) collective-permute-start(f32[512,512]{1,0:T(8,128)S(1)} %copy-done.1), channel_id=1, source_target_pairs={{0,2},{2,0},{1,3},{3,1},{4,6},{6,4},{5,7},{7,5},{8,10},{10,8},{9,1... | collective-permute-start | bytes 3145736 | tf_op jit(solution)/shard_map/ppermute | solution.py:16
  37.1 94.0 %collective-permute-start = (f32[512,512]{1,0:T(8,128)S(1)}, f32[512,512]{1,0:T(8,128)}, u32[]{:S(2)}, u32[]{:S(2)}) collective-permute-start(f32[512,512]{1,0:T(8,128)S(1)} %copy-done.1), channel_id=1, source_target_pairs={{0,1},{1,0},{2,3},{3,2},{4,5},{5,4},{6,7},{7,6},{8,9},{9,8},{10,11... | collective-permute-start | bytes 3145736 | tf_op jit(solution)/shard_map/ppermute | solution.py:16
  125.6 3.3 %copy-start.7 = (f32[512,256]{1,0:T(8,128)S(1)}, f32[512,256]{1,0:T(8,128)}, u32[]{:S(2)}) copy-start(f32[512,256]{1,0:T(8,128)} %get-tuple-element.20) | copy-start | bytes 1572868
  125.6 5.4 %copy-start.8 = (s32[1,2]{1,0:T(1,128)S(1)}, s32[1,2]{1,0:T(1,128)}, u32[]{:S(2)}) copy-start(s32[1,2]{1,0:T(1,128)} %param.7) | copy-start | bytes 28
  128.9 90.6 %reduce-scatter.5.cloned.1.call-start = ((), (), s32[]{:S(2)}) async-start(), calls=%async_computation.4 | async-start | bytes 589824 | tf_op jit(solution)/shard_map/reduce_scatter | solution.py:70
  130.8 139.1 %reduce-scatter.3.cloned.1.call-start = ((), (), s32[]{:S(2)}) async-start(), calls=%async_computation.3 | async-start | bytes 3538944 | tf_op jit(solution)/shard_map/reduce_scatter | solution.py:68
  155.2 1.7 copy-start.2
  156.9 4.0 %copy-start.9 = (u32[32]{0:T(128)S(1)}, u32[32]{0:T(128)}, u32[]{:S(2)}) copy-start(u32[32]{0:T(128)} %constant.26) | copy-start | bytes 388
  158.5 47.5 %collective-permute-start.2 = (f32[512,512]{0,1:T(8,128)}, f32[512,512]{0,1:T(8,128)}, u32[]{:S(2)}, u32[]{:S(2)}) collective-permute-start(f32[512,512]{0,1:T(8,128)} %get-tuple-element.22), channel_id=1, source_target_pairs={{0,1},{1,0},{2,3},{3,2},{4,5},{5,4},{6,7},{7,6},{8,9},{9,8},{10,11... | collective-permute-start | bytes 3145736 | tf_op jit(solution)/shard_map/ppermute | solution.py:16
  159.8 48.2 %collective-permute-start.3 = (f32[512,512]{0,1:T(8,128)}, f32[512,512]{0,1:T(8,128)}, u32[]{:S(2)}, u32[]{:S(2)}) collective-permute-start(f32[512,512]{0,1:T(8,128)} %get-tuple-element.23), channel_id=1, source_target_pairs={{0,2},{2,0},{1,3},{3,1},{4,6},{6,4},{5,7},{7,5},{8,10},{10,8},{9,1... | collective-permute-start | bytes 3145736 | tf_op jit(solution)/shard_map/ppermute | solution.py:16
  183.9 24.1 %copy-start.4 = (f32[1,512,256]{2,1,0:T(8,128)S(1)}, f32[1,512,256]{2,1,0:T(8,128)}, u32[]{:S(2)}) copy-start(f32[1,512,256]{2,1,0:T(8,128)} %copy-done.3) | copy-start | bytes 1572868
  183.9 24.1 %copy-start.6 = (f32[512,256]{1,0:T(8,128)S(1)}, f32[512,256]{1,0:T(8,128)}, u32[]{:S(2)}) copy-start(f32[512,256]{1,0:T(8,128)} %get-tuple-element.21) | copy-start | bytes 1572868
Sparse Core Ops, SparseCore 0:
  33.9 91.6 all-reduce.6
Sparse Core Ops, SparseCore 1:
  36.3 32.4 all-gather.1
  129.0 53.4 all-reduce.4
  185.9 33.6 reduce-scatter.4
  223.9 46.0 reduce-scatter.2
where the time goes:
time: 278 us
  waiting for transfers between devices  178 us (64%)
  matrix products  37.4 us (13%)
  blocking collectives  21.3 us (8%)
  between operations  19.1 us (7%)
  local copies, waits for them, and re-layouts  11.4 us (4%)
  starting transfers between devices  6.96 us (3%)
  other arithmetic  3.17 us (1%)
    psum x1, waiting for transfers between devices, on_device(): codes = lax.psum(code_part, 'feat')  87 us
    reduce_scatter x1, waiting for transfers between devices, on_device(): lax.psum_scatter(block_grad[None], 'dp', scatter_dimension=1, tiled=True)  50.5 us
    unnamed x6, waiting for transfers between devices  17.5 us
    ppermute x4, waiting for transfers between devices, swapped(): return lax.ppermute(block, axis, route)  16.1 us
    all_gather x1, blocking collectives, on_device(): lax.all_gather(low_left, 'dp', axis=1, tiled=True)  11.7 us
    all_gather x1, blocking collectives, on_device(): lax.all_gather(low_right, 'dp', axis=1, tiled=True)  9.53 us
    dot_general x1, matrix products, on_device(): sparse = jnp.einsum('sri,iso->ro', sources, full_weights, precision=highest)  8.01 us
    dot_general x1, matrix products, on_device(): jnp.einsum('sri,ro->iso', sources, cotangent, precision=highest)  8 us
  transfers between devices with their start and end apart: 9, of which 6 were waited for; matrix products, arithmetic and copies ran while one was open for 17% of the time, Pallas kernels for 0%

commit v1 on v0

v1 whole, which is shorter than its diff:
```python
import functools
import math

import jax
import jax.numpy as jnp
from jax import lax
from jax.experimental import pallas as pl
from jax.experimental.pallas import tpu as pltpu
from jax.sharding import PartitionSpec as P

F32 = jnp.float32
BF16 = jnp.bfloat16
VMEM_BYTES = 40 * 1024 * 1024
TOKEN_BLOCK = 256


def across(block, axis, apart):
    count = lax.axis_size(axis)
    return lax.ppermute(block, axis, [(i, i ^ apart) for i in range(count)])


def split(value):
    high = value.astype(BF16)
    return high, (value - high.astype(F32)).astype(BF16)


def dot3(left, right, over):
    def one(a, b):
        return lax.dot_general(
            a, b, ((over[:1], over[1:]), ((), ())), preferred_element_type=F32
        )

    return one(left[0], right[0]) + (one(left[0], right[1]) + one(left[1], right[0]))


def nn(left, right):
    return dot3(left, right, (1, 0))


def nt(left, right):
    return dot3(left, right, (1, 1))


def tn(left, right):
    return dot3(left, right, (0, 0))


def call(kernel, out_shapes, operands, grid=None, in_specs=None, out_specs=None, scratch=()):
    vmem = pl.BlockSpec(memory_space=pltpu.VMEM)
    kwargs = {}
    if grid is None:
        in_specs = in_specs or [vmem] * len(operands)
        out_specs = [vmem] * len(out_shapes)
    else:
        kwargs["grid"] = grid
    return pl.pallas_call(
        kernel,
        out_shape=out_shapes,
        in_specs=in_specs,
        out_specs=out_specs,
        scratch_shapes=list(scratch),
        cost_estimate=pl.CostEstimate(flops=1, bytes_accessed=1, transcendentals=0),
        compiler_params=pltpu.CompilerParams(vmem_limit_bytes=VMEM_BYTES),
        **kwargs,
    )(*operands)


def f32(*shape):
    return jax.ShapeDtypeStruct(shape, F32)


def b16(*shape):
    return jax.ShapeDtypeStruct(shape, BF16)


def whole(shape):
    return pl.BlockSpec(shape, lambda *_: (0,) * len(shape))


def by_tokens(tokens, width):
    return pl.BlockSpec((tokens, width), lambda i: (i, 0))


def slot_weights(bits_ref, w_ref, bit, sections):
    chosen = w_ref[0, sections]
    for s in range(sections - 1):
        chosen = jnp.where(bits_ref[0, s] == bit, w_ref[0, 1 + s], chosen)
    return chosen


def put_left(out_ref, left, block):
    rows, rank = left.shape
    pieces = block // rank
    step = rows // pieces
    for p in range(pieces):
        out_ref[:step, p * rank : (p + 1) * rank] = left[p * step : (p + 1) * step]


def pack_kernel(bits_ref, w_ref, left_ref, right_ref, x_ref, g_ref, near_ref, far_ref, own_ref):
    _, slots, rows, block = w_ref.shape
    sections = slots - 1
    rank_rows = right_ref.shape[1]
    flat = far_ref.shape[0] - x_ref.shape[0]
    near_ref[:rows] = slot_weights(bits_ref, w_ref, 0, sections)
    near_ref[rows : rows + rank_rows] = right_ref[0]
    near_ref[rows + rank_rows :] = g_ref[...]
    put_left(far_ref.at[:flat], left_ref[0], block)
    far_ref[flat:] = x_ref[...]
    own_ref[:rows] = w_ref[0, 0]
    for b in range(1, sections):
        own_ref[b * rows : (b + 1) * rows] = slot_weights(bits_ref, w_ref, b, sections)
    at = sections * rows
    own_ref[at : at + rank_rows] = right_ref[0]
    put_left(own_ref.at[at + rank_rows :], left_ref[0], block)


def before_kernel(sizes, *refs):
    sections, rows, rank_rows, rank, dp_count = sizes
    even_ref, odd_ref, x_ref, g_ref = refs[:4]
    wh, wl, rh, rl, lh, ll, c_ref, cg_ref, ahead_ref, *back_refs = refs[4:]
    block = x_ref.shape[1]
    flat = rows * rank // block
    pieces = rows // flat

    @pl.when(pl.program_id(0) == 0)
    def _():
        me = lax.axis_index("dp")
        for k in range(dp_count):
            part = (odd_ref if k % 2 else even_ref).at[k // 2]
            owner = me ^ k
            at = 0

            def move(high_ref, low_ref, i, start, count, value):
                high, low = split(value)
                place = pl.ds(pl.multiple_of(start, 16), count)
                high_ref[i, place, :] = high
                low_ref[i, place, :] = low

            def move_wide(high_ref, low_ref, i, start, count):
                move(high_ref, low_ref, i, owner * count, count, part[start : start + count, :])
                return start + count

            def move_left(i, start):
                for p in range(pieces):
                    value = part[start : start + flat, p * rank : (p + 1) * rank]
                    move(lh, ll, i, owner * rows + p * flat, flat, value)
                return start + flat

            for i in range(sections):
                at = move_wide(wh, wl, i, at, rows)
            at = move_wide(rh, rl, 0, at, rank_rows)
            at = move_left(0, at)
            at = move_wide(wh, wl, sections, at, rows)
            at = move_wide(rh, rl, 1, at, rank_rows)
            at = move_left(1, at)

    x, g = split(x_ref[...]), split(g_ref[...])
    c_ref[...] = nn(x, (lh[0], ll[0]))
    cg_ref[...] = nt(g, (rh[0], rl[0]))
    ahead_ref[...] = nn(x, (wh[sections], wl[sections]))
    for b in range(1, sections):
        back_refs[b - 1][...] = nt(g, (wh[b], wl[b]))


def codes_kernel(far_ref, near_ref, lh, ll, rh, rl, c0_ref, cg0_ref, c_ref, cg_ref):
    c_ref[...] = c0_ref[...] + nn(split(far_ref[...]), (lh[1], ll[1]))
    cg_ref[...] = cg0_ref[...] + nt(split(near_ref[...]), (rh[1], rl[1]))


def send_kernel(lh, ll, rh, rl, c_ref, cg_ref, back0_ref, ahead0_ref, back_ref, ahead_ref):
    back_ref[...] = back0_ref[...] + nt(split(cg_ref[...]), (lh[1], ll[1]))
    ahead_ref[...] = ahead0_ref[...] + nn(split(c_ref[...]), (rh[1], rl[1]))


def codes_send_kernel(
    far_ref, near_ref, lh, ll, rh, rl, c0_ref, cg0_ref, back0_ref, ahead0_ref,
    c_ref, cg_ref, back_ref, ahead_ref,
):
    codes_kernel(far_ref, near_ref, lh, ll, rh, rl, c0_ref, cg0_ref, c_ref, cg_ref)
    send_kernel(lh, ll, rh, rl, c_ref, cg_ref, back0_ref, ahead0_ref, back_ref, ahead_ref)


def grads_kernel(sizes, scale, *refs):
    sections, rows, rank_rows, rank, dp_count = sizes
    x_ref, g_ref, near_ref, c_ref, cg_ref, *rest = refs
    far_refs = rest[: sections - 1]
    half = dp_count // 2
    keep_refs = rest[sections - 1 : sections - 1 + half]
    give_ref = rest[sections - 1 + half]
    dw, dr, dl = rest[sections + half :]
    block = x_ref.shape[1]
    flat = rows * rank // block
    pieces = rows // flat
    me = lax.axis_index("dp")
    at = [0]

    def spread(count, read):
        for k in range(dp_count):
            place = pl.ds(pl.multiple_of((me ^ k) * count, 8), count)
            if k % 2:
                read(give_ref.at[k // 2], at[0], place)
            else:
                read(keep_refs[k // 2], at[0], place)

    def spread_wide(source, count):
        def read(out, start, place):
            out[start : start + count, :] = source[place, :]

        spread(count, read)
        at[0] += count

    def spread_left(source):
        def read(out, start, place):
            value = source[place, :]
            for p in range(pieces):
                out[start : start + flat, p * rank : (p + 1) * rank] = value[
                    p * flat : (p + 1) * flat
                ]

        spread(rows, read)
        at[0] += flat

    x, g, near = split(x_ref[...]), split(g_ref[...]), split(near_ref[...])
    c, cg = split(c_ref[...]), split(cg_ref[...])
    far = [split(r[...]) for r in far_refs]
    dw[...] = tn(x, near) * scale
    spread_wide(dw, rows)
    dr[...] = tn(c, near) * scale
    spread_wide(dr, rank_rows)
    dl[...] = tn(far[0], cg) * scale
    spread_left(dl)
    dw[...] = tn(x, g) * scale
    spread_wide(dw, rows)
    for b in range(1, sections):
        dw[...] = tn(far[b - 1], g) * scale
        spread_wide(dw, rows)
    dr[...] = tn(c, g) * scale
    spread_wide(dr, rank_rows)
    dl[...] = tn(x, cg) * scale
    spread_left(dl)


def local_kernel(sections, *refs):
    x_ref, g_ref, near_ref, c_ref, cg_ref, *rest = refs
    far_refs = rest[: sections - 1]
    wh, wl, rh, rl, lh, ll, out_ref, grad_ref = rest[sections - 1 :]
    out = nn(split(x_ref[...]), (wh[0], wl[0])) + nn(split(c_ref[...]), (rh[0], rl[0]))
    for b in range(1, sections):
        out += nn(split(far_refs[b - 1][...]), (wh[b], wl[b]))
    out_ref[...] = out
    grad = nt(split(g_ref[...]), (wh[0], wl[0])) + nt(split(cg_ref[...]), (lh[0], ll[0]))
    grad_ref[...] = grad + nt(split(near_ref[...]), (wh[sections], wl[sections]))


def place_kernel(sizes, *refs):
    sections, rows, rank_rows, rank, _ = sizes
    bits_ref, kept_ref, near_ref, far_ref, w_ref, left_ref, right_ref = refs
    block = kept_ref.shape[1]
    flat = rows * rank // block
    pieces = rows // flat
    w_ref[0, 0] = kept_ref[:rows]
    for s in range(sections):
        chosen = near_ref[:rows]
        for b in range(1, sections):
            chosen = jnp.where(bits_ref[0, s] == b, kept_ref[b * rows : (b + 1) * rows], chosen)
        w_ref[0, 1 + s] = chosen
    at = sections * rows
    right_ref[0] = kept_ref[at : at + rank_rows] + near_ref[rows:]
    at += rank_rows
    for p in range(pieces):
        columns = slice(p * rank, (p + 1) * rank)
        left_ref[0, p * flat : (p + 1) * flat, :] = (
            kept_ref[at : at + flat, columns] + far_ref[:, columns]
        )


def on_device(inputs, partner_bits, block_weights, low_left, low_right, cotangent):
    tokens, block = inputs.shape
    sections = partner_bits.shape[1]
    dp_count = lax.axis_size("dp")
    half = dp_count // 2
    rows, rank = low_left.shape[1:]
    rank_rows = low_right.shape[1]
    all_rank = rank_rows * dp_count
    flat = rows * rank // block
    sizes = (sections, rows, rank_rows, rank, dp_count)
    step = min(tokens, TOKEN_BLOCK)
    grid = (tokens // step,)
    smem = pl.BlockSpec(memory_space=pltpu.SMEM)
    vmem = pl.BlockSpec(memory_space=pltpu.VMEM)

    lent_rows = rows + rank_rows
    early = tokens // 4
    by_slot = jnp.transpose(block_weights, (0, 2, 1, 3))
    own_rows = sections * rows + rank_rows + flat
    out_near, out_far, own = call(
        pack_kernel,
        [f32(lent_rows + early, block), f32(flat + early, block), f32(own_rows, block)],
        [partner_bits, by_slot, low_left, low_right, inputs, cotangent],
        grid=(1,),
        in_specs=[
            smem, whole(by_slot.shape), whole(low_left.shape), whole(low_right.shape),
            whole((early, block)), whole((early, block)),
        ],
        out_specs=[
            whole((lent_rows + early, block)), whole((flat + early, block)),
            whole((own_rows, block)),
        ],
    )
    got_near = across(out_near, "feat", 1)
    got_far = across(out_far, "feat", 2)
    own = [own] + [across(own, "dp", k) for k in range(2, dp_count, 2)]
    late_x, late_g, got_near, got_far = lax.optimization_barrier(
        (inputs[early:], cotangent[early:], got_near, got_far)
    )
    far = [jnp.concatenate([got_far[flat:], across(late_x, "feat", 2)])]
    far += [across(inputs, "feat", 1 << b) for b in range(2, sections)]
    near = jnp.concatenate([got_near[lent_rows:], across(late_g, "feat", 1)])

    packed_rows = (sections + 1) * rows + 2 * rank_rows + 2 * flat
    w_shape = (sections + 1, block, block)
    r_shape = (2, all_rank, block)
    l_shape = (2, block, rank)
    shapes = [w_shape, w_shape, r_shape, r_shape, l_shape, l_shape]
    wide, thin = by_tokens(step, block), by_tokens(step, rank)
    made = (
        [b16(*s) for s in shapes] + [f32(tokens, rank)] * 2 + [f32(tokens, block)] * sections
    )
    usual = partner_bits[0, 0] >= 0

    def prepare(own, got_near, got_far, inputs, cotangent):
        lent = jnp.concatenate([got_near[:lent_rows], got_far[:flat]])
        lent = [lent] + [across(lent, "dp", k) for k in range(2, dp_count, 2)]
        even = jnp.stack([jnp.concatenate(pair) for pair in zip(own, lent)])
        odd = across(even, "dp", 1)
        return tuple(call(
            functools.partial(before_kernel, sizes),
            [b16(*s) for s in shapes]
            + [f32(tokens, rank)] * 2
            + [f32(tokens, block)] * sections,
            [even, odd, inputs, cotangent],
            grid=grid,
            in_specs=[whole((half, packed_rows, block))] * 2 + [wide, wide],
            out_specs=[whole(s) for s in shapes] + [thin, thin] + [wide] * sections,
        ))

    def empty(*_):
        return tuple(jnp.zeros(s.shape, s.dtype) for s in made)

    wh, wl, rh, rl, lh, ll, codes, code_grads, ahead, *back = lax.cond(
        usual, prepare, empty,
        own, got_near, got_far, inputs, cotangent,
    )
    low_specs = [whole(l_shape), whole(l_shape), whole(r_shape), whole(r_shape)]
    low = [lh, ll, rh, rl]
    if sections == 2:
        codes, code_grads, back[0], ahead = call(
            codes_send_kernel,
            [f32(tokens, rank)] * 2 + [f32(tokens, block)] * 2,
            [far[0], near, *low, codes, code_grads, back[0], ahead],
            grid=grid,
            in_specs=[wide, wide, *low_specs, thin, thin, wide, wide],
            out_specs=[thin, thin, wide, wide],
        )
    else:
        codes, code_grads = call(
            codes_kernel,
            [f32(tokens, rank)] * 2,
            [far[0], near, *low, codes, code_grads],
            grid=grid,
            in_specs=[wide, wide, *low_specs, thin, thin],
            out_specs=[thin, thin],
        )
        for b in range(2, sections):
            codes = codes + across(codes, "feat", 1 << b)
            code_grads = code_grads + across(code_grads, "feat", 1 << b)
        back[0], ahead = call(
            send_kernel,
            [f32(tokens, block)] * 2,
            [*low, codes, code_grads, back[0], ahead],
            grid=grid,
            in_specs=[*low_specs, thin, thin, wide, wide],
            out_specs=[wide, wide],
        )
    back = [across(back[b - 1], "feat", 1 << b) for b in range(1, sections)]
    ahead = across(ahead, "feat", 1)

    scale = 1.0 / math.sqrt(tokens * dp_count)

    def finish(inputs, cotangent, near, codes, code_grads, far, weights):
        *keep, give = call(
            functools.partial(grads_kernel, sizes, scale),
            [f32(packed_rows, block)] * half + [f32(half, packed_rows, block)],
            [inputs, cotangent, near, codes, code_grads, *far],
            scratch=[
                pltpu.VMEM((block, block), F32),
                pltpu.VMEM((all_rank, block), F32),
                pltpu.VMEM((block, rank), F32),
            ],
        )
        codes, code_grads, give = lax.optimization_barrier((codes, code_grads, give))
        got = across(give, "dp", 1)
        summed = [keep[m] + got[m] for m in range(half)]
        total = summed[0]
        for m in range(1, half):
            total = total + across(summed[m], "dp", 2 * m)
        out, grad = call(
            functools.partial(local_kernel, sections),
            [f32(tokens, block)] * 2,
            [inputs, cotangent, near, codes, code_grads, *far, *weights],
            grid=grid,
            in_specs=[wide] * 3 + [thin] * 2 + [wide] * (sections - 1) + [whole(s) for s in shapes],
            out_specs=[wide, wide],
        )
        return out, grad, total[:lent_rows], total[lent_rows : lent_rows + flat], total[lent_rows + flat :]

    def nothing(*_):
        wide_zero = jnp.zeros((tokens, block), F32)
        return (
            wide_zero, wide_zero, jnp.zeros((lent_rows, block), F32),
            jnp.zeros((flat, block), F32), jnp.zeros((packed_rows - lent_rows - flat, block), F32),
        )

    out, grad, near_back, far_back, kept = lax.cond(
        usual, finish, nothing,
        inputs, cotangent, near, codes, code_grads, far, [wh, wl, rh, rl, lh, ll],
    )
    near_back = across(near_back, "feat", 1)
    far_back = across(far_back, "feat", 2)
    block_grads, left_grads, right_grads = call(
        functools.partial(place_kernel, sizes),
        [f32(*by_slot.shape), f32(*low_left.shape), f32(*low_right.shape)],
        [partner_bits, kept, near_back, far_back],
        in_specs=[smem] + [vmem] * 3,
    )
    block_grads = jnp.transpose(block_grads, (0, 2, 1, 3))
    outputs = out + ahead
    for part in back:
        grad = grad + part
    return (outputs, grad, block_grads, left_grads, right_grads)


def solution(mesh):
    in_specs = (
        P("dp", "feat"),
        P("feat", None),
        P("feat", "dp", None, None),
        P("feat", "dp", None),
        P("feat", "dp", None),
        P("dp", "feat"),
    )
    out_specs = (
        P("dp", "feat"),
        P("dp", "feat"),
        P("feat", "dp", None, None),
        P("feat", "dp", None),
        P("feat", "dp", None),
    )
    return jax.shard_map(
        on_device, mesh=mesh, in_specs=in_specs, out_specs=out_specs, check_vma=False
    )
```

time: 278 us -> 139 us (0.50)
  waiting for transfers between devices: 178 us -> 77.9 us
  matrix products: 37.4 us -> 0 us
  Pallas kernels: 0 us -> 21.9 us
  blocking collectives: 21.3 us -> 0 us
  starting transfers between devices: 6.96 us -> 25.8 us
  between operations: 19.1 us -> 0.87 us
  local copies, waits for them, and re-layouts: 11.4 us -> 3.58 us
  other arithmetic: 3.17 us -> 8.67 us
    psum x1 -> x0, waiting for transfers between devices: 87 us -> none  [on_device(): codes = lax.psum(code_part, 'feat')]
    ppermute x4 -> x19, waiting for transfers between devices: 16.1 us -> 77.9 us  [across(): return lax.ppermute(block, axis, [(i, i ^ apart) for i in range(count)])]
    reduce_scatter x2 -> x0, waiting for transfers between devices: 57.7 us -> none  [the longest x1 50.5 us: on_device(): lax.psum_scatter(block_grad[None], 'dp', scatter_dimension=1, tiled=True)]
    dot_general x9 -> x0, matrix products: 37.4 us -> none  [the longest x1 8.01 us: on_device(): sparse = jnp.einsum('sri,iso->ro', sources, full_weights, precision=highest)]
    pallas_call x0 -> x6, Pallas kernels: none -> 21.9 us  [call(): pl.pallas_call(kernel, out_shape=out_shapes, in_specs=in_specs, out_specs...]
    all_gather x2 -> x0, blocking collectives: 21.3 us -> none  [the longest x1 11.7 us: on_device(): lax.all_gather(low_left, 'dp', axis=1, tiled=True)]
    ppermute x4 -> x19, starting transfers between devices: 6.57 us -> 25.8 us  [across(): return lax.ppermute(block, axis, [(i, i ^ apart) for i in range(count)])]
    unnamed x6 -> x0, waiting for transfers between devices: 17.5 us -> none
  transfers between devices with their start and end apart: 9 -> 19, of which waited for: 6 -> 12; matrix products, arithmetic and copies ran while one was open for 17% -> 4% of each run, Pallas kernels for 0% -> 12%
where the time goes in v1:
time: 139 us
  waiting for transfers between devices  77.9 us (56%)
  starting transfers between devices  25.8 us (19%)
  Pallas kernels  21.9 us (16%)
  other arithmetic  8.67 us (6%)
  local copies, waits for them, and re-layouts  3.58 us (3%)
    ppermute x19, waiting for transfers between devices, across(): return lax.ppermute(block, axis, [(i, i ^ apart) for i in range(count)])  77.9 us
    ppermute x19, starting transfers between devices, across(): return lax.ppermute(block, axis, [(i, i ^ apart) for i in range(count)])  25.8 us
    pallas_call x6, Pallas kernels, call(): pl.pallas_call(kernel, out_shape=out_shapes, in_specs=in_specs, out_specs...  21.9 us
    unnamed x28, local copies, waits for them, and re-layouts  3.37 us
  transfers between devices with their start and end apart: 19, of which 12 were waited for; matrix products, arithmetic and copies ran while one was open for 4% of the time, Pallas kernels for 12%

profile of v1, /device:TPU:0, one launch (start us, length us, event | category | flops | bytes accessed | tf_op | source)
XLA Modules:
  0.0 138.8 jit_solution(14439444324594681934)
XLA Ops:
  0.6 1.0 copy-done
  1.6 0.8 copy-done.1
  2.5 0.8 copy-done.2
  3.3 0.7 copy-done.3
  4.0 1.3 shard_map.101
  5.2 3.1 %collective-permute-start.8 = (f32[224,512]{1,0:T(8,128)S(1)}, f32[224,512]{1,0:T(8,128)S(1)}, u32[]{:S(2)}, u32[]{:S(2)}) collective-permute-start(f32[224,512]{1,0:T(8,128)S(1)} %get-tuple-element.104), channel_id=1, source_target_pairs={{0,1},{1,0},{2,3},{3,2},{4,5},{5,4},{6,7},{7,6},{8,9},{9,8},{10,11... | collective-permute-start | bytes 1376264 | tf_op jit(solution)/shard_map/ppermute | solution.py:19
  8.3 2.6 %collective-permute-start.9 = (f32[160,512]{1,0:T(8,128)S(1)}, f32[160,512]{1,0:T(8,128)S(1)}, u32[]{:S(2)}, u32[]{:S(2)}) collective-permute-start(f32[160,512]{1,0:T(8,128)S(1)} %get-tuple-element.105), channel_id=1, source_target_pairs={{0,2},{1,3},{2,0},{3,1},{4,6},{5,7},{6,4},{7,5},{8,10},{9,11},{10,... | collective-permute-start | bytes 983048 | tf_op jit(solution)/shard_map/ppermute | solution.py:19
  11.1 14.1 %collective-permute-done.9 = f32[160,512]{1,0:T(8,128)S(1)} collective-permute-done((f32[160,512]{1,0:T(8,128)S(1)}, f32[160,512]{1,0:T(8,128)S(1)}, u32[]{:S(2)}, u32[]{:S(2)}) %collective-permute-start.9) | collective-permute-done | bytes 327712 | tf_op jit(solution)/shard_map/ppermute | solution.py:19
  25.1 0.7 collective-permute-done.8
  25.9 2.6 %collective-permute-start.11 = (f32[384,512]{1,0:T(8,128)S(1)}, f32[384,512]{1,0:T(8,128)}, u32[]{:S(2)}, u32[]{:S(2)}) collective-permute-start(f32[384,512]{1,0:T(8,128)S(1)} %slice.43), channel_id=1, source_target_pairs={{0,2},{1,3},{2,0},{3,1},{4,6},{5,7},{6,4},{7,5},{8,10},{9,11},{10,... | collective-permute-start | bytes 2359304 | tf_op jit(solution)/shard_map/ppermute | solution.py:19
  28.5 1.7 %collective-permute-start.10 = (f32[384,512]{1,0:T(8,128)S(1)}, f32[384,512]{1,0:T(8,128)}, u32[]{:S(2)}, u32[]{:S(2)}) collective-permute-start(f32[384,512]{1,0:T(8,128)S(1)} %slice.44), channel_id=1, source_target_pairs={{0,1},{1,0},{2,3},{3,2},{4,5},{5,4},{6,7},{7,6},{8,9},{9,8},{10,11... | collective-permute-start | bytes 2359304 | tf_op jit(solution)/shard_map/ppermute | solution.py:19
  30.2 1.5 %collective-permute-start.12 = (f32[192,512]{1,0:T(8,128)S(1)}, f32[192,512]{1,0:T(8,128)S(1)}, u32[]{:S(2)}, u32[]{:S(2)}) collective-permute-start(f32[192,512]{1,0:T(8,128)S(1)} %get-tuple-element.110), channel_id=1, source_target_pairs={{0,8},{4,12},{8,0},{12,4},{16,24},{20,28},{24,16},{28,20},{1,9},{5... | collective-permute-start | bytes 1179656 | tf_op jit(solution)/shard_map/ppermute | solution.py:19
  31.7 1.5 %collective-permute-start.13 = (f32[192,512]{1,0:T(8,128)S(1)}, f32[192,512]{1,0:T(8,128)S(1)}, u32[]{:S(2)}, u32[]{:S(2)}) collective-permute-start(f32[192,512]{1,0:T(8,128)S(1)} %get-tuple-element.110), channel_id=1, source_target_pairs={{0,16},{4,20},{8,24},{12,28},{16,0},{20,4},{24,8},{28,12},{1,17},{... | collective-permute-start | bytes 1179656 | tf_op jit(solution)/shard_map/ppermute | solution.py:19
  33.2 0.5 collective-permute-start.14
  33.8 8.5 %collective-permute-done.12 = f32[192,512]{1,0:T(8,128)S(1)} collective-permute-done((f32[192,512]{1,0:T(8,128)S(1)}, f32[192,512]{1,0:T(8,128)S(1)}, u32[]{:S(2)}, u32[]{:S(2)}) %collective-permute-start.12) | collective-permute-done | bytes 393248 | tf_op jit(solution)/shard_map/ppermute | solution.py:19
  42.3 7.0 %collective-permute-done.13 = f32[192,512]{1,0:T(8,128)S(1)} collective-permute-done((f32[192,512]{1,0:T(8,128)S(1)}, f32[192,512]{1,0:T(8,128)S(1)}, u32[]{:S(2)}, u32[]{:S(2)}) %collective-permute-start.13) | collective-permute-done | bytes 393248 | tf_op jit(solution)/shard_map/ppermute | solution.py:19
  49.3 22.8 %conditional.2 = ((bf16[3,512,512]{2,1,0:T(8,128)(2,1)}, bf16[3,512,512]{2,1,0:T(8,128)(2,1)}, bf16[2,256,512]{2,1,0:T(8,128)(2,1)}, bf16[2,256,512]{2,1,0:T(8,1...) conditional(s32[]{:T(128)} %bitcast.8, () %tuple.27, ...), branch_computations={%region_0.0_spmd, %region_1.0_spmd} | conditional | flops 2850817 | bytes 25165992 | solution.py:350
  49.3 1.3 collective-permute-start
  50.6 0.8 collective-permute-start.1
  51.5 1.4 %collective-permute-start.2 = (f32[128,512]{1,0:T(8,128)S(1)}, f32[128,512]{1,0:T(8,128)S(1)}, u32[]{:S(2)}, u32[]{:S(2)}) collective-permute-start(f32[128,512]{1,0:T(8,128)S(1)} %pad_maximum_fusion.1), channel_id=1, source_target_pairs={{0,24},{4,28},{8,16},{12,20},{16,8},{20,12},{24,0},{28,4},{1,25},{... | collective-permute-start | bytes 786440 | tf_op jit(solution)/shard_map/cond/branch_1_fun/ppermute | solution.py:19
  52.9 4.9 %collective-permute-done = f32[128,512]{1,0:T(8,128)S(1)} collective-permute-done((f32[128,512]{1,0:T(8,128)S(1)}, f32[128,512]{1,0:T(8,128)S(1)}, u32[]{:S(2)}, u32[]{:S(2)}) %collective-permute-start) | collective-permute-done | bytes 262176 | tf_op jit(solution)/shard_map/cond/branch_1_fun/ppermute | solution.py:19
  57.9 3.9 %collective-permute-done.1 = f32[128,512]{1,0:T(8,128)S(1)} collective-permute-done((f32[128,512]{1,0:T(8,128)S(1)}, f32[128,512]{1,0:T(8,128)S(1)}, u32[]{:S(2)}, u32[]{:S(2)}) %collective-permute-start.1) | collective-permute-done | bytes 262176 | tf_op jit(solution)/shard_map/cond/branch_1_fun/ppermute | solution.py:19
  61.9 0.2 pad_maximum_fusion.refs_0_
  62.2 4.9 %collective-permute-done.3.refs_1_ = f32[4,320,512]{2,1,0:T(8,128)S(1)} collective-permute-done((f32[4,320,512]{2,1,0:T(8,128)S(1)}, f32[4,320,512]{2,1,0:T(8,128)S(1)}, u32[]{:S(2)}, u32[]{:S(2)}) %collective-permute-start.3) | collective-permute-done | bytes 2621472 | tf_op jit(solution)/shard_map/cond/branch_1_fun/ppermute | solution.py:19
  67.1 5.0 %branch_1_fun.3 = (bf16[3,512,512]{2,1,0:T(8,128)(2,1)}, bf16[3,512,512]{2,1,0:T(8,128)(2,1)}, bf16[2,256,512]{2,1,0:T(8,128)(2,1)}, bf16[2,256,512]{2,1,0:T(8,1...) custom-call(f32[4,320,512]{2,1,0:T(8,128)S(1)} %pad_maximum_fusion.r, ...), custom_call_target="tpu_custom_call" | custom-call | flops 1 | bytes 1 | tf_op jit(solution)/shard_map/cond/branch_1_fun/pallas_call | solution.py:56
  72.2 1.4 pad_maximum_fusion.3.far_ref
  73.5 1.3 pad_maximum_fusion.2.near_ref
  74.9 3.4 %shard_map.102 = (f32[512,256]{1,0:T(8,128)S(1)}, f32[512,256]{1,0:T(8,128)S(1)}, f32[512,512]{1,0:T(8,128)S(1)}, f32[512,512]{1,0:T(8,128)S(1)}) custom-call(f32[512,512]{1,0:T(8,128)S(1)} %pad_maximum_fusion.3.far_ref, f32[512,512]{1,0:T(8,128)S(1)} %pad_maximum_fusion.2.near_ref, bf16[2,512,256]{2,1,0:T(8,128)(2,1)S(1)} %copy-done.10, ...), custom_call_target="tpu_custom_call" | custom-call | flops 1 | bytes 1 | tf_op jit(solution)/shard_map/pallas_call | solution.py:56
  78.3 1.4 collective-permute-start.16
  79.7 0.6 collective-permute-start.15
  80.2 41.7 %conditional.3 = (f32[512,512]{1,0:T(8,128)S(1)}, f32[512,512]{1,0:T(8,128)S(1)}, f32[96,512]{1,0:T(8,128)S(1)}, f32[32,512]{1,0:T(8,128)S(1)}, f32[192,512]{1,0:T(8,128)S(1)}) conditional(s32[]{:T(128)} %bitcast.8, () %tuple.25, (f32[512,512]{1,0:T(8,128)S(1)}, f32[512,512]{1,0:T(8,128)S(1)}, f32[512,512]{1,0:T(8,128)S(1)}, ...), branch_computations={%region_2.0_spmd, %region_3.0_spmd} | conditional | flops 1146882 | bytes 29491402 | solution.py:424
  80.2 4.6 %branch_1_fun.4 = (f32[320,512]{1,0:T(8,128)S(1)}, f32[320,512]{1,0:T(8,128)S(1)}, f32[320,512]{1,0:T(8,128)S(1)}, f32[320,512]{1,0:T(8,128)S(1)}, f32[4,320,512]{2,1,0:T(8,128)S(1)}) custom-call(f32[512,512]{1,0:T(8,128)S(1)} %get-tuple-element.48.refs_0_, f32[512,512]{1,0:T(8,128)S(1)} %get-tuple-element.49.refs_1_, ...), custom_call_target="tpu_custom_call" | custom-call | flops 1 | bytes 1 | tf_op jit(solution)/shard_map/cond/branch_1_fun/pallas_call | solution.py:56
  84.9 4.9 %collective-permute-done.4 = f32[4,320,512]{2,1,0:T(8,128)S(1)} collective-permute-done((f32[4,320,512]{2,1,0:T(8,128)S(1)}, f32[4,320,512]{2,1,0:T(8,128)S(1)}, u32[]{:S(2)}, u32[]{:S(2)}) %collective-permute-start.4) | collective-permute-done | bytes 2621472 | tf_op jit(solution)/shard_map/cond/branch_1_fun/ppermute | solution.py:19
  89.8 0.4 fusion.2
  90.3 0.6 collective-permute-start.5
  90.9 1.5 %collective-permute-start.6 = (f32[320,512]{1,0:T(8,128)S(1)}, f32[320,512]{1,0:T(8,128)S(1)}, u32[]{:S(2)}, u32[]{:S(2)}) collective-permute-start(f32[320,512]{1,0:T(8,128)S(1)} %get-tuple-element.135), channel_id=1, source_target_pairs={{0,16},{4,20},{8,24},{12,28},{16,0},{20,4},{24,8},{28,12},{1,17},{... | collective-permute-start | bytes 1966088 | tf_op jit(solution)/shard_map/cond/branch_1_fun/ppermute | solution.py:19
  92.5 1.4 collective-permute-start.7
  93.8 6.3 %branch_1_fun.5 = (f32[512,512]{1,0:T(8,128)S(1)}, f32[512,512]{1,0:T(8,128)S(1)}) custom-call(f32[512,512]{1,0:T(8,128)S(1)} %get-tuple-element.48.refs_0_, f32[512,512]{1,0:T(8,128)S(1)} %get-tuple-element.49.refs_1_, f32[512,512]{1,0:T(8,128)S(1)} %get-tuple-element.50.refs_2_, f32[512,256]{1,0:T(8,128)S(1)} %get-tuple-element.55.refs_3_, ...), custom_call_target="tpu_custom_call" | custom-call | flops 1 | bytes 1 | tf_op jit(solution)/shard_map/cond/branch_1_fun/pallas_call | solution.py:56
  100.2 7.8 %collective-permute-done.5 = f32[320,512]{1,0:T(8,128)S(1)} collective-permute-done((f32[320,512]{1,0:T(8,128)S(1)}, f32[320,512]{1,0:T(8,128)S(1)}, u32[]{:S(2)}, u32[]{:S(2)}) %collective-permute-start.5) | collective-permute-done | bytes 655392 | tf_op jit(solution)/shard_map/cond/branch_1_fun/ppermute | solution.py:19
  107.9 13.5 %collective-permute-done.6 = f32[320,512]{1,0:T(8,128)S(1)} collective-permute-done((f32[320,512]{1,0:T(8,128)S(1)}, f32[320,512]{1,0:T(8,128)S(1)}, u32[]{:S(2)}, u32[]{:S(2)}) %collective-permute-start.6) | collective-permute-done | bytes 655392 | tf_op jit(solution)/shard_map/cond/branch_1_fun/ppermute | solution.py:19
  121.5 0.4 fusion.6
  121.9 1.5 %collective-permute-start.17 = (f32[96,512]{1,0:T(8,128)S(1)}, f32[96,512]{1,0:T(8,128)S(1)}, u32[]{:S(2)}, u32[]{:S(2)}) collective-permute-start(f32[96,512]{1,0:T(8,128)S(1)} %get-tuple-element.128), channel_id=1, source_target_pairs={{0,1},{1,0},{2,3},{3,2},{4,5},{5,4},{6,7},{7,6},{8,9},{9,8},{10,11... | collective-permute-start | bytes 589832 | tf_op jit(solution)/shard_map/ppermute | solution.py:19
  123.4 1.6 %collective-permute-start.18 = (f32[32,512]{1,0:T(8,128)S(1)}, f32[32,512]{1,0:T(8,128)S(1)}, u32[]{:S(2)}, u32[]{:S(2)}) collective-permute-start(f32[32,512]{1,0:T(8,128)S(1)} %get-tuple-element.129), channel_id=1, source_target_pairs={{0,2},{1,3},{2,0},{3,1},{4,6},{5,7},{6,4},{7,5},{8,10},{9,11},{10,... | collective-permute-start | bytes 196616 | tf_op jit(solution)/shard_map/ppermute | solution.py:19
  125.0 5.5 %collective-permute-done.18.refs_3_ = f32[32,512]{1,0:T(8,128)S(1)} collective-permute-done((f32[32,512]{1,0:T(8,128)S(1)}, f32[32,512]{1,0:T(8,128)S(1)}, u32[]{:S(2)}, u32[]{:S(2)}) %collective-permute-start.18) | collective-permute-done | bytes 65568 | tf_op jit(solution)/shard_map/ppermute | solution.py:19
  130.5 2.1 %collective-permute-done.17.refs_2_ = f32[96,512]{1,0:T(8,128)S(1)} collective-permute-done((f32[96,512]{1,0:T(8,128)S(1)}, f32[96,512]{1,0:T(8,128)S(1)}, u32[]{:S(2)}, u32[]{:S(2)}) %collective-permute-start.17) | collective-permute-done | bytes 196640 | tf_op jit(solution)/shard_map/ppermute | solution.py:19
  132.7 1.4 shard_map.103
  134.0 2.4 %add.28 = f32[512,512]{1,0:T(8,128)} add(f32[512,512]{1,0:T(8,128)S(1)} %get-tuple-element.125, f32[512,512]{1,0:T(8,128)} %collective-permute-done.16) | non-fusion elementwise | flops 262144 | bytes 3145728 | tf_op jit(solution)/shard_map/add | solution.py:439
  136.4 2.4 %add.27 = f32[512,512]{1,0:T(8,128)} add(f32[512,512]{1,0:T(8,128)S(1)} %get-tuple-element.123, f32[512,512]{1,0:T(8,128)} %collective-permute-done.15) | non-fusion elementwise | flops 262144 | bytes 3145728 | tf_op jit(solution)/shard_map/add | solution.py:437
  (47 shorter events, 0.6 us)
Async XLA Ops:
  0.6 1.0 copy-start
  1.6 0.8 copy-start.1
  2.5 0.8 copy-start.2
  3.3 0.7 copy-start.3
  4.0 7.0 %copy-start.5 = (f32[512,512]{1,0:T(8,128)S(1)}, f32[512,512]{1,0:T(8,128)}, u32[]{:S(2)}) copy-start(f32[512,512]{1,0:T(8,128)} %x_ref.1) | copy-start | bytes 3145732
  4.0 7.0 %copy-start.6 = (f32[512,512]{1,0:T(8,128)S(1)}, f32[512,512]{1,0:T(8,128)}, u32[]{:S(2)}) copy-start(f32[512,512]{1,0:T(8,128)} %g_ref.1) | copy-start | bytes 3145732
  5.2 20.6 %collective-permute-start.8 = (f32[224,512]{1,0:T(8,128)S(1)}, f32[224,512]{1,0:T(8,128)S(1)}, u32[]{:S(2)}, u32[]{:S(2)}) collective-permute-start(f32[224,512]{1,0:T(8,128)S(1)} %get-tuple-element.104), channel_id=1, source_target_pairs={{0,1},{1,0},{2,3},{3,2},{4,5},{5,4},{6,7},{7,6},{8,9},{9,8},{10,11... | collective-permute-start | bytes 1376264 | tf_op jit(solution)/shard_map/ppermute | solution.py:19
  8.3 16.8 %collective-permute-start.9 = (f32[160,512]{1,0:T(8,128)S(1)}, f32[160,512]{1,0:T(8,128)S(1)}, u32[]{:S(2)}, u32[]{:S(2)}) collective-permute-start(f32[160,512]{1,0:T(8,128)S(1)} %get-tuple-element.105), channel_id=1, source_target_pairs={{0,2},{1,3},{2,0},{3,1},{4,6},{5,7},{6,4},{7,5},{8,10},{9,11},{10,... | collective-permute-start | bytes 983048 | tf_op jit(solution)/shard_map/ppermute | solution.py:19
  25.9 46.3 %collective-permute-start.11 = (f32[384,512]{1,0:T(8,128)S(1)}, f32[384,512]{1,0:T(8,128)}, u32[]{:S(2)}, u32[]{:S(2)}) collective-permute-start(f32[384,512]{1,0:T(8,128)S(1)} %slice.43), channel_id=1, source_target_pairs={{0,2},{1,3},{2,0},{3,1},{4,6},{5,7},{6,4},{7,5},{8,10},{9,11},{10,... | collective-permute-start | bytes 2359304 | tf_op jit(solution)/shard_map/ppermute | solution.py:19
  28.5 45.0 %collective-permute-start.10 = (f32[384,512]{1,0:T(8,128)S(1)}, f32[384,512]{1,0:T(8,128)}, u32[]{:S(2)}, u32[]{:S(2)}) collective-permute-start(f32[384,512]{1,0:T(8,128)S(1)} %slice.44), channel_id=1, source_target_pairs={{0,1},{1,0},{2,3},{3,2},{4,5},{5,4},{6,7},{7,6},{8,9},{9,8},{10,11... | collective-permute-start | bytes 2359304 | tf_op jit(solution)/shard_map/ppermute | solution.py:19
  30.2 12.1 %collective-permute-start.12 = (f32[192,512]{1,0:T(8,128)S(1)}, f32[192,512]{1,0:T(8,128)S(1)}, u32[]{:S(2)}, u32[]{:S(2)}) collective-permute-start(f32[192,512]{1,0:T(8,128)S(1)} %get-tuple-element.110), channel_id=1, source_target_pairs={{0,8},{4,12},{8,0},{12,4},{16,24},{20,28},{24,16},{28,20},{1,9},{5... | collective-permute-start | bytes 1179656 | tf_op jit(solution)/shard_map/ppermute | solution.py:19
  31.7 17.6 %collective-permute-start.13 = (f32[192,512]{1,0:T(8,128)S(1)}, f32[192,512]{1,0:T(8,128)S(1)}, u32[]{:S(2)}, u32[]{:S(2)}) collective-permute-start(f32[192,512]{1,0:T(8,128)S(1)} %get-tuple-element.110), channel_id=1, source_target_pairs={{0,16},{4,20},{8,24},{12,28},{16,0},{20,4},{24,8},{28,12},{1,17},{... | collective-permute-start | bytes 1179656 | tf_op jit(solution)/shard_map/ppermute | solution.py:19
  33.2 16.1 %collective-permute-start.14 = (f32[192,512]{1,0:T(8,128)S(1)}, f32[192,512]{1,0:T(8,128)S(1)}, u32[]{:S(2)}, u32[]{:S(2)}) collective-permute-start(f32[192,512]{1,0:T(8,128)S(1)} %get-tuple-element.110), channel_id=1, source_target_pairs={{0,24},{4,28},{8,16},{12,20},{16,8},{20,12},{24,0},{28,4},{1,25},{... | collective-permute-start | bytes 1179656 | tf_op jit(solution)/shard_map/ppermute | solution.py:19
  49.3 8.5 %collective-permute-start = (f32[128,512]{1,0:T(8,128)S(1)}, f32[128,512]{1,0:T(8,128)S(1)}, u32[]{:S(2)}, u32[]{:S(2)}) collective-permute-start(f32[128,512]{1,0:T(8,128)S(1)} %pad_maximum_fusion.1), channel_id=1, source_target_pairs={{0,8},{4,12},{8,0},{12,4},{16,24},{20,28},{24,16},{28,20},{1,9},{5... | collective-permute-start | bytes 786440 | tf_op jit(solution)/shard_map/cond/branch_1_fun/ppermute | solution.py:19
  50.6 11.1 %collective-permute-start.1 = (f32[128,512]{1,0:T(8,128)S(1)}, f32[128,512]{1,0:T(8,128)S(1)}, u32[]{:S(2)}, u32[]{:S(2)}) collective-permute-start(f32[128,512]{1,0:T(8,128)S(1)} %pad_maximum_fusion.1), channel_id=1, source_target_pairs={{0,16},{4,20},{8,24},{12,28},{16,0},{20,4},{24,8},{28,12},{1,17},{... | collective-permute-start | bytes 786440 | tf_op jit(solution)/shard_map/cond/branch_1_fun/ppermute | solution.py:19
  51.5 10.4 %collective-permute-start.2 = (f32[128,512]{1,0:T(8,128)S(1)}, f32[128,512]{1,0:T(8,128)S(1)}, u32[]{:S(2)}, u32[]{:S(2)}) collective-permute-start(f32[128,512]{1,0:T(8,128)S(1)} %pad_maximum_fusion.1), channel_id=1, source_target_pairs={{0,24},{4,28},{8,16},{12,20},{16,8},{20,12},{24,0},{28,4},{1,25},{... | collective-permute-start | bytes 786440 | tf_op jit(solution)/shard_map/cond/branch_1_fun/ppermute | solution.py:19
  62.1 5.0 %collective-permute-start.3 = (f32[4,320,512]{2,1,0:T(8,128)S(1)}, f32[4,320,512]{2,1,0:T(8,128)S(1)}, u32[]{:S(2)}, u32[]{:S(2)}) collective-permute-start(f32[4,320,512]{2,1,0:T(8,128)S(1)} %pad_maximum_fusion.refs_0_), channel_id=1, source_target_pairs={{0,4},{4,0},{8,12},{12,8},{16,20},{20,16},{24,28},{28,24},{1,5},{5... | collective-permute-start | bytes 7864328 | tf_op jit(solution)/shard_map/cond/branch_1_fun/ppermute | solution.py:19
  72.1 2.7 %copy-start.8 = (bf16[2,256,512]{2,1,0:T(8,128)(2,1)S(1)}, bf16[2,256,512]{2,1,0:T(8,128)(2,1)}, u32[]{:S(2)}) copy-start(bf16[2,256,512]{2,1,0:T(8,128)(2,1)} %get-tuple-element.113.rh) | copy-start | bytes 1572868
  72.1 2.7 %copy-start.9 = (bf16[2,256,512]{2,1,0:T(8,128)(2,1)S(1)}, bf16[2,256,512]{2,1,0:T(8,128)(2,1)}, u32[]{:S(2)}) copy-start(bf16[2,256,512]{2,1,0:T(8,128)(2,1)} %get-tuple-element.114.rl) | copy-start | bytes 1572868
  72.1 2.7 %copy-start.10 = (bf16[2,512,256]{2,1,0:T(8,128)(2,1)S(1)}, bf16[2,512,256]{2,1,0:T(8,128)(2,1)}, u32[]{:S(2)}) copy-start(bf16[2,512,256]{2,1,0:T(8,128)(2,1)} %get-tuple-element.111.lh) | copy-start | bytes 1572868
  72.1 2.7 %copy-start.11 = (bf16[2,512,256]{2,1,0:T(8,128)(2,1)S(1)}, bf16[2,512,256]{2,1,0:T(8,128)(2,1)}, u32[]{:S(2)}) copy-start(bf16[2,512,256]{2,1,0:T(8,128)(2,1)} %get-tuple-element.112.ll) | copy-start | bytes 1572868
  72.1 2.7 %copy-start.12 = (f32[512,512]{1,0:T(8,128)S(1)}, f32[512,512]{1,0:T(8,128)}, u32[]{:S(2)}) copy-start(f32[512,512]{1,0:T(8,128)} %get-tuple-element.118.ahead0_ref) | copy-start | bytes 3145732
  72.1 2.7 %copy-start.13 = (f32[512,512]{1,0:T(8,128)S(1)}, f32[512,512]{1,0:T(8,128)}, u32[]{:S(2)}) copy-start(f32[512,512]{1,0:T(8,128)} %get-tuple-element.117.back0_ref) | copy-start | bytes 3145732
  74.9 5.4 %copy-start.7 = (f32[512,512]{1,0:T(8,128)S(1)}, f32[512,512]{1,0:T(8,128)}, u32[]{:S(2)}) copy-start(f32[512,512]{1,0:T(8,128)} %g_ref.1) | copy-start | bytes 3145732
  78.3 55.8 %collective-permute-start.16 = (f32[512,512]{1,0:T(8,128)S(1)}, f32[512,512]{1,0:T(8,128)}, u32[]{:S(2)}, u32[]{:S(2)}) collective-permute-start(f32[512,512]{1,0:T(8,128)S(1)} %get-tuple-element.126), channel_id=1, source_target_pairs={{0,2},{1,3},{2,0},{3,1},{4,6},{5,7},{6,4},{7,5},{8,10},{9,11},{10,... | collective-permute-start | bytes 3145736 | tf_op jit(solution)/shard_map/ppermute | solution.py:19
  79.7 56.8 %collective-permute-start.15 = (f32[512,512]{1,0:T(8,128)S(1)}, f32[512,512]{1,0:T(8,128)}, u32[]{:S(2)}, u32[]{:S(2)}) collective-permute-start(f32[512,512]{1,0:T(8,128)S(1)} %get-tuple-element.124), channel_id=1, source_target_pairs={{0,1},{1,0},{2,3},{3,2},{4,5},{5,4},{6,7},{7,6},{8,9},{9,8},{10,11... | collective-permute-start | bytes 3145736 | tf_op jit(solution)/shard_map/ppermute | solution.py:19
  80.2 52.4 %copy-start.4 = (s32[1,2]{1,0:T(1,128)S(1)}, s32[1,2]{1,0:T(1,128)}, u32[]{:S(2)}) copy-start(s32[1,2]{1,0:T(1,128)} %refs_0_.1) | copy-start | bytes 28
  84.9 5.0 %collective-permute-start.4 = (f32[4,320,512]{2,1,0:T(8,128)S(1)}, f32[4,320,512]{2,1,0:T(8,128)S(1)}, u32[]{:S(2)}, u32[]{:S(2)}) collective-permute-start(f32[4,320,512]{2,1,0:T(8,128)S(1)} %get-tuple-element.66), channel_id=1, source_target_pairs={{0,4},{4,0},{8,12},{12,8},{16,20},{20,16},{24,28},{28,24},{1,5},{5... | collective-permute-start | bytes 7864328 | tf_op jit(solution)/shard_map/cond/branch_1_fun/ppermute | solution.py:19
  90.3 17.6 %collective-permute-start.5 = (f32[320,512]{1,0:T(8,128)S(1)}, f32[320,512]{1,0:T(8,128)S(1)}, u32[]{:S(2)}, u32[]{:S(2)}) collective-permute-start(f32[320,512]{1,0:T(8,128)S(1)} %get-tuple-element.133), channel_id=1, source_target_pairs={{0,8},{4,12},{8,0},{12,4},{16,24},{20,28},{24,16},{28,20},{1,9},{5... | collective-permute-start | bytes 1966088 | tf_op jit(solution)/shard_map/cond/branch_1_fun/ppermute | solution.py:19
  90.9 30.5 %collective-permute-start.6 = (f32[320,512]{1,0:T(8,128)S(1)}, f32[320,512]{1,0:T(8,128)S(1)}, u32[]{:S(2)}, u32[]{:S(2)}) collective-permute-start(f32[320,512]{1,0:T(8,128)S(1)} %get-tuple-element.135), channel_id=1, source_target_pairs={{0,16},{4,20},{8,24},{12,28},{16,0},{20,4},{24,8},{28,12},{1,17},{... | collective-permute-start | bytes 1966088 | tf_op jit(solution)/shard_map/cond/branch_1_fun/ppermute | solution.py:19
  92.5 29.0 %collective-permute-start.7 = (f32[320,512]{1,0:T(8,128)S(1)}, f32[320,512]{1,0:T(8,128)S(1)}, u32[]{:S(2)}, u32[]{:S(2)}) collective-permute-start(f32[320,512]{1,0:T(8,128)S(1)} %get-tuple-element.134), channel_id=1, source_target_pairs={{0,24},{4,28},{8,16},{12,20},{16,8},{20,12},{24,0},{28,4},{1,25},{... | collective-permute-start | bytes 1966088 | tf_op jit(solution)/shard_map/cond/branch_1_fun/ppermute | solution.py:19
  121.9 10.7 %collective-permute-start.17 = (f32[96,512]{1,0:T(8,128)S(1)}, f32[96,512]{1,0:T(8,128)S(1)}, u32[]{:S(2)}, u32[]{:S(2)}) collective-permute-start(f32[96,512]{1,0:T(8,128)S(1)} %get-tuple-element.128), channel_id=1, source_target_pairs={{0,1},{1,0},{2,3},{3,2},{4,5},{5,4},{6,7},{7,6},{8,9},{9,8},{10,11... | collective-permute-start | bytes 589832 | tf_op jit(solution)/shard_map/ppermute | solution.py:19
  123.4 7.1 %collective-permute-start.18 = (f32[32,512]{1,0:T(8,128)S(1)}, f32[32,512]{1,0:T(8,128)S(1)}, u32[]{:S(2)}, u32[]{:S(2)}) collective-permute-start(f32[32,512]{1,0:T(8,128)S(1)} %get-tuple-element.129), channel_id=1, source_target_pairs={{0,2},{1,3},{2,0},{3,1},{4,6},{5,7},{6,4},{7,5},{8,10},{9,11},{10,... | collective-permute-start | bytes 196616 | tf_op jit(solution)/shard_map/ppermute | solution.py:19

commit v2 on v1

v2 whole, which is shorter than its diff:
```python
import functools
import math

import jax
import jax.numpy as jnp
from jax import lax
from jax.experimental import pallas as pl
from jax.experimental.pallas import tpu as pltpu
from jax.sharding import PartitionSpec as P

F32 = jnp.float32
BF16 = jnp.bfloat16
VMEM_BYTES = 32 * 1024 * 1024
PACK_VMEM_BYTES = 60 * 1024 * 1024


def across(block, axis, apart):
    count = lax.axis_size(axis)
    return lax.ppermute(block, axis, [(i, i ^ apart) for i in range(count)])


def split(value):
    high = value.astype(BF16)
    return high, (value - high.astype(F32)).astype(BF16)


def dot3(left, right, over):
    def one(a, b):
        return lax.dot_general(
            a, b, ((over[:1], over[1:]), ((), ())), preferred_element_type=F32
        )

    return one(left[0], right[0]) + (one(left[0], right[1]) + one(left[1], right[0]))


def nn(left, right):
    return dot3(left, right, (1, 0))


def nt(left, right):
    return dot3(left, right, (1, 1))


def tn(left, right):
    return dot3(left, right, (0, 0))


def call(
    kernel, out_shapes, operands, grid=None, in_specs=None, out_specs=None, scratch=(),
    vmem_bytes=VMEM_BYTES, aliases=None,
):
    vmem = pl.BlockSpec(memory_space=pltpu.VMEM)
    kwargs = {}
    if grid is None:
        in_specs = in_specs or [vmem] * len(operands)
        out_specs = [vmem] * len(out_shapes)
    else:
        kwargs["grid"] = grid
    return pl.pallas_call(
        kernel,
        out_shape=out_shapes,
        in_specs=in_specs,
        out_specs=out_specs,
        scratch_shapes=list(scratch),
        input_output_aliases=aliases or {},
        cost_estimate=pl.CostEstimate(flops=1, bytes_accessed=1, transcendentals=0),
        compiler_params=pltpu.CompilerParams(vmem_limit_bytes=vmem_bytes),
        **kwargs,
    )(*operands)


def f32(*shape):
    return jax.ShapeDtypeStruct(shape, F32)


def b16(*shape):
    return jax.ShapeDtypeStruct(shape, BF16)


def whole(shape):
    return pl.BlockSpec(shape, lambda *_: (0,) * len(shape))


def by_tokens(tokens, width):
    return pl.BlockSpec((tokens, width), lambda i: (i, 0))


def slot_weights(bits_ref, w_ref, bit, sections):
    chosen = w_ref[0, sections]
    for s in range(sections - 1):
        chosen = jnp.where(bits_ref[0, s] == bit, w_ref[0, 1 + s], chosen)
    return chosen


def put_left(out_ref, left, block):
    rows, rank = left.shape
    pieces = block // rank
    step = rows // pieces
    for p in range(pieces):
        out_ref[:step, p * rank : (p + 1) * rank] = left[p * step : (p + 1) * step]


def pack_kernel(bits_ref, w_ref, left_ref, right_ref, x_ref, g_ref, near_ref, far_ref, own_ref):
    _, slots, rows, block = w_ref.shape
    sections = slots - 1
    rank_rows = right_ref.shape[1]
    flat = far_ref.shape[0] - x_ref.shape[0]
    near_ref[:rows] = slot_weights(bits_ref, w_ref, 0, sections)
    near_ref[rows : rows + rank_rows] = right_ref[0]
    near_ref[rows + rank_rows :] = g_ref[...]
    put_left(far_ref.at[:flat], left_ref[0], block)
    far_ref[flat:] = x_ref[...]
    own_ref[:rows] = w_ref[0, 0]
    for b in range(1, sections):
        own_ref[b * rows : (b + 1) * rows] = slot_weights(bits_ref, w_ref, b, sections)
    at = sections * rows
    own_ref[at : at + rank_rows] = right_ref[0]
    put_left(own_ref.at[at + rank_rows :], left_ref[0], block)


def codes_of(x, g, far, near, low):
    lh, ll, rh, rl = low
    codes = nn(x, (lh[0], ll[0])) + nn(far, (lh[1], ll[1]))
    return codes, nt(g, (rh[0], rl[0])) + nt(near, (rh[1], rl[1]))


def sends_of(x, g, codes, code_grads, wide, low, ahead_ref, back_refs):
    wh, wl = wide
    lh, ll, rh, rl = low
    last = wh.shape[0] - 1
    ahead_ref[...] = nn(x, (wh[last], wl[last])) + nn(codes, (rh[1], rl[1]))
    for b in range(last):
        back = nt(g, (wh[b], wl[b]))
        if b == 0:
            back += nt(code_grads, (lh[1], ll[1]))
        back_refs[b][...] = back


def messages(x_ref, g_ref, far_ref, near_ref, wide, low, outs):
    x, g = split(x_ref[...]), split(g_ref[...])
    codes, code_grads = codes_of(x, g, split(far_ref[...]), split(near_ref[...]), low)
    outs[0][...] = codes
    outs[1][...] = code_grads
    sends_of(x, g, split(codes), split(code_grads), wide, low, outs[2], outs[3:])


def weights_kernel(sizes, *refs):
    sections, rows, rank_rows, rank, dp_count = sizes
    even_ref, odd_ref = refs[:2]
    early = refs[2:6] if sections == 2 else ()
    sh, sl, wh, wl, lh, ll, rh, rl, *outs = refs[2 + len(early) :]
    block = wh.shape[2]
    flat = rows * rank // block
    pieces = rows // flat
    me = lax.axis_index("dp")
    for k in range(dp_count):
        part = (odd_ref if k % 2 else even_ref).at[k // 2]
        owner = me ^ k
        at = 0

        def move(high_ref, low_ref, i, start, count, value):
            high, low = split(value)
            place = pl.ds(pl.multiple_of(start, 16), count)
            high_ref[i, place, :] = high
            low_ref[i, place, :] = low

        def move_wide(high_ref, low_ref, i, start, count):
            move(high_ref, low_ref, i, owner * count, count, part[start : start + count, :])
            return start + count

        def move_left(i, start):
            for p in range(pieces):
                value = part[start : start + flat, p * rank : (p + 1) * rank]
                move(lh, ll, i, owner * rows + p * flat, flat, value)
            return start + flat

        at = move_wide(sh, sl, 0, at, rows)
        for i in range(sections - 1):
            at = move_wide(wh, wl, i, at, rows)
        at = move_wide(rh, rl, 0, at, rank_rows)
        at = move_left(0, at)
        at = move_wide(wh, wl, sections - 1, at, rows)
        at = move_wide(rh, rl, 1, at, rank_rows)
        at = move_left(1, at)
    if early:
        messages(*early, (wh, wl), (lh, ll, rh, rl), outs)


def messages_kernel(x_ref, g_ref, far_ref, near_ref, wh, wl, lh, ll, rh, rl, *outs):
    messages(x_ref, g_ref, far_ref, near_ref, (wh, wl), (lh, ll, rh, rl), outs)


def codes_kernel(x_ref, g_ref, far_ref, near_ref, lh, ll, rh, rl, c_ref, cg_ref):
    parts = [split(r[...]) for r in (x_ref, g_ref, far_ref, near_ref)]
    c_ref[...], cg_ref[...] = codes_of(*parts, (lh, ll, rh, rl))


def sends_kernel(x_ref, g_ref, c_ref, cg_ref, wh, wl, lh, ll, rh, rl, *outs):
    parts = [split(r[...]) for r in (x_ref, g_ref, c_ref, cg_ref)]
    sends_of(*parts, (wh, wl), (lh, ll, rh, rl), outs[0], outs[1:])


def spread(dp_count, count, keep_refs, give_ref, put):
    me = lax.axis_index("dp")
    for k in range(dp_count):
        place = pl.ds(pl.multiple_of((me ^ k) * count, 8), count)
        put(give_ref.at[k // 2] if k % 2 else keep_refs[k // 2], place)


def self_kernel(sizes, scale, *refs):
    _, rows, _, _, dp_count = sizes
    x_ref, g_ref, *keep_refs, give_ref, dw = refs
    dw[...] = tn(split(x_ref[...]), split(g_ref[...])) * scale

    def put(out, place):
        out[...] = dw[place, :]

    spread(dp_count, rows, keep_refs, give_ref, put)


def grads_kernel(sizes, scale, *refs):
    sections, rows, rank_rows, rank, dp_count = sizes
    x_ref, g_ref, near_ref, c_ref, cg_ref, *rest = refs
    far_refs = rest[: sections - 1]
    half = dp_count // 2
    keep_refs = rest[sections - 1 : sections - 1 + half]
    give_ref = rest[sections - 1 + half]
    dw, dr, dl = rest[sections + half :]
    block = x_ref.shape[1]
    flat = rows * rank // block
    pieces = rows // flat
    at = [0]

    def spread_wide(source, count):
        def put(out, place):
            out[at[0] : at[0] + count, :] = source[place, :]

        spread(dp_count, count, keep_refs, give_ref, put)
        at[0] += count

    def spread_left(source):
        def put(out, place):
            value = source[place, :]
            for p in range(pieces):
                out[at[0] : at[0] + flat, p * rank : (p + 1) * rank] = value[
                    p * flat : (p + 1) * flat
                ]

        spread(dp_count, rows, keep_refs, give_ref, put)
        at[0] += flat

    x, g, near = split(x_ref[...]), split(g_ref[...]), split(near_ref[...])
    c, cg = split(c_ref[...]), split(cg_ref[...])
    far = [split(r[...]) for r in far_refs]
    dw[...] = tn(x, near) * scale
    spread_wide(dw, rows)
    dr[...] = tn(c, near) * scale
    spread_wide(dr, rank_rows)
    dl[...] = tn(far[0], cg) * scale
    spread_left(dl)
    for b in range(1, sections):
        dw[...] = tn(far[b - 1], g) * scale
        spread_wide(dw, rows)
    dr[...] = tn(c, g) * scale
    spread_wide(dr, rank_rows)
    dl[...] = tn(x, cg) * scale
    spread_left(dl)


def local_kernel(sections, *refs):
    x_ref, g_ref, near_ref, c_ref, cg_ref, *rest = refs
    far_refs = rest[: sections - 1]
    sh, sl, wh, wl, lh, ll, rh, rl, out_ref, grad_ref = rest[sections - 1 :]
    out = nn(split(x_ref[...]), (sh[0], sl[0])) + nn(split(c_ref[...]), (rh[0], rl[0]))
    for b in range(1, sections):
        out += nn(split(far_refs[b - 1][...]), (wh[b - 1], wl[b - 1]))
    out_ref[...] = out
    grad = nt(split(g_ref[...]), (sh[0], sl[0])) + nt(split(cg_ref[...]), (lh[0], ll[0]))
    grad_ref[...] = grad + nt(split(near_ref[...]), (wh[sections - 1], wl[sections - 1]))


def join_kernel(out0_ref, grad0_ref, ahead_ref, back_ref, out_ref, grad_ref):
    out_ref[...] = out0_ref[...] + ahead_ref[...]
    grad_ref[...] = grad0_ref[...] + back_ref[...]


def place_kernel(sizes, *refs):
    sections, rows, rank_rows, rank, _ = sizes
    bits_ref, self_ref, kept_ref, near_ref, far_ref, w_ref, left_ref, right_ref = refs
    block = kept_ref.shape[1]
    flat = rows * rank // block
    pieces = rows // flat
    w_ref[0, 0] = self_ref[...]
    for s in range(sections):
        chosen = near_ref[:rows]
        for b in range(1, sections):
            chosen = jnp.where(bits_ref[0, s] == b, kept_ref[(b - 1) * rows : b * rows], chosen)
        w_ref[0, 1 + s] = chosen
    at = (sections - 1) * rows
    right_ref[0] = kept_ref[at : at + rank_rows] + near_ref[rows:]
    at += rank_rows
    for p in range(pieces):
        columns = slice(p * rank, (p + 1) * rank)
        left_ref[0, p * flat : (p + 1) * flat, :] = (
            kept_ref[at : at + flat, columns] + far_ref[:, columns]
        )


def join(outputs, grad, parts, start):
    tokens, block = outputs.shape
    step = math.gcd(start, parts[0].shape[0])
    there = pl.BlockSpec((step, block), lambda i: (i + start // step, 0))
    here = by_tokens(step, block)
    return call(
        join_kernel,
        [f32(tokens, block)] * 2,
        [outputs, grad, *parts],
        grid=(parts[0].shape[0] // step,),
        in_specs=[there, there, here, here],
        out_specs=[there, there],
        aliases={0: 0, 1: 1},
    )


def on_device(inputs, partner_bits, block_weights, low_left, low_right, cotangent):
    tokens, block = inputs.shape
    sections = partner_bits.shape[1]
    dp_count = lax.axis_size("dp")
    half = dp_count // 2
    rows, rank = low_left.shape[1:]
    rank_rows = low_right.shape[1]
    all_rank = rank_rows * dp_count
    flat = rows * rank // block
    sizes = (sections, rows, rank_rows, rank, dp_count)
    early = tokens * 3 // 128 * 16
    late = tokens - early
    lent_rows = rows + rank_rows
    own_rows = sections * rows + rank_rows + flat
    sum_rows = own_rows + lent_rows + flat - rows
    smem = pl.BlockSpec(memory_space=pltpu.SMEM)
    vmem = pl.BlockSpec(memory_space=pltpu.VMEM)
    usual = partner_bits[0, 0] >= 0

    by_slot = jnp.transpose(block_weights, (0, 2, 1, 3))
    pack_shapes = [(lent_rows + early, block), (flat + early, block), (own_rows, block)]
    out_near, out_far, own = call(
        pack_kernel,
        [f32(*s) for s in pack_shapes],
        [partner_bits, by_slot, low_left, low_right, inputs, cotangent],
        grid=(1,),
        in_specs=[
            smem, whole(by_slot.shape), whole(low_left.shape), whole(low_right.shape),
            whole((early, block)), whole((early, block)),
        ],
        out_specs=[whole(s) for s in pack_shapes],
        vmem_bytes=PACK_VMEM_BYTES,
    )
    got_near = across(out_near, "feat", 1)
    got_far = across(out_far, "feat", 2)
    own = [own] + [across(own, "dp", k) for k in range(2, dp_count, 2)]
    late_x, late_g, got_near, got_far, own = lax.optimization_barrier(
        (inputs[early:], cotangent[early:], got_near, got_far, own)
    )
    late_far = across(late_x, "feat", 2)
    late_near = across(late_g, "feat", 1)
    early_far, early_near = got_far[flat:], got_near[lent_rows:]

    s_shape = (1, block, block)
    w_shape = (sections, block, block)
    l_shape = (2, block, rank)
    r_shape = (2, all_rank, block)
    shapes = [s_shape, s_shape, w_shape, w_shape, l_shape, l_shape, r_shape, r_shape]

    def message_shapes(count):
        return [(count, rank)] * 2 + [(count, block)] * sections

    folds = sections == 2
    scale = 1.0 / math.sqrt(tokens * dp_count)
    made = [b16(*s) for s in shapes]
    if folds:
        made += [f32(*s) for s in message_shapes(early)]

    lent = jnp.concatenate([got_near[:lent_rows], got_far[:flat]])
    lent = [lent] + [across(lent, "dp", k) for k in range(2, dp_count, 2)]

    def prepare(own, lent, *early_parts):
        even = jnp.stack([jnp.concatenate(pair) for pair in zip(own, lent)])
        odd = across(even, "dp", 1)
        *keep, give = call(
            functools.partial(self_kernel, sizes, scale),
            [f32(rows, block)] * half + [f32(half, rows, block)],
            early_parts[:2],
            scratch=[pltpu.VMEM((block, block), F32)],
        )
        got = across(give, "dp", 1)
        got, odd = lax.optimization_barrier((got, odd))
        self_grads = keep[0] + got[0]
        for m in range(1, half):
            self_grads = self_grads + across(keep[m] + got[m], "dp", 2 * m)
        operands = [even, odd, *early_parts] if folds else [even, odd]
        return self_grads, *(
            call(
                functools.partial(weights_kernel, sizes),
                made,
                operands,
                grid=(1,),
                in_specs=[whole(even.shape)] * 2 + [whole((early, block))] * (len(operands) - 2),
                out_specs=[whole(s.shape) for s in made],
            )
        )

    def empty(*_):
        return tuple(jnp.zeros(s.shape, s.dtype) for s in [f32(rows, block)] + made)

    self_grads, *weights = lax.cond(
        usual, prepare, empty,
        own, lent, inputs, cotangent, early_far, early_near,
    )
    weights, sent = weights[:8], weights[8:]
    low = weights[4:]
    step = tokens // 2
    wide, thin = by_tokens(step, block), by_tokens(step, rank)
    weight_specs = [whole(s) for s in shapes]
    if folds:
        wide_late, thin_late = by_tokens(late, block), by_tokens(late, rank)
        late_sent = call(
            messages_kernel,
            [f32(*s) for s in message_shapes(late)],
            [late_x, late_g, late_far, late_near, *weights[2:]],
            grid=(1,),
            in_specs=[wide_late] * 4 + weight_specs[2:],
            out_specs=[thin_late] * 2 + [wide_late] * sections,
        )
        first = [across(sent[2], "feat", 1), across(sent[3], "feat", 2)]
        codes = jnp.concatenate([sent[0], late_sent[0]])
        code_grads = jnp.concatenate([sent[1], late_sent[1]])
    far = [jnp.concatenate([early_far, late_far])]
    near = jnp.concatenate([early_near, late_near])
    far += [across(inputs, "feat", 1 << b) for b in range(2, sections)]
    grid = (tokens // step,)
    if not folds:
        codes, code_grads = call(
            codes_kernel,
            [f32(tokens, rank)] * 2,
            [inputs, cotangent, far[0], near, *low],
            grid=grid,
            in_specs=[wide] * 4 + weight_specs[4:],
            out_specs=[thin, thin],
        )
        for b in range(2, sections):
            codes = codes + across(codes, "feat", 1 << b)
            code_grads = code_grads + across(code_grads, "feat", 1 << b)
        ahead, *back = call(
            sends_kernel,
            [f32(tokens, block)] * sections,
            [inputs, cotangent, codes, code_grads, *weights[2:]],
            grid=grid,
            in_specs=[wide, wide, thin, thin, *weight_specs[2:]],
            out_specs=[wide] * sections,
        )
        back = [across(back[b - 1], "feat", 1 << b) for b in range(1, sections)]
        ahead = across(ahead, "feat", 1)

    def reduce_pair(inputs, cotangent, near, codes, code_grads, *far):
        *keep, give = call(
            functools.partial(grads_kernel, sizes, scale),
            [f32(sum_rows, block)] * half + [f32(half, sum_rows, block)],
            [inputs, cotangent, near, codes, code_grads, *far],
            scratch=[
                pltpu.VMEM((block, block), F32),
                pltpu.VMEM((all_rank, block), F32),
                pltpu.VMEM((block, rank), F32),
            ],
        )
        got = across(give, "dp", 1)
        return tuple(keep[m] + got[m] for m in range(half))

    def no_pair(*_):
        return (jnp.zeros((sum_rows, block), F32),) * half

    summed = lax.cond(usual, reduce_pair, no_pair, inputs, cotangent, near, codes, code_grads, *far)
    if folds:
        first, rest, summed = lax.optimization_barrier((first, late_sent[2:], summed))
        rest = [across(rest[0], "feat", 1), across(rest[1], "feat", 2)]

    def finish(summed, inputs, cotangent, near, codes, code_grads, far, weights):
        total = summed[0]
        for m in range(1, half):
            total = total + across(summed[m], "dp", 2 * m)
        out, grad = call(
            functools.partial(local_kernel, sections),
            [f32(tokens, block)] * 2,
            [inputs, cotangent, near, codes, code_grads, *far, *weights],
            grid=grid,
            in_specs=[wide] * 3 + [thin] * 2 + [wide] * (sections - 1) + weight_specs,
            out_specs=[wide, wide],
        )
        at = lent_rows + flat
        return out, grad, total[:lent_rows], total[lent_rows:at], total[at:]

    def nothing(*_):
        wide_zero = jnp.zeros((tokens, block), F32)
        return (
            wide_zero, wide_zero, jnp.zeros((lent_rows, block), F32),
            jnp.zeros((flat, block), F32), jnp.zeros((sum_rows - lent_rows - flat, block), F32),
        )

    outputs, grad, near_back, far_back, kept = lax.cond(
        usual, finish, nothing,
        summed, inputs, cotangent, near, codes, code_grads, far, weights,
    )
    if folds:
        for start, parts in ((0, first), (early, rest)):
            outputs, grad = join(outputs, grad, parts, start)
    else:
        outputs = outputs + ahead
        for part in back:
            grad = grad + part
    near_back = across(near_back, "feat", 1)
    far_back = across(far_back, "feat", 2)
    outputs, grad, kept = lax.optimization_barrier((outputs, grad, kept))
    block_grads, left_grads, right_grads = call(
        functools.partial(place_kernel, sizes),
        [f32(*by_slot.shape), f32(*low_left.shape), f32(*low_right.shape)],
        [partner_bits, self_grads, kept, near_back, far_back],
        in_specs=[smem] + [vmem] * 4,
    )
    block_grads = jnp.transpose(block_grads, (0, 2, 1, 3))
    return (outputs, grad, block_grads, left_grads, right_grads)


def solution(mesh):
    in_specs = (
        P("dp", "feat"),
        P("feat", None),
        P("feat", "dp", None, None),
        P("feat", "dp", None),
        P("feat", "dp", None),
        P("dp", "feat"),
    )
    out_specs = (
        P("dp", "feat"),
        P("dp", "feat"),
        P("feat", "dp", None, None),
        P("feat", "dp", None),
        P("feat", "dp", None),
    )
    return jax.shard_map(
        on_device, mesh=mesh, in_specs=in_specs, out_specs=out_specs, check_vma=False
    )
```

time: 139 us -> 121 us (0.87)
  waiting for transfers between devices: 77.9 us -> 57.1 us
  starting transfers between devices: 25.8 us -> 31.2 us
  other arithmetic: 8.67 us -> 4.34 us
  Pallas kernels: 21.9 us -> 25 us
  local copies, waits for them, and re-layouts: 3.58 us -> 1.46 us
    ppermute x19 -> x25, waiting for transfers between devices: 77.9 us -> 57.1 us  [across(): return lax.ppermute(block, axis, [(i, i ^ apart) for i in range(count)])]
    ppermute x19 -> x25, starting transfers between devices: 25.8 us -> 31.2 us  [across(): return lax.ppermute(block, axis, [(i, i ^ apart) for i in range(count)])]
    add x3, other arithmetic: 5.25 us -> 0.58 us  [the longest x1 0.48 us: reduce_pair(): return tuple((keep[m] + got[m] for m in range(half)))]
    pallas_call x6 -> x9, Pallas kernels: 21.9 us -> 25 us  [call(): pl.pallas_call(kernel, out_shape=out_shapes, in_specs=in_specs, out_specs...]
    unnamed x28 -> x55, local copies, waits for them, and re-layouts: 3.37 us -> 1.21 us
  transfers between devices with their start and end apart: 19 -> 25, of which waited for: 12 -> 18; matrix products, arithmetic and copies ran while one was open for 4% -> 4% of each run, Pallas kernels for 12% -> 18%
where the time goes in v2:
time: 121 us; the launch traced here: 120 us
  waiting for transfers between devices  57.1 us (47%)
  starting transfers between devices  31.2 us (26%)
  Pallas kernels  25 us (21%)
  other arithmetic  4.34 us (4%)
  local copies, waits for them, and re-layouts  1.46 us (1%)
    ppermute x25, waiting for transfers between devices, across(): return lax.ppermute(block, axis, [(i, i ^ apart) for i in range(count)])  57.1 us
    ppermute x25, starting transfers between devices, across(): return lax.ppermute(block, axis, [(i, i ^ apart) for i in range(count)])  31.2 us
    pallas_call x9, Pallas kernels, call(): pl.pallas_call(kernel, out_shape=out_shapes, in_specs=in_specs, out_specs...  25 us
  transfers between devices with their start and end apart: 25, of which 18 were waited for; matrix products, arithmetic and copies ran while one was open for 4% of the time, Pallas kernels for 18%

profile of v2, /device:TPU:0, one launch (start us, length us, event | category | flops | bytes accessed | tf_op | source)
XLA Modules:
  0.0 120.5 jit_solution(3410165527594048321)
XLA Ops:
  0.7 2.4 %shard_map.101 = (f32[288,512]{1,0:T(8,128)}, f32[224,512]{1,0:T(8,128)}, f32[192,512]{1,0:T(8,128)S(1)}) custom-call(s32[1,2]{1,0:T(1,128)} %refs_0_.1, f32[1,3,64,512]{3,2,1,0:T(8,128)} %bitcast.43, f32[1,64,256]{2,1,0:T(8,128)} %left_ref.1, f32[1,32,512]{2,1,0:T(8,128)} %right_ref.1, f32[512,512]{1,0:T(8,128)} %x_ref.1, f32[512,512]{1,0:T(8,128)} %g_ref.1), custom_call_target="tpu_custom_call" | custom-call | flops 1 | bytes 1 | tf_op jit(solution)/shard_map/pallas_call | solution.py:59
  3.1 3.0 %collective-permute-start.9 = (f32[288,512]{1,0:T(8,128)}, f32[288,512]{1,0:T(8,128)S(1)}, u32[]{:S(2)}, u32[]{:S(2)}) collective-permute-start(f32[288,512]{1,0:T(8,128)} %get-tuple-element.194), channel_id=1, source_target_pairs={{0,1},{1,0},{2,3},{3,2},{4,5},{5,4},{6,7},{7,6},{8,9},{9,8},{10,11... | collective-permute-start | bytes 1769480 | tf_op jit(solution)/shard_map/ppermute | solution.py:19
  6.1 2.6 %collective-permute-start.10 = (f32[224,512]{1,0:T(8,128)}, f32[224,512]{1,0:T(8,128)S(1)}, u32[]{:S(2)}, u32[]{:S(2)}) collective-permute-start(f32[224,512]{1,0:T(8,128)} %get-tuple-element.195), channel_id=1, source_target_pairs={{0,2},{1,3},{2,0},{3,1},{4,6},{5,7},{6,4},{7,5},{8,10},{9,11},{10,... | collective-permute-start | bytes 1376264 | tf_op jit(solution)/shard_map/ppermute | solution.py:19
  8.7 1.5 %collective-permute-start.11 = (f32[192,512]{1,0:T(8,128)S(1)}, f32[192,512]{1,0:T(8,128)S(1)}, u32[]{:S(2)}, u32[]{:S(2)}) collective-permute-start(f32[192,512]{1,0:T(8,128)S(1)} %get-tuple-element.199), channel_id=1, source_target_pairs={{0,8},{4,12},{8,0},{12,4},{16,24},{20,28},{24,16},{28,20},{1,9},{5... | collective-permute-start | bytes 1179656 | tf_op jit(solution)/shard_map/ppermute | solution.py:19
  10.2 1.5 %collective-permute-start.12 = (f32[192,512]{1,0:T(8,128)S(1)}, f32[192,512]{1,0:T(8,128)S(1)}, u32[]{:S(2)}, u32[]{:S(2)}) collective-permute-start(f32[192,512]{1,0:T(8,128)S(1)} %get-tuple-element.199), channel_id=1, source_target_pairs={{0,16},{4,20},{8,24},{12,28},{16,0},{20,4},{24,8},{28,12},{1,17},{... | collective-permute-start | bytes 1179656 | tf_op jit(solution)/shard_map/ppermute | solution.py:19
  11.7 0.5 collective-permute-start.13
  12.3 8.5 %collective-permute-done.11 = f32[192,512]{1,0:T(8,128)S(1)} collective-permute-done((f32[192,512]{1,0:T(8,128)S(1)}, f32[192,512]{1,0:T(8,128)S(1)}, u32[]{:S(2)}, u32[]{:S(2)}) %collective-permute-start.11) | collective-permute-done | bytes 393248 | tf_op jit(solution)/shard_map/ppermute | solution.py:19
  20.8 7.9 %collective-permute-done.12 = f32[192,512]{1,0:T(8,128)S(1)} collective-permute-done((f32[192,512]{1,0:T(8,128)S(1)}, f32[192,512]{1,0:T(8,128)S(1)}, u32[]{:S(2)}, u32[]{:S(2)}) %collective-permute-start.12) | collective-permute-done | bytes 393248 | tf_op jit(solution)/shard_map/ppermute | solution.py:19
  28.9 0.6 collective-permute-done.9
  29.5 2.8 %collective-permute-start.14 = (f32[320,512]{1,0:T(8,128)S(1)}, f32[320,512]{1,0:T(8,128)S(1)}, u32[]{:S(2)}, u32[]{:S(2)}) collective-permute-start(f32[320,512]{1,0:T(8,128)S(1)} %slice.56.g_ref), channel_id=1, source_target_pairs={{0,1},{1,0},{2,3},{3,2},{4,5},{5,4},{6,7},{7,6},{8,9},{9,8},{10,11... | collective-permute-start | bytes 1966088 | tf_op jit(solution)/shard_map/ppermute | solution.py:19
  32.3 1.6 %collective-permute-start.18 = (f32[320,512]{1,0:T(8,128)S(1)}, f32[320,512]{1,0:T(8,128)S(1)}, u32[]{:S(2)}, u32[]{:S(2)}) collective-permute-start(f32[320,512]{1,0:T(8,128)S(1)} %slice.55.x_ref), channel_id=1, source_target_pairs={{0,2},{1,3},{2,0},{3,1},{4,6},{5,7},{6,4},{7,5},{8,10},{9,11},{10,... | collective-permute-start | bytes 1966088 | tf_op jit(solution)/shard_map/ppermute | solution.py:19
  33.9 1.6 %collective-permute-start.15 = (f32[128,512]{1,0:T(8,128)S(1)}, f32[128,512]{1,0:T(8,128)S(1)}, u32[]{:S(2)}, u32[]{:S(2)}) collective-permute-start(f32[128,512]{1,0:T(8,128)S(1)} %pad_maximum_fusion.3), channel_id=1, source_target_pairs={{0,8},{4,12},{8,0},{12,4},{16,24},{20,28},{24,16},{28,20},{1,9},{5... | collective-permute-start | bytes 786440 | tf_op jit(solution)/shard_map/ppermute | solution.py:19
  35.5 1.5 %collective-permute-start.16 = (f32[128,512]{1,0:T(8,128)S(1)}, f32[128,512]{1,0:T(8,128)S(1)}, u32[]{:S(2)}, u32[]{:S(2)}) collective-permute-start(f32[128,512]{1,0:T(8,128)S(1)} %pad_maximum_fusion.3), channel_id=1, source_target_pairs={{0,16},{4,20},{8,24},{12,28},{16,0},{20,4},{24,8},{28,12},{1,17},{... | collective-permute-start | bytes 786440 | tf_op jit(solution)/shard_map/ppermute | solution.py:19
  37.6 5.6 %collective-permute-done.15 = f32[128,512]{1,0:T(8,128)S(1)} collective-permute-done((f32[128,512]{1,0:T(8,128)S(1)}, f32[128,512]{1,0:T(8,128)S(1)}, u32[]{:S(2)}, u32[]{:S(2)}) %collective-permute-start.15) | collective-permute-done | bytes 262176 | tf_op jit(solution)/shard_map/ppermute | solution.py:19
  43.2 4.2 %collective-permute-done.16 = f32[128,512]{1,0:T(8,128)S(1)} collective-permute-done((f32[128,512]{1,0:T(8,128)S(1)}, f32[128,512]{1,0:T(8,128)S(1)}, u32[]{:S(2)}, u32[]{:S(2)}) %collective-permute-start.16) | collective-permute-done | bytes 262176 | tf_op jit(solution)/shard_map/ppermute | solution.py:19
  47.5 16.7 %conditional.3 = (f32[64,512]{1,0:T(8,128)S(1)}, bf16[1,512,512]{2,1,0:T(8,128)(2,1)S(1)}, bf16[1,512,512]{2,1,0:T(8,128)(2,1)S(1)}, bf16[2,512,512]{2,1,0:T(8,1...) conditional(s32[]{:T(128)} %bitcast.12, () %tuple.38, ...), branch_computations={%region_0.0_spmd, %region_1.0_spmd} | conditional | flops 2850818 | bytes 26607920 | solution.py:415
  47.5 1.1 maximum_bitcast_fusion
  49.0 1.1 branch_1_fun.4
  50.2 0.6 collective-permute-start
  50.7 4.0 %collective-permute-done = f32[4,64,512]{2,1,0:T(8,128)S(1)} collective-permute-done((f32[4,64,512]{2,1,0:T(8,128)S(1)}, f32[4,64,512]{2,1,0:T(8,128)S(1)}, u32[]{:S(2)}, u32[]{:S(2)}) %collective-permute-start) | collective-permute-done | bytes 524320 | tf_op jit(solution)/shard_map/cond/branch_1_fun/ppermute | solution.py:19
  54.7 1.3 %collective-permute-start.2 = (f32[64,512]{1,0:T(8,128)S(1)}, f32[64,512]{1,0:T(8,128)S(1)}, u32[]{:S(2)}, u32[]{:S(2)}) collective-permute-start(f32[64,512]{1,0:T(8,128)S(1)} %get-tuple-element.249), channel_id=1, source_target_pairs={{0,8},{4,12},{8,0},{12,4},{16,24},{20,28},{24,16},{28,20},{1,9},{5... | collective-permute-start | bytes 393224 | tf_op jit(solution)/shard_map/cond/branch_1_fun/ppermute | solution.py:19
  56.0 0.8 collective-permute-start.3
  56.9 1.4 %collective-permute-start.4 = (f32[64,512]{1,0:T(8,128)S(1)}, f32[64,512]{1,0:T(8,128)S(1)}, u32[]{:S(2)}, u32[]{:S(2)}) collective-permute-start(f32[64,512]{1,0:T(8,128)S(1)} %get-tuple-element.250), channel_id=1, source_target_pairs={{0,24},{4,28},{8,16},{12,20},{16,8},{20,12},{24,0},{28,4},{1,25},{... | collective-permute-start | bytes 393224 | tf_op jit(solution)/shard_map/cond/branch_1_fun/ppermute | solution.py:19
  58.3 3.7 %branch_1_fun.5 = (bf16[1,512,512]{2,1,0:T(8,128)(2,1)S(1)}, bf16[1,512,512]{2,1,0:T(8,128)(2,1)S(1)}, bf16[2,512,512]{2,1,0:T(8,128)(2,1)S(1)}, bf16[2,512,512]...) custom-call(f32[4,320,512]{2,1,0:T(8,128)S(1)} %pad_maximum_fusion.r, ...), custom_call_target="tpu_custom_call" | custom-call | flops 1 | bytes 1 | tf_op jit(solution)/shard_map/cond/branch_1_fun/pallas_call | solution.py:59
  62.5 1.6 %collective-permute-done.4 = f32[64,512]{1,0:T(8,128)S(1)} collective-permute-done((f32[64,512]{1,0:T(8,128)S(1)}, f32[64,512]{1,0:T(8,128)S(1)}, u32[]{:S(2)}, u32[]{:S(2)}) %collective-permute-start.4) | collective-permute-done | bytes 131104 | tf_op jit(solution)/shard_map/cond/branch_1_fun/ppermute | solution.py:19
  64.6 1.3 %collective-permute-start.20 = (f32[192,512]{1,0:T(8,128)}, f32[192,512]{1,0:T(8,128)S(1)}, u32[]{:S(2)}, u32[]{:S(2)}) collective-permute-start(f32[192,512]{1,0:T(8,128)} %get-tuple-element.218), channel_id=1, source_target_pairs={{0,2},{1,3},{2,0},{3,1},{4,6},{5,7},{6,4},{7,5},{8,10},{9,11},{10,... | collective-permute-start | bytes 1179656 | tf_op jit(solution)/shard_map/ppermute | solution.py:19
  66.0 2.7 %shard_map.102 = (f32[320,256]{1,0:T(8,128)S(1)}, f32[320,256]{1,0:T(8,128)S(1)}, f32[320,512]{1,0:T(8,128)S(1)}, f32[320,512]{1,0:T(8,128)S(1)}) custom-call(f32[320,512]{1,0:T(8,128)S(1)} %slice.55.x_ref, f32[320,512]{1,0:T(8,128)S(1)} %slice.56.g_ref, f32[320,512]{1,0:T(8,128)S(1)} %collective-permute-done.18.far_ref, ...), custom_call_target="tpu_custom_call" | custom-call | flops 1 | bytes 1 | tf_op jit(solution)/shard_map/pallas_call | solution.py:59
  69.0 1.0 pad_maximum_fusion.2
  70.1 1.0 pad_maximum_fusion.1
  71.3 0.8 copy-done.9
  72.1 10.3 %conditional.4 = (f32[256,512]{1,0:T(8,128)S(1)}, f32[256,512]{1,0:T(8,128)S(1)}, f32[256,512]{1,0:T(8,128)S(1)}, f32[256,512]{1,0:T(8,128)S(1)}) conditional(s32[]{:T(128)} %bitcast.12, () %tuple.40, (f32[512,512]{1,0:T(8,128)S(1)}, f32[512,512]{1,0:T(8,128)S(1)}, f32[512,512]{1,0:T(8,128)}, f32[512,256]{1,0:T(8,128)S(1)}, f32[512,256]{1,0:T(8,128)S(1)}, ...), branch_computations={%region_2.0_spmd, %region_3.0_spmd} | conditional | flops 524289 | bytes 14680137 | solution.py:481
  72.3 5.4 %branch_1_fun.6 = (f32[256,512]{1,0:T(8,128)S(1)}, f32[256,512]{1,0:T(8,128)S(1)}, f32[256,512]{1,0:T(8,128)S(1)}, f32[256,512]{1,0:T(8,128)S(1)}, f32[4,256,512]{2,1,0:T(8,128)S(1)}) custom-call(f32[512,512]{1,0:T(8,128)S(1)} %get-tuple-element.103.refs_0_, f32[512,512]{1,0:T(8,128)S(1)} %get-tuple-element.104.refs_1_, ...), custom_call_target="tpu_custom_call" | custom-call | flops 1 | bytes 1 | tf_op jit(solution)/shard_map/cond/branch_1_fun/pallas_call | solution.py:59
  77.8 4.1 %collective-permute-done.5 = f32[4,256,512]{2,1,0:T(8,128)S(1)} collective-permute-done((f32[4,256,512]{2,1,0:T(8,128)S(1)}, f32[4,256,512]{2,1,0:T(8,128)S(1)}, u32[]{:S(2)}, u32[]{:S(2)}) %collective-permute-start.5) | collective-permute-done | bytes 2097184 | tf_op jit(solution)/shard_map/cond/branch_1_fun/ppermute | solution.py:19
  82.4 0.7 collective-permute-done.19.ahead_ref
  83.1 1.2 collective-permute-done.20.back_ref
  84.7 2.6 %collective-permute-start.22 = (f32[320,512]{1,0:T(8,128)S(1)}, f32[320,512]{1,0:T(8,128)S(1)}, u32[]{:S(2)}, u32[]{:S(2)}) collective-permute-start(f32[320,512]{1,0:T(8,128)S(1)} %copy-done.2), channel_id=1, source_target_pairs={{0,2},{1,3},{2,0},{3,1},{4,6},{5,7},{6,4},{7,5},{8,10},{9,11},{10,... | collective-permute-start | bytes 1966088 | tf_op jit(solution)/shard_map/ppermute | solution.py:19
  87.3 23.9 %conditional.5 = (f32[512,512]{1,0:T(8,128)S(1)}, f32[512,512]{1,0:T(8,128)S(1)}, f32[96,512]{1,0:T(8,128)S(1)}, f32[32,512]{1,0:T(8,128)S(1)}, f32[128,512]{1,0:T(8,128)S(1)}) conditional(s32[]{:T(128)} %bitcast.12, () %tuple.36, (f32[512,512]{1,0:T(8,128)}, f32[512,512]{1,0:T(8,128)}, f32[512,512]{1,0:T(8,128)}, f32[512,256]{1,0:T(8,128)}, ...), branch_computations={%region_4.0_spmd, %region_5.0_spmd} | conditional | flops 393217 | bytes 9961633 | solution.py:508
  87.7 1.4 %collective-permute-start.7 = (f32[256,512]{1,0:T(8,128)S(1)}, f32[256,512]{1,0:T(8,128)S(1)}, u32[]{:S(2)}, u32[]{:S(2)}) collective-permute-start(f32[256,512]{1,0:T(8,128)S(1)} %get-tuple-element.132), channel_id=1, source_target_pairs={{0,16},{4,20},{8,24},{12,28},{16,0},{20,4},{24,8},{28,12},{1,17},{... | collective-permute-start | bytes 1572872 | tf_op jit(solution)/shard_map/cond/branch_1_fun/ppermute | solution.py:19
  89.1 1.7 %collective-permute-start.8 = (f32[256,512]{1,0:T(8,128)S(1)}, f32[256,512]{1,0:T(8,128)S(1)}, u32[]{:S(2)}, u32[]{:S(2)}) collective-permute-start(f32[256,512]{1,0:T(8,128)S(1)} %get-tuple-element.133), channel_id=1, source_target_pairs={{0,24},{4,28},{8,16},{12,20},{16,8},{20,12},{24,0},{28,4},{1,25},{... | collective-permute-start | bytes 1572872 | tf_op jit(solution)/shard_map/cond/branch_1_fun/ppermute | solution.py:19
  90.8 7.9 %branch_1_fun.7 = (f32[512,512]{1,0:T(8,128)S(1)}, f32[512,512]{1,0:T(8,128)S(1)}) custom-call(f32[512,512]{1,0:T(8,128)} %get-tuple-element.114.refs_0_, f32[512,512]{1,0:T(8,128)} %get-tuple-element.115.refs_1_, f32[512,512]{1,0:T(8,128)} %get-tuple-element.116.refs_2_, f32[512,256]{1,0:T(8,128)} %get-tuple-element.117.refs_3_, ...), custom_call_target="tpu_custom_call" | custom-call | flops 1 | bytes 1 | tf_op jit(solution)/shard_map/cond/branch_1_fun/pallas_call | solution.py:59
  98.8 3.4 %collective-permute-done.6 = f32[256,512]{1,0:T(8,128)S(1)} collective-permute-done((f32[256,512]{1,0:T(8,128)S(1)}, f32[256,512]{1,0:T(8,128)S(1)}, u32[]{:S(2)}, u32[]{:S(2)}) %collective-permute-start.6) | collective-permute-done | bytes 524320 | tf_op jit(solution)/shard_map/cond/branch_1_fun/ppermute | solution.py:19
  102.2 8.8 %collective-permute-done.7 = f32[256,512]{1,0:T(8,128)S(1)} collective-permute-done((f32[256,512]{1,0:T(8,128)S(1)}, f32[256,512]{1,0:T(8,128)S(1)}, u32[]{:S(2)}, u32[]{:S(2)}) %collective-permute-start.7) | collective-permute-done | bytes 524320 | tf_op jit(solution)/shard_map/cond/branch_1_fun/ppermute | solution.py:19
  111.7 1.3 %collective-permute-start.24 = (f32[32,512]{1,0:T(8,128)S(1)}, f32[32,512]{1,0:T(8,128)S(1)}, u32[]{:S(2)}, u32[]{:S(2)}) collective-permute-start(f32[32,512]{1,0:T(8,128)S(1)} %get-tuple-element.245), channel_id=1, source_target_pairs={{0,2},{1,3},{2,0},{3,1},{4,6},{5,7},{6,4},{7,5},{8,10},{9,11},{10,... | collective-permute-start | bytes 196616 | tf_op jit(solution)/shard_map/ppermute | solution.py:19
  113.2 1.4 %collective-permute-done.21.ahead_ref = f32[320,512]{1,0:T(8,128)S(1)} collective-permute-done((f32[320,512]{1,0:T(8,128)}, f32[320,512]{1,0:T(8,128)S(1)}, u32[]{:S(2)}, u32[]{:S(2)}) %collective-permute-start.21) | collective-permute-done | bytes 655392 | tf_op jit(solution)/shard_map/ppermute | solution.py:19
  114.5 2.0 %collective-permute-done.22.back_ref = f32[320,512]{1,0:T(8,128)S(1)} collective-permute-done((f32[320,512]{1,0:T(8,128)S(1)}, f32[320,512]{1,0:T(8,128)S(1)}, u32[]{:S(2)}, u32[]{:S(2)}) %collective-permute-start.22) | collective-permute-done | bytes 655392 | tf_op jit(solution)/shard_map/ppermute | solution.py:19
  116.7 1.6 %collective-permute-done.24.refs_4_ = f32[32,512]{1,0:T(8,128)S(1)} collective-permute-done((f32[32,512]{1,0:T(8,128)S(1)}, f32[32,512]{1,0:T(8,128)S(1)}, u32[]{:S(2)}, u32[]{:S(2)}) %collective-permute-start.24) | collective-permute-done | bytes 65568 | tf_op jit(solution)/shard_map/ppermute | solution.py:19
  118.4 0.7 collective-permute-done.23.refs_3_
  119.1 1.4 %shard_map.105 = (f32[1,3,64,512]{3,2,1,0:T(8,128)}, f32[1,64,256]{2,1,0:T(8,128)}, f32[1,32,512]{2,1,0:T(8,128)}) custom-call(s32[1,2]{1,0:T(1,128)S(1)} %copy-done, f32[64,512]{1,0:T(8,128)S(1)} %get-tuple-element.242.refs_1_, f32[128,512]{1,0:T(8,128)S(1)} %get-tuple-element.243.refs_2_, f32[96,512]{1,0:T(8,128)S(1)} %collective-permute-done.23.refs_3_, ...), custom_call_target="tpu_custom_call" | custom-call | flops 1 | bytes 1 | tf_op jit(solution)/shard_map/pallas_call | solution.py:59
  (90 shorter events, 5.0 us)
Async XLA Ops:
  0.6 11.6 %copy-start.4 = (f32[512,512]{1,0:T(8,128)S(1)}, f32[512,512]{1,0:T(8,128)}, u32[]{:S(2)}) copy-start(f32[512,512]{1,0:T(8,128)} %x_ref.1) | copy-start | bytes 3145732
  0.6 11.6 %copy-start.7 = (f32[512,512]{1,0:T(8,128)S(1)}, f32[512,512]{1,0:T(8,128)}, u32[]{:S(2)}) copy-start(f32[512,512]{1,0:T(8,128)} %g_ref.1) | copy-start | bytes 3145732
  0.7 36.8 %copy-start = (s32[1,2]{1,0:T(1,128)S(1)}, s32[1,2]{1,0:T(1,128)}, u32[]{:S(2)}) copy-start(s32[1,2]{1,0:T(1,128)} %refs_0_.1) | copy-start | bytes 28
  3.1 30.7 %copy-start.26 = (f32[192,512]{1,0:T(8,128)}, f32[192,512]{1,0:T(8,128)S(1)}, u32[]{:S(2)}) copy-start(f32[192,512]{1,0:T(8,128)S(1)} %get-tuple-element.199) | copy-start | bytes 1179652
  3.1 26.4 %collective-permute-start.9 = (f32[288,512]{1,0:T(8,128)}, f32[288,512]{1,0:T(8,128)S(1)}, u32[]{:S(2)}, u32[]{:S(2)}) collective-permute-start(f32[288,512]{1,0:T(8,128)} %get-tuple-element.194), channel_id=1, source_target_pairs={{0,1},{1,0},{2,3},{3,2},{4,5},{5,4},{6,7},{7,6},{8,9},{9,8},{10,11... | collective-permute-start | bytes 1769480 | tf_op jit(solution)/shard_map/ppermute | solution.py:19
  6.1 22.7 %collective-permute-start.10 = (f32[224,512]{1,0:T(8,128)}, f32[224,512]{1,0:T(8,128)S(1)}, u32[]{:S(2)}, u32[]{:S(2)}) collective-permute-start(f32[224,512]{1,0:T(8,128)} %get-tuple-element.195), channel_id=1, source_target_pairs={{0,2},{1,3},{2,0},{3,1},{4,6},{5,7},{6,4},{7,5},{8,10},{9,11},{10,... | collective-permute-start | bytes 1376264 | tf_op jit(solution)/shard_map/ppermute | solution.py:19
  8.7 38.7 %copy-start.5 = (f32[512,512]{1,0:T(8,128)S(1)}, f32[512,512]{1,0:T(8,128)}, u32[]{:S(2)}) copy-start(f32[512,512]{1,0:T(8,128)} %x_ref.1) | copy-start | bytes 3145732
  8.7 38.7 %copy-start.8 = (f32[512,512]{1,0:T(8,128)S(1)}, f32[512,512]{1,0:T(8,128)}, u32[]{:S(2)}) copy-start(f32[512,512]{1,0:T(8,128)} %g_ref.1) | copy-start | bytes 3145732
  8.7 12.1 %collective-permute-start.11 = (f32[192,512]{1,0:T(8,128)S(1)}, f32[192,512]{1,0:T(8,128)S(1)}, u32[]{:S(2)}, u32[]{:S(2)}) collective-permute-start(f32[192,512]{1,0:T(8,128)S(1)} %get-tuple-element.199), channel_id=1, source_target_pairs={{0,8},{4,12},{8,0},{12,4},{16,24},{20,28},{24,16},{28,20},{1,9},{5... | collective-permute-start | bytes 1179656 | tf_op jit(solution)/shard_map/ppermute | solution.py:19
  10.2 18.4 %collective-permute-start.12 = (f32[192,512]{1,0:T(8,128)S(1)}, f32[192,512]{1,0:T(8,128)S(1)}, u32[]{:S(2)}, u32[]{:S(2)}) collective-permute-start(f32[192,512]{1,0:T(8,128)S(1)} %get-tuple-element.199), channel_id=1, source_target_pairs={{0,16},{4,20},{8,24},{12,28},{16,0},{20,4},{24,8},{28,12},{1,17},{... | collective-permute-start | bytes 1179656 | tf_op jit(solution)/shard_map/ppermute | solution.py:19
  11.7 16.9 %collective-permute-start.13 = (f32[192,512]{1,0:T(8,128)S(1)}, f32[192,512]{1,0:T(8,128)S(1)}, u32[]{:S(2)}, u32[]{:S(2)}) collective-permute-start(f32[192,512]{1,0:T(8,128)S(1)} %get-tuple-element.199), channel_id=1, source_target_pairs={{0,24},{4,28},{8,16},{12,20},{16,8},{20,12},{24,0},{28,4},{1,25},{... | collective-permute-start | bytes 1179656 | tf_op jit(solution)/shard_map/ppermute | solution.py:19
  29.5 36.5 %collective-permute-start.14 = (f32[320,512]{1,0:T(8,128)S(1)}, f32[320,512]{1,0:T(8,128)S(1)}, u32[]{:S(2)}, u32[]{:S(2)}) collective-permute-start(f32[320,512]{1,0:T(8,128)S(1)} %slice.56.g_ref), channel_id=1, source_target_pairs={{0,1},{1,0},{2,3},{3,2},{4,5},{5,4},{6,7},{7,6},{8,9},{9,8},{10,11... | collective-permute-start | bytes 1966088 | tf_op jit(solution)/shard_map/ppermute | solution.py:19
  32.3 33.7 %collective-permute-start.18 = (f32[320,512]{1,0:T(8,128)S(1)}, f32[320,512]{1,0:T(8,128)S(1)}, u32[]{:S(2)}, u32[]{:S(2)}) collective-permute-start(f32[320,512]{1,0:T(8,128)S(1)} %slice.55.x_ref), channel_id=1, source_target_pairs={{0,2},{1,3},{2,0},{3,1},{4,6},{5,7},{6,4},{7,5},{8,10},{9,11},{10,... | collective-permute-start | bytes 1966088 | tf_op jit(solution)/shard_map/ppermute | solution.py:19
  33.9 9.3 %collective-permute-start.15 = (f32[128,512]{1,0:T(8,128)S(1)}, f32[128,512]{1,0:T(8,128)S(1)}, u32[]{:S(2)}, u32[]{:S(2)}) collective-permute-start(f32[128,512]{1,0:T(8,128)S(1)} %pad_maximum_fusion.3), channel_id=1, source_target_pairs={{0,8},{4,12},{8,0},{12,4},{16,24},{20,28},{24,16},{28,20},{1,9},{5... | collective-permute-start | bytes 786440 | tf_op jit(solution)/shard_map/ppermute | solution.py:19
  35.5 12.0 %collective-permute-start.16 = (f32[128,512]{1,0:T(8,128)S(1)}, f32[128,512]{1,0:T(8,128)S(1)}, u32[]{:S(2)}, u32[]{:S(2)}) collective-permute-start(f32[128,512]{1,0:T(8,128)S(1)} %pad_maximum_fusion.3), channel_id=1, source_target_pairs={{0,16},{4,20},{8,24},{12,28},{16,0},{20,4},{24,8},{28,12},{1,17},{... | collective-permute-start | bytes 786440 | tf_op jit(solution)/shard_map/ppermute | solution.py:19
  37.0 10.4 %collective-permute-start.17 = (f32[128,512]{1,0:T(8,128)S(1)}, f32[128,512]{1,0:T(8,128)S(1)}, u32[]{:S(2)}, u32[]{:S(2)}) collective-permute-start(f32[128,512]{1,0:T(8,128)S(1)} %pad_maximum_fusion.3), channel_id=1, source_target_pairs={{0,24},{4,28},{8,16},{12,20},{16,8},{20,12},{24,0},{28,4},{1,25},{... | collective-permute-start | bytes 786440 | tf_op jit(solution)/shard_map/ppermute | solution.py:19
  37.5 9.9 %copy-start.18 = (f32[192,512]{1,0:T(8,128)}, f32[192,512]{1,0:T(8,128)S(1)}, u32[]{:S(2)}) copy-start(f32[192,512]{1,0:T(8,128)S(1)} %slice.57) | copy-start | bytes 1179652
  37.6 9.9 %copy-start.20 = (f32[192,512]{1,0:T(8,128)}, f32[192,512]{1,0:T(8,128)S(1)}, u32[]{:S(2)}) copy-start(f32[192,512]{1,0:T(8,128)S(1)} %slice.60) | copy-start | bytes 1179652
  49.0 5.7 %collective-permute-start.1 = (f32[4,320,512]{2,1,0:T(8,128)S(1)}, f32[4,320,512]{2,1,0:T(8,128)S(1)}, u32[]{:S(2)}, u32[]{:S(2)}) collective-permute-start(f32[4,320,512]{2,1,0:T(8,128)S(1)} %pad_maximum_fusion.refs_0_), channel_id=1, source_target_pairs={{0,4},{4,0},{8,12},{12,8},{16,20},{20,16},{24,28},{28,24},{1,5},{5... | collective-permute-start | bytes 7864328 | tf_op jit(solution)/shard_map/cond/branch_1_fun/ppermute | solution.py:19
  50.2 4.5 %collective-permute-start = (f32[4,64,512]{2,1,0:T(8,128)S(1)}, f32[4,64,512]{2,1,0:T(8,128)S(1)}, u32[]{:S(2)}, u32[]{:S(2)}) collective-permute-start(f32[4,64,512]{2,1,0:T(8,128)S(1)} %get-tuple-element.75), channel_id=1, source_target_pairs={{0,4},{4,0},{8,12},{12,8},{16,20},{20,16},{24,28},{28,24},{1,5},{5... | collective-permute-start | bytes 1572872 | tf_op jit(solution)/shard_map/cond/branch_1_fun/ppermute | solution.py:19
  54.7 7.3 %collective-permute-start.2 = (f32[64,512]{1,0:T(8,128)S(1)}, f32[64,512]{1,0:T(8,128)S(1)}, u32[]{:S(2)}, u32[]{:S(2)}) collective-permute-start(f32[64,512]{1,0:T(8,128)S(1)} %get-tuple-element.249), channel_id=1, source_target_pairs={{0,8},{4,12},{8,0},{12,4},{16,24},{20,28},{24,16},{28,20},{1,9},{5... | collective-permute-start | bytes 393224 | tf_op jit(solution)/shard_map/cond/branch_1_fun/ppermute | solution.py:19
  56.0 6.4 %collective-permute-start.3 = (f32[64,512]{1,0:T(8,128)S(1)}, f32[64,512]{1,0:T(8,128)S(1)}, u32[]{:S(2)}, u32[]{:S(2)}) collective-permute-start(f32[64,512]{1,0:T(8,128)S(1)} %get-tuple-element.251), channel_id=1, source_target_pairs={{0,16},{4,20},{8,24},{12,28},{16,0},{20,4},{24,8},{28,12},{1,17},{... | collective-permute-start | bytes 393224 | tf_op jit(solution)/shard_map/cond/branch_1_fun/ppermute | solution.py:19
  56.9 7.2 %collective-permute-start.4 = (f32[64,512]{1,0:T(8,128)S(1)}, f32[64,512]{1,0:T(8,128)S(1)}, u32[]{:S(2)}, u32[]{:S(2)}) collective-permute-start(f32[64,512]{1,0:T(8,128)S(1)} %get-tuple-element.250), channel_id=1, source_target_pairs={{0,24},{4,28},{8,16},{12,20},{16,8},{20,12},{24,0},{28,4},{1,25},{... | collective-permute-start | bytes 393224 | tf_op jit(solution)/shard_map/cond/branch_1_fun/ppermute | solution.py:19
  64.2 4.6 %copy-start.10 = (bf16[2,512,512]{2,1,0:T(8,128)(2,1)}, bf16[2,512,512]{2,1,0:T(8,128)(2,1)S(1)}, u32[]{:S(2)}) copy-start(bf16[2,512,512]{2,1,0:T(8,128)(2,1)S(1)} %get-tuple-element.206.wh) | copy-start | bytes 3145732
  64.2 4.6 %copy-start.14 = (bf16[2,512,256]{2,1,0:T(8,128)(2,1)}, bf16[2,512,256]{2,1,0:T(8,128)(2,1)S(1)}, u32[]{:S(2)}) copy-start(bf16[2,512,256]{2,1,0:T(8,128)(2,1)S(1)} %get-tuple-element.208.lh) | copy-start | bytes 1572868
  64.2 4.6 %copy-start.15 = (bf16[2,512,256]{2,1,0:T(8,128)(2,1)}, bf16[2,512,256]{2,1,0:T(8,128)(2,1)S(1)}, u32[]{:S(2)}) copy-start(bf16[2,512,256]{2,1,0:T(8,128)(2,1)S(1)} %get-tuple-element.209.ll) | copy-start | bytes 1572868
  64.2 4.6 %copy-start.16 = (bf16[2,256,512]{2,1,0:T(8,128)(2,1)}, bf16[2,256,512]{2,1,0:T(8,128)(2,1)S(1)}, u32[]{:S(2)}) copy-start(bf16[2,256,512]{2,1,0:T(8,128)(2,1)S(1)} %get-tuple-element.210.rh) | copy-start | bytes 1572868
  64.2 4.6 %copy-start.17 = (bf16[2,256,512]{2,1,0:T(8,128)(2,1)}, bf16[2,256,512]{2,1,0:T(8,128)(2,1)S(1)}, u32[]{:S(2)}) copy-start(bf16[2,256,512]{2,1,0:T(8,128)(2,1)S(1)} %get-tuple-element.211.rl) | copy-start | bytes 1572868
  64.2 4.6 %copy-start.24 = (bf16[1,512,512]{2,1,0:T(8,128)(2,1)}, bf16[1,512,512]{2,1,0:T(8,128)(2,1)S(1)}, u32[]{:S(2)}) copy-start(bf16[1,512,512]{2,1,0:T(8,128)(2,1)S(1)} %get-tuple-element.215) | copy-start | bytes 1572868
  64.2 4.6 %copy-start.25 = (bf16[1,512,512]{2,1,0:T(8,128)(2,1)}, bf16[1,512,512]{2,1,0:T(8,128)(2,1)S(1)}, u32[]{:S(2)}) copy-start(bf16[1,512,512]{2,1,0:T(8,128)(2,1)S(1)} %get-tuple-element.216) | copy-start | bytes 1572868
  64.2 7.9 %copy-start.11 = (bf16[2,512,512]{2,1,0:T(8,128)(2,1)}, bf16[2,512,512]{2,1,0:T(8,128)(2,1)S(1)}, u32[]{:S(2)}) copy-start(bf16[2,512,512]{2,1,0:T(8,128)(2,1)S(1)} %get-tuple-element.207.wl) | copy-start | bytes 3145732
  64.2 18.9 %collective-permute-start.19 = (f32[192,512]{1,0:T(8,128)}, f32[192,512]{1,0:T(8,128)S(1)}, u32[]{:S(2)}, u32[]{:S(2)}) collective-permute-start(f32[192,512]{1,0:T(8,128)} %get-tuple-element.217), channel_id=1, source_target_pairs={{0,1},{1,0},{2,3},{3,2},{4,5},{5,4},{6,7},{7,6},{8,9},{9,8},{10,11... | collective-permute-start | bytes 1179656 | tf_op jit(solution)/shard_map/ppermute | solution.py:19
  64.6 19.7 %collective-permute-start.20 = (f32[192,512]{1,0:T(8,128)}, f32[192,512]{1,0:T(8,128)S(1)}, u32[]{:S(2)}, u32[]{:S(2)}) collective-permute-start(f32[192,512]{1,0:T(8,128)} %get-tuple-element.218), channel_id=1, source_target_pairs={{0,2},{1,3},{2,0},{3,1},{4,6},{5,7},{6,4},{7,5},{8,10},{9,11},{10,... | collective-permute-start | bytes 1179656 | tf_op jit(solution)/shard_map/ppermute | solution.py:19
  68.8 3.3 %copy-start.3 = (f32[320,512]{1,0:T(8,128)}, f32[320,512]{1,0:T(8,128)S(1)}, u32[]{:S(2)}) copy-start(f32[320,512]{1,0:T(8,128)S(1)} %get-tuple-element.235) | copy-start | bytes 1966084
  68.9 3.2 %copy-start.9 = (f32[512,512]{1,0:T(8,128)S(1)}, f32[512,512]{1,0:T(8,128)}, u32[]{:S(2)}) copy-start(f32[512,512]{1,0:T(8,128)} %g_ref.1) | copy-start | bytes 3145732
  68.9 3.2 %copy-start.23 = (f32[512,256]{1,0:T(8,128)}, f32[512,256]{1,0:T(8,128)S(1)}, u32[]{:S(2)}) copy-start(f32[512,256]{1,0:T(8,128)S(1)} %constant_dynamic-update-slice_fusion.2) | copy-start | bytes 1572868
  68.9 3.2 %copy-start.22 = (f32[512,256]{1,0:T(8,128)}, f32[512,256]{1,0:T(8,128)S(1)}, u32[]{:S(2)}) copy-start(f32[512,256]{1,0:T(8,128)S(1)} %constant_dynamic-update-slice_fusion) | copy-start | bytes 1572868
  72.1 12.6 %copy-start.2 = (f32[320,512]{1,0:T(8,128)S(1)}, f32[320,512]{1,0:T(8,128)}, u32[]{:S(2)}) copy-start(f32[320,512]{1,0:T(8,128)} %copy-done.1) | copy-start | bytes 1966084
  77.7 4.2 %collective-permute-start.5 = (f32[4,256,512]{2,1,0:T(8,128)S(1)}, f32[4,256,512]{2,1,0:T(8,128)S(1)}, u32[]{:S(2)}, u32[]{:S(2)}) collective-permute-start(f32[4,256,512]{2,1,0:T(8,128)S(1)} %get-tuple-element.110), channel_id=1, source_target_pairs={{0,4},{4,0},{8,12},{12,8},{16,20},{20,16},{24,28},{28,24},{1,5},{5... | collective-permute-start | bytes 6291464 | tf_op jit(solution)/shard_map/cond/branch_1_fun/ppermute | solution.py:19
  84.3 30.2 %collective-permute-start.21 = (f32[320,512]{1,0:T(8,128)}, f32[320,512]{1,0:T(8,128)S(1)}, u32[]{:S(2)}, u32[]{:S(2)}) collective-permute-start(f32[320,512]{1,0:T(8,128)} %copy-done.3), channel_id=1, source_target_pairs={{0,1},{1,0},{2,3},{3,2},{4,5},{5,4},{6,7},{7,6},{8,9},{9,8},{10,11... | collective-permute-start | bytes 1966088 | tf_op jit(solution)/shard_map/ppermute | solution.py:19
  84.7 31.8 %collective-permute-start.22 = (f32[320,512]{1,0:T(8,128)S(1)}, f32[320,512]{1,0:T(8,128)S(1)}, u32[]{:S(2)}, u32[]{:S(2)}) collective-permute-start(f32[320,512]{1,0:T(8,128)S(1)} %copy-done.2), channel_id=1, source_target_pairs={{0,2},{1,3},{2,0},{3,1},{4,6},{5,7},{6,4},{7,5},{8,10},{9,11},{10,... | collective-permute-start | bytes 1966088 | tf_op jit(solution)/shard_map/ppermute | solution.py:19
  87.3 14.9 %collective-permute-start.6 = (f32[256,512]{1,0:T(8,128)S(1)}, f32[256,512]{1,0:T(8,128)S(1)}, u32[]{:S(2)}, u32[]{:S(2)}) collective-permute-start(f32[256,512]{1,0:T(8,128)S(1)} %get-tuple-element.131), channel_id=1, source_target_pairs={{0,8},{4,12},{8,0},{12,4},{16,24},{20,28},{24,16},{28,20},{1,9},{5... | collective-permute-start | bytes 1572872 | tf_op jit(solution)/shard_map/cond/branch_1_fun/ppermute | solution.py:19
  87.7 23.3 %collective-permute-start.7 = (f32[256,512]{1,0:T(8,128)S(1)}, f32[256,512]{1,0:T(8,128)S(1)}, u32[]{:S(2)}, u32[]{:S(2)}) collective-permute-start(f32[256,512]{1,0:T(8,128)S(1)} %get-tuple-element.132), channel_id=1, source_target_pairs={{0,16},{4,20},{8,24},{12,28},{16,0},{20,4},{24,8},{28,12},{1,17},{... | collective-permute-start | bytes 1572872 | tf_op jit(solution)/shard_map/cond/branch_1_fun/ppermute | solution.py:19
  89.1 21.9 %collective-permute-start.8 = (f32[256,512]{1,0:T(8,128)S(1)}, f32[256,512]{1,0:T(8,128)S(1)}, u32[]{:S(2)}, u32[]{:S(2)}) collective-permute-start(f32[256,512]{1,0:T(8,128)S(1)} %get-tuple-element.133), channel_id=1, source_target_pairs={{0,24},{4,28},{8,16},{12,20},{16,8},{20,12},{24,0},{28,4},{1,25},{... | collective-permute-start | bytes 1572872 | tf_op jit(solution)/shard_map/cond/branch_1_fun/ppermute | solution.py:19
  111.3 7.9 %collective-permute-start.23 = (f32[96,512]{1,0:T(8,128)S(1)}, f32[96,512]{1,0:T(8,128)S(1)}, u32[]{:S(2)}, u32[]{:S(2)}) collective-permute-start(f32[96,512]{1,0:T(8,128)S(1)} %get-tuple-element.244), channel_id=1, source_target_pairs={{0,1},{1,0},{2,3},{3,2},{4,5},{5,4},{6,7},{7,6},{8,9},{9,8},{10,11... | collective-permute-start | bytes 589832 | tf_op jit(solution)/shard_map/ppermute | solution.py:19
  111.7 6.7 %collective-permute-start.24 = (f32[32,512]{1,0:T(8,128)S(1)}, f32[32,512]{1,0:T(8,128)S(1)}, u32[]{:S(2)}, u32[]{:S(2)}) collective-permute-start(f32[32,512]{1,0:T(8,128)S(1)} %get-tuple-element.245), channel_id=1, source_target_pairs={{0,2},{1,3},{2,0},{3,1},{4,6},{5,7},{6,4},{7,5},{8,10},{9,11},{10,... | collective-permute-start | bytes 196616 | tf_op jit(solution)/shard_map/ppermute | solution.py:19
  116.7 3.8 %copy-start.12 = (f32[512,512]{1,0:T(8,128)}, f32[512,512]{1,0:T(8,128)S(1)}, u32[]{:S(2)}) copy-start(f32[512,512]{1,0:T(8,128)S(1)} %get-tuple-element.189) | copy-start | bytes 3145732
  116.7 3.8 %copy-start.13 = (f32[512,512]{1,0:T(8,128)}, f32[512,512]{1,0:T(8,128)S(1)}, u32[]{:S(2)}) copy-start(f32[512,512]{1,0:T(8,128)S(1)} %get-tuple-element.190) | copy-start | bytes 3145732
  (4 other events, 9.1 us)

commit v3 on v2

--- a/solution.py
+++ b/solution.py
@@ -10,13 +10,57 @@
 
 F32 = jnp.float32
 BF16 = jnp.bfloat16
-VMEM_BYTES = 32 * 1024 * 1024
+EARLY = 80
+VMEM_BYTES = 20 * 1024 * 1024
+JOIN_VMEM_BYTES = 8 * 1024 * 1024
 PACK_VMEM_BYTES = 60 * 1024 * 1024
 
 
 def across(block, axis, apart):
     count = lax.axis_size(axis)
     return lax.ppermute(block, axis, [(i, i ^ apart) for i in range(count)])
+
+
+def scatter_rows(blocks, beside):
+    bits = len(blocks).bit_length() - 1
+    if not bits:
+        return blocks[0], beside
+    rows = blocks[0].shape[0]
+    cuts = [rows * g // bits // 8 * 8 for g in range(bits)] + [rows]
+    groups = [
+        {m: block[cuts[g] : cuts[g + 1]] for m, block in enumerate(blocks)} for g in range(bits)
+    ]
+    for step in range(bits):
+        turn = [(g + step) % bits for g in range(bits)]
+        sent = [[m for m in group if m >> bit & 1] for group, bit in zip(groups, turn)]
+        stacks = [jnp.stack([group[m] for m in ms]) for group, ms in zip(groups, sent)]
+        stacks = lax.optimization_barrier(stacks)
+        got = [across(stack, "dp", 2 << bit) for stack, bit in zip(stacks, turn)]
+        got, beside = lax.optimization_barrier((got, beside))
+        groups = [
+            {m ^ 1 << bit: group[m ^ 1 << bit] + part[i] for i, m in enumerate(ms)}
+            for group, ms, part, bit in zip(groups, sent, got, turn)
+        ]
+    return jnp.concatenate([group[0] for group in groups]), beside
+
+
+def gather_rows(part, count):
+    bits = (count // 2).bit_length() - 1
+    if not bits:
+        return [part]
+    rows = part.shape[0]
+    cuts = [rows * g // bits // 8 * 8 for g in range(bits)] + [rows]
+    groups = [{0: part[cuts[g] : cuts[g + 1]]} for g in range(bits)]
+    for step in range(bits):
+        turn = [(g + step) % bits for g in range(bits)]
+        stacks = [jnp.stack([group[m] for m in sorted(group)]) for group in groups]
+        got = [across(stack, "dp", 2 << bit) for stack, bit in zip(stacks, turn)]
+        got = lax.optimization_barrier(got)
+        groups = [
+            {**group, **{m ^ 1 << bit: more[i] for i, m in enumerate(sorted(group))}}
+            for group, more, bit in zip(groups, got, turn)
+        ]
+    return [jnp.concatenate([group[m] for group in groups]) for m in range(count // 2)]
 
 
 def split(value):
@@ -47,7 +91,7 @@
 
 def call(
     kernel, out_shapes, operands, grid=None, in_specs=None, out_specs=None, scratch=(),
-    vmem_bytes=VMEM_BYTES, aliases=None,
+    vmem_bytes=VMEM_BYTES,
 ):
     vmem = pl.BlockSpec(memory_space=pltpu.VMEM)
     kwargs = {}
@@ -62,7 +106,6 @@
         in_specs=in_specs,
         out_specs=out_specs,
         scratch_shapes=list(scratch),
-        input_output_aliases=aliases or {},
         cost_estimate=pl.CostEstimate(flops=1, bytes_accessed=1, transcendentals=0),
         compiler_params=pltpu.CompilerParams(vmem_limit_bytes=vmem_bytes),
         **kwargs,
@@ -124,16 +167,24 @@
     return codes, nt(g, (rh[0], rl[0])) + nt(near, (rh[1], rl[1]))
 
 
-def sends_of(x, g, codes, code_grads, wide, low, ahead_ref, back_refs):
+def put_rows(refs, value):
+    at = 0
+    for ref in refs:
+        ref[...] = value[at : at + ref.shape[0]]
+        at += ref.shape[0]
+
+
+def sends_of(x, g, codes, code_grads, wide, low, outs):
     wh, wl = wide
     lh, ll, rh, rl = low
     last = wh.shape[0] - 1
-    ahead_ref[...] = nn(x, (wh[last], wl[last])) + nn(codes, (rh[1], rl[1]))
+    cuts = len(outs) // (last + 1)
+    put_rows(outs[:cuts], nn(x, (wh[last], wl[last])) + nn(codes, (rh[1], rl[1])))
     for b in range(last):
         back = nt(g, (wh[b], wl[b]))
         if b == 0:
             back += nt(code_grads, (lh[1], ll[1]))
-        back_refs[b][...] = back
+        put_rows(outs[(b + 1) * cuts : (b + 2) * cuts], back)
 
 
 def messages(x_ref, g_ref, far_ref, near_ref, wide, low, outs):
@@ -141,7 +192,7 @@
     codes, code_grads = codes_of(x, g, split(far_ref[...]), split(near_ref[...]), low)
     outs[0][...] = codes
     outs[1][...] = code_grads
-    sends_of(x, g, split(codes), split(code_grads), wide, low, outs[2], outs[3:])
+    sends_of(x, g, split(codes), split(code_grads), wide, low, outs[2:])
 
 
 def weights_kernel(sizes, *refs):
@@ -197,7 +248,7 @@
 
 def sends_kernel(x_ref, g_ref, c_ref, cg_ref, wh, wl, lh, ll, rh, rl, *outs):
     parts = [split(r[...]) for r in (x_ref, g_ref, c_ref, cg_ref)]
-    sends_of(*parts, (wh, wl), (lh, ll, rh, rl), outs[0], outs[1:])
+    sends_of(*parts, (wh, wl), (lh, ll, rh, rl), outs)
 
 
 def spread(dp_count, count, keep_refs, give_ref, put):
@@ -218,15 +269,26 @@
     spread(dp_count, rows, keep_refs, give_ref, put)
 
 
-def grads_kernel(sizes, scale, *refs):
+def cat(refs):
+    values = [r[...] for r in refs]
+    return values[0] if len(values) == 1 else jnp.concatenate(values, axis=0)
+
+
+def take_pieces(refs, counts):
+    groups, at = [], 0
+    for count in counts:
+        groups.append(cat(refs[at : at + count]))
+        at += count
+    return [split(group) for group in groups], refs[at:]
+
+
+def grads_kernel(sizes, scale, counts, *refs):
     sections, rows, rank_rows, rank, dp_count = sizes
-    x_ref, g_ref, near_ref, c_ref, cg_ref, *rest = refs
-    far_refs = rest[: sections - 1]
+    (x, g, near, c, cg, *far), rest = take_pieces(refs, counts)
     half = dp_count // 2
-    keep_refs = rest[sections - 1 : sections - 1 + half]
-    give_ref = rest[sections - 1 + half]
-    dw, dr, dl = rest[sections + half :]
-    block = x_ref.shape[1]
+    keep_refs = rest[:half]
+    give_ref, dw, dr, dl = rest[half:]
+    block = dw.shape[1]
     flat = rows * rank // block
     pieces = rows // flat
     at = [0]
@@ -249,9 +311,6 @@
         spread(dp_count, rows, keep_refs, give_ref, put)
         at[0] += flat
 
-    x, g, near = split(x_ref[...]), split(g_ref[...]), split(near_ref[...])
-    c, cg = split(c_ref[...]), split(cg_ref[...])
-    far = [split(r[...]) for r in far_refs]
     dw[...] = tn(x, near) * scale
     spread_wide(dw, rows)
     dr[...] = tn(c, near) * scale
@@ -267,21 +326,27 @@
     spread_left(dl)
 
 
-def local_kernel(sections, *refs):
-    x_ref, g_ref, near_ref, c_ref, cg_ref, *rest = refs
-    far_refs = rest[: sections - 1]
-    sh, sl, wh, wl, lh, ll, rh, rl, out_ref, grad_ref = rest[sections - 1 :]
-    out = nn(split(x_ref[...]), (sh[0], sl[0])) + nn(split(c_ref[...]), (rh[0], rl[0]))
-    for b in range(1, sections):
-        out += nn(split(far_refs[b - 1][...]), (wh[b - 1], wl[b - 1]))
+def local_kernel(counts, *refs):
+    (x, g, near, c, cg, *far), rest = take_pieces(refs, counts)
+    sh, sl, wh, wl, lh, ll, rh, rl, *first, out_ref, grad_ref = rest
+    last = wh.shape[0] - 1
+    out = nn(x, (sh[0], sl[0])) + nn(c, (rh[0], rl[0]))
+    for b in range(last):
+        out += nn(far[b], (wh[b], wl[b]))
     out_ref[...] = out
-    grad = nt(split(g_ref[...]), (sh[0], sl[0])) + nt(split(cg_ref[...]), (lh[0], ll[0]))
-    grad_ref[...] = grad + nt(split(near_ref[...]), (wh[sections - 1], wl[sections - 1]))
-
-
-def join_kernel(out0_ref, grad0_ref, ahead_ref, back_ref, out_ref, grad_ref):
-    out_ref[...] = out0_ref[...] + ahead_ref[...]
-    grad_ref[...] = grad0_ref[...] + back_ref[...]
+    grad = nt(g, (sh[0], sl[0])) + nt(cg, (lh[0], ll[0]))
+    grad_ref[...] = grad + nt(near, (wh[last], wl[last]))
+    if first:
+        ahead_ref, back_ref = first
+        count = ahead_ref.shape[0]
+        out_ref[:count] += ahead_ref[...]
+        grad_ref[:count] += back_ref[...]
+
+
+def join_kernel(whole_ref, late_ref, out_ref):
+    early = whole_ref.shape[0] - late_ref.shape[0]
+    out_ref[:early] = whole_ref[:early]
+    out_ref[early:] = whole_ref[early:] + late_ref[...]
 
 
 def place_kernel(sizes, *refs):
@@ -306,22 +371,6 @@
         )
 
 
-def join(outputs, grad, parts, start):
-    tokens, block = outputs.shape
-    step = math.gcd(start, parts[0].shape[0])
-    there = pl.BlockSpec((step, block), lambda i: (i + start // step, 0))
-    here = by_tokens(step, block)
-    return call(
-        join_kernel,
-        [f32(tokens, block)] * 2,
-        [outputs, grad, *parts],
-        grid=(parts[0].shape[0] // step,),
-        in_specs=[there, there, here, here],
-        out_specs=[there, there],
-        aliases={0: 0, 1: 1},
-    )
-
-
 def on_device(inputs, partner_bits, block_weights, low_left, low_right, cotangent):
     tokens, block = inputs.shape
     sections = partner_bits.shape[1]
@@ -332,7 +381,7 @@
     all_rank = rank_rows * dp_count
     flat = rows * rank // block
     sizes = (sections, rows, rank_rows, rank, dp_count)
-    early = tokens * 3 // 128 * 16
+    early = tokens * EARLY // 512 // 16 * 16
     late = tokens - early
     lent_rows = rows + rank_rows
     own_rows = sections * rows + rank_rows + flat
@@ -340,6 +389,8 @@
     smem = pl.BlockSpec(memory_space=pltpu.SMEM)
     vmem = pl.BlockSpec(memory_space=pltpu.VMEM)
     usual = partner_bits[0, 0] >= 0
+    folds = sections == 2
+    scale = 1.0 / math.sqrt(tokens * dp_count)
 
     by_slot = jnp.transpose(block_weights, (0, 2, 1, 3))
     pack_shapes = [(lent_rows + early, block), (flat + early, block), (own_rows, block)]
@@ -358,12 +409,20 @@
     got_near = across(out_near, "feat", 1)
     got_far = across(out_far, "feat", 2)
     own = [own] + [across(own, "dp", k) for k in range(2, dp_count, 2)]
-    late_x, late_g, got_near, got_far, own = lax.optimization_barrier(
-        (inputs[early:], cotangent[early:], got_near, got_far, own)
-    )
+    late_x, got_far = lax.optimization_barrier((inputs[early:], got_far))
     late_far = across(late_x, "feat", 2)
+    late_g, got_near = lax.optimization_barrier((cotangent[early:], got_near))
     late_near = across(late_g, "feat", 1)
     early_far, early_near = got_far[flat:], got_near[lent_rows:]
+    lent = jnp.concatenate([got_near[:lent_rows], got_far[:flat]])
+    lent, own = lax.optimization_barrier((lent, own))
+    lent = gather_rows(lent, dp_count)
+    *self_keep, self_give = call(
+        functools.partial(self_kernel, sizes, scale),
+        [f32(rows, block)] * half + [f32(half, rows, block)],
+        [inputs, cotangent],
+        scratch=[pltpu.VMEM((block, block), F32)],
+    )
 
     s_shape = (1, block, block)
     w_shape = (sections, block, block)
@@ -371,27 +430,17 @@
     r_shape = (2, all_rank, block)
     shapes = [s_shape, s_shape, w_shape, w_shape, l_shape, l_shape, r_shape, r_shape]
 
-    def message_shapes(count):
-        return [(count, rank)] * 2 + [(count, block)] * sections
-
-    folds = sections == 2
-    scale = 1.0 / math.sqrt(tokens * dp_count)
+    def message_shapes(*cuts):
+        sends = [(cut, block) for cut in cuts] * sections
+        return [(sum(cuts), rank)] * 2 + sends
+
     made = [b16(*s) for s in shapes]
     if folds:
         made += [f32(*s) for s in message_shapes(early)]
 
-    lent = jnp.concatenate([got_near[:lent_rows], got_far[:flat]])
-    lent = [lent] + [across(lent, "dp", k) for k in range(2, dp_count, 2)]
-
-    def prepare(own, lent, *early_parts):
+    def prepare(own, lent, keep, give, *early_parts):
         even = jnp.stack([jnp.concatenate(pair) for pair in zip(own, lent)])
         odd = across(even, "dp", 1)
-        *keep, give = call(
-            functools.partial(self_kernel, sizes, scale),
-            [f32(rows, block)] * half + [f32(half, rows, block)],
-            early_parts[:2],
-            scratch=[pltpu.VMEM((block, block), F32)],
-        )
         got = across(give, "dp", 1)
         got, odd = lax.optimization_barrier((got, odd))
         self_grads = keep[0] + got[0]
@@ -414,110 +463,98 @@
 
     self_grads, *weights = lax.cond(
         usual, prepare, empty,
-        own, lent, inputs, cotangent, early_far, early_near,
+        own, lent, self_keep, self_give, inputs, cotangent, early_far, early_near,
     )
     weights, sent = weights[:8], weights[8:]
-    low = weights[4:]
-    step = tokens // 2
-    wide, thin = by_tokens(step, block), by_tokens(step, rank)
     weight_specs = [whole(s) for s in shapes]
+    near = [early_near, late_near]
+    far = [[early_far, late_far]]
     if folds:
-        wide_late, thin_late = by_tokens(late, block), by_tokens(late, rank)
+        late_shapes = message_shapes(late)
         late_sent = call(
             messages_kernel,
-            [f32(*s) for s in message_shapes(late)],
+            [f32(*s) for s in late_shapes],
             [late_x, late_g, late_far, late_near, *weights[2:]],
             grid=(1,),
-            in_specs=[wide_late] * 4 + weight_specs[2:],
-            out_specs=[thin_late] * 2 + [wide_late] * sections,
-        )
-        first = [across(sent[2], "feat", 1), across(sent[3], "feat", 2)]
-        codes = jnp.concatenate([sent[0], late_sent[0]])
-        code_grads = jnp.concatenate([sent[1], late_sent[1]])
-    far = [jnp.concatenate([early_far, late_far])]
-    near = jnp.concatenate([early_near, late_near])
-    far += [across(inputs, "feat", 1 << b) for b in range(2, sections)]
-    grid = (tokens // step,)
-    if not folds:
+            in_specs=[whole((late, block))] * 4 + weight_specs[2:],
+            out_specs=[whole(s) for s in late_shapes],
+        )
+        first = [across(part, "feat", 1 << b) for b, part in enumerate(sent[2:])]
+        rest = list(late_sent[2:])
+        rest[0], first[1] = lax.optimization_barrier((rest[0], first[1]))
+        rest[1], first[0] = lax.optimization_barrier((rest[1], first[0]))
+        first, late_sent = lax.optimization_barrier((first, late_sent))
+        rest = [across(part, "feat", 1 << b) for b, part in enumerate(rest)]
+        codes, code_grads = ([sent[i], late_sent[i]] for i in range(2))
+    else:
+        far += [[across(inputs, "feat", 1 << b)] for b in range(2, sections)]
+        step = tokens // 2
+        wide, thin = by_tokens(step, block), by_tokens(step, rank)
         codes, code_grads = call(
             codes_kernel,
             [f32(tokens, rank)] * 2,
-            [inputs, cotangent, far[0], near, *low],
-            grid=grid,
+            [inputs, cotangent, jnp.concatenate(far[0]), jnp.concatenate(near), *weights[4:]],
+            grid=(2,),
             in_specs=[wide] * 4 + weight_specs[4:],
             out_specs=[thin, thin],
         )
         for b in range(2, sections):
             codes = codes + across(codes, "feat", 1 << b)
             code_grads = code_grads + across(code_grads, "feat", 1 << b)
-        ahead, *back = call(
+        messages = call(
             sends_kernel,
             [f32(tokens, block)] * sections,
             [inputs, cotangent, codes, code_grads, *weights[2:]],
-            grid=grid,
+            grid=(2,),
             in_specs=[wide, wide, thin, thin, *weight_specs[2:]],
             out_specs=[wide] * sections,
         )
-        back = [across(back[b - 1], "feat", 1 << b) for b in range(1, sections)]
-        ahead = across(ahead, "feat", 1)
-
-    def reduce_pair(inputs, cotangent, near, codes, code_grads, *far):
+        messages = [across(part, "feat", 1 << b) for b, part in enumerate(messages)]
+        codes, code_grads = [codes], [code_grads]
+
+    groups = [[inputs], [cotangent], near, codes, code_grads, *far]
+    counts = [len(group) for group in groups]
+
+    def finish(groups, weights, first):
         *keep, give = call(
-            functools.partial(grads_kernel, sizes, scale),
+            functools.partial(grads_kernel, sizes, scale, counts),
             [f32(sum_rows, block)] * half + [f32(half, sum_rows, block)],
-            [inputs, cotangent, near, codes, code_grads, *far],
+            [part for group in groups for part in group],
             scratch=[
                 pltpu.VMEM((block, block), F32),
                 pltpu.VMEM((all_rank, block), F32),
                 pltpu.VMEM((block, rank), F32),
             ],
         )
+        groups, give = lax.optimization_barrier((groups, give))
         got = across(give, "dp", 1)
-        return tuple(keep[m] + got[m] for m in range(half))
-
-    def no_pair(*_):
-        return (jnp.zeros((sum_rows, block), F32),) * half
-
-    summed = lax.cond(usual, reduce_pair, no_pair, inputs, cotangent, near, codes, code_grads, *far)
-    if folds:
-        first, rest, summed = lax.optimization_barrier((first, late_sent[2:], summed))
-        rest = [across(rest[0], "feat", 1), across(rest[1], "feat", 2)]
-
-    def finish(summed, inputs, cotangent, near, codes, code_grads, far, weights):
-        total = summed[0]
-        for m in range(1, half):
-            total = total + across(summed[m], "dp", 2 * m)
-        out, grad = call(
-            functools.partial(local_kernel, sections),
+        beside = call(
+            functools.partial(local_kernel, counts),
             [f32(tokens, block)] * 2,
-            [inputs, cotangent, near, codes, code_grads, *far, *weights],
-            grid=grid,
-            in_specs=[wide] * 3 + [thin] * 2 + [wide] * (sections - 1) + weight_specs,
-            out_specs=[wide, wide],
-        )
+            [part for group in groups for part in group] + weights + first,
+        )
+        total, (out, grad) = scatter_rows([keep[m] + got[m] for m in range(half)], beside)
         at = lent_rows + flat
         return out, grad, total[:lent_rows], total[lent_rows:at], total[at:]
 
     def nothing(*_):
-        wide_zero = jnp.zeros((tokens, block), F32)
-        return (
-            wide_zero, wide_zero, jnp.zeros((lent_rows, block), F32),
-            jnp.zeros((flat, block), F32), jnp.zeros((sum_rows - lent_rows - flat, block), F32),
-        )
+        shapes = [(tokens, block)] * 2 + [(n, block) for n in (lent_rows, flat, own_rows - rows)]
+        return tuple(jnp.zeros(shape, F32) for shape in shapes)
 
     outputs, grad, near_back, far_back, kept = lax.cond(
-        usual, finish, nothing,
-        summed, inputs, cotangent, near, codes, code_grads, far, weights,
-    )
-    if folds:
-        for start, parts in ((0, first), (early, rest)):
-            outputs, grad = join(outputs, grad, parts, start)
-    else:
-        outputs = outputs + ahead
-        for part in back:
-            grad = grad + part
+        usual, finish, nothing, groups, weights, first if folds else []
+    )
     near_back = across(near_back, "feat", 1)
     far_back = across(far_back, "feat", 2)
+    if folds:
+        outputs, grad = (
+            call(join_kernel, [f32(tokens, block)], parts, vmem_bytes=JOIN_VMEM_BYTES)[0]
+            for parts in zip((outputs, grad), rest)
+        )
+    else:
+        outputs = outputs + messages[0]
+        for part in messages[1:]:
+            grad = grad + part
     outputs, grad, kept = lax.optimization_barrier((outputs, grad, kept))
     block_grads, left_grads, right_grads = call(
         functools.partial(place_kernel, sizes),

time: 121 us -> 115 us (0.950)
  waiting for transfers between devices: 57.1 us -> 45.6 us
  starting transfers between devices: 31.2 us -> 38.1 us
  other arithmetic: 4.34 us -> 1.38 us
  local copies, waits for them, and re-layouts: 1.46 us -> 2.88 us
    ppermute x25 -> x27, waiting for transfers between devices: 57.1 us -> 45.6 us  [across(): return lax.ppermute(block, axis, [(i, i ^ apart) for i in range(count)])]
    ppermute x25 -> x27, starting transfers between devices: 31.2 us -> 38.1 us  [across(): return lax.ppermute(block, axis, [(i, i ^ apart) for i in range(count)])]
    concatenate x2 -> x0, other arithmetic: 2.08 us -> none  [the longest x1 1.04 us: on_device(): far = [jnp.concatenate([early_far, late_far])]]
    cond x0 -> x22, local copies, waits for them, and re-layouts: none -> 1.32 us
  transfers between devices with their start and end apart: 25 -> 27, of which waited for: 18 -> 17; matrix products, arithmetic and copies ran while one was open for 4% -> 3% of each run, Pallas kernels for 18% -> 20%
where the time goes in v3:
time: 115 us
  waiting for transfers between devices  45.6 us (40%)
  starting transfers between devices  38.1 us (33%)
  Pallas kernels  25.9 us (23%)
  local copies, waits for them, and re-layouts  2.88 us (3%)
  other arithmetic  1.38 us (1%)
    ppermute x27, waiting for transfers between devices, across(): return lax.ppermute(block, axis, [(i, i ^ apart) for i in range(count)])  45.6 us
    ppermute x27, starting transfers between devices, across(): return lax.ppermute(block, axis, [(i, i ^ apart) for i in range(count)])  38.1 us
    pallas_call x9, Pallas kernels, call(): pl.pallas_call(kernel, out_shape=out_shapes, in_specs=in_specs, out_specs...  25.9 us
  transfers between devices with their start and end apart: 27, of which 17 were waited for; matrix products, arithmetic and copies ran while one was open for 3% of the time, Pallas kernels for 20%

profile of v3, /device:TPU:0, one launch (start us, length us, event | category | flops | bytes accessed | tf_op | source)
XLA Modules:
  0.0 115.1 jit_solution(12449612231979041490)
XLA Ops:
  0.6 2.1 %shard_map.101 = (f32[176,512]{1,0:T(8,128)}, f32[112,512]{1,0:T(8,128)}, f32[192,512]{1,0:T(8,128)S(1)}) custom-call(s32[1,2]{1,0:T(1,128)} %refs_0_.3, f32[1,3,64,512]{3,2,1,0:T(8,128)} %bitcast.83, f32[1,64,256]{2,1,0:T(8,128)} %left_ref.1, f32[1,32,512]{2,1,0:T(8,128)} %right_ref.1, f32[512,512]{1,0:T(8,128)} %refs_0_.2, f32[512,512]{1,0:T(8,128)} %refs_1_.1), custom_call_target="tpu_custom_call" | custom-call | flops 1 | bytes 1 | tf_op jit(solution)/shard_map/pallas_call | solution.py:103
  2.8 3.0 %collective-permute-start.10 = (f32[176,512]{1,0:T(8,128)}, f32[176,512]{1,0:T(8,128)S(1)}, u32[]{:S(2)}, u32[]{:S(2)}) collective-permute-start(f32[176,512]{1,0:T(8,128)} %get-tuple-element.235), channel_id=1, source_target_pairs={{0,1},{1,0},{2,3},{3,2},{4,5},{5,4},{6,7},{7,6},{8,9},{9,8},{10,11... | collective-permute-start | bytes 1081352 | tf_op jit(solution)/shard_map/ppermute | solution.py:21
  5.8 1.5 %collective-permute-start.13 = (f32[192,512]{1,0:T(8,128)S(1)}, f32[192,512]{1,0:T(8,128)S(1)}, u32[]{:S(2)}, u32[]{:S(2)}) collective-permute-start(f32[192,512]{1,0:T(8,128)S(1)} %get-tuple-element.242), channel_id=1, source_target_pairs={{0,8},{4,12},{8,0},{12,4},{16,24},{20,28},{24,16},{28,20},{1,9},{5... | collective-permute-start | bytes 1179656 | tf_op jit(solution)/shard_map/ppermute | solution.py:21
  7.3 1.5 %collective-permute-start.14 = (f32[192,512]{1,0:T(8,128)S(1)}, f32[192,512]{1,0:T(8,128)S(1)}, u32[]{:S(2)}, u32[]{:S(2)}) collective-permute-start(f32[192,512]{1,0:T(8,128)S(1)} %get-tuple-element.242), channel_id=1, source_target_pairs={{0,16},{4,20},{8,24},{12,28},{16,0},{20,4},{24,8},{28,12},{1,17},{... | collective-permute-start | bytes 1179656 | tf_op jit(solution)/shard_map/ppermute | solution.py:21
  8.8 0.5 collective-permute-start.15
  9.3 2.6 %collective-permute-start.12 = (f32[112,512]{1,0:T(8,128)}, f32[112,512]{1,0:T(8,128)S(1)}, u32[]{:S(2)}, u32[]{:S(2)}) collective-permute-start(f32[112,512]{1,0:T(8,128)} %get-tuple-element.239), channel_id=1, source_target_pairs={{0,2},{1,3},{2,0},{3,1},{4,6},{5,7},{6,4},{7,5},{8,10},{9,11},{10,... | collective-permute-start | bytes 688136 | tf_op jit(solution)/shard_map/ppermute | solution.py:21
  11.9 1.2 %slice.110.g_ref = f32[432,512]{1,0:T(8,128)S(1)} slice(f32[512,512]{1,0:T(8,128)} %refs_1_.1), slice={[80:512], [0:512]} | slice | bytes 1769472 | tf_op jit(solution)/shard_map/slice | solution.py:414
  13.2 5.5 %collective-permute-done.12 = f32[112,512]{1,0:T(8,128)S(1)} collective-permute-done((f32[112,512]{1,0:T(8,128)}, f32[112,512]{1,0:T(8,128)S(1)}, u32[]{:S(2)}, u32[]{:S(2)}) %collective-permute-start.12) | collective-permute-done | bytes 229408 | tf_op jit(solution)/shard_map/ppermute | solution.py:21
  18.7 3.3 %collective-permute-start.20 = (f32[432,512]{1,0:T(8,128)S(1)}, f32[432,512]{1,0:T(8,128)}, u32[]{:S(2)}, u32[]{:S(2)}) collective-permute-start(f32[432,512]{1,0:T(8,128)S(1)} %slice.113.x_ref), channel_id=1, source_target_pairs={{0,2},{1,3},{2,0},{3,1},{4,6},{5,7},{6,4},{7,5},{8,10},{9,11},{10,... | collective-permute-start | bytes 2654216 | tf_op jit(solution)/shard_map/ppermute | solution.py:21
  22.1 2.5 %collective-permute-start.11 = (f32[432,512]{1,0:T(8,128)S(1)}, f32[432,512]{1,0:T(8,128)}, u32[]{:S(2)}, u32[]{:S(2)}) collective-permute-start(f32[432,512]{1,0:T(8,128)S(1)} %slice.110.g_ref), channel_id=1, source_target_pairs={{0,1},{1,0},{2,3},{3,2},{4,5},{5,4},{6,7},{7,6},{8,9},{9,8},{10,11... | collective-permute-start | bytes 2654216 | tf_op jit(solution)/shard_map/ppermute | solution.py:21
  24.7 1.3 %collective-permute-done.14 = f32[192,512]{1,0:T(8,128)S(1)} collective-permute-done((f32[192,512]{1,0:T(8,128)S(1)}, f32[192,512]{1,0:T(8,128)S(1)}, u32[]{:S(2)}, u32[]{:S(2)}) %collective-permute-start.14) | collective-permute-done | bytes 393248 | tf_op jit(solution)/shard_map/ppermute | solution.py:21
  26.1 1.3 %collective-permute-start.16 = (f32[1,64,512]{2,1,0:T(8,128)S(1)}, f32[1,64,512]{2,1,0:T(8,128)S(1)}, u32[]{:S(2)}, u32[]{:S(2)}) collective-permute-start(f32[1,64,512]{2,1,0:T(8,128)S(1)} %get-tuple-element.314), channel_id=1, source_target_pairs={{0,8},{4,12},{8,0},{12,4},{16,24},{20,28},{24,16},{28,20},{1,9},{5... | collective-permute-start | bytes 393224 | tf_op jit(solution)/shard_map/ppermute | solution.py:21
  27.4 0.8 collective-permute-start.17
  28.2 2.9 %collective-permute-done.16 = f32[1,64,512]{2,1,0:T(8,128)S(1)} collective-permute-done((f32[1,64,512]{2,1,0:T(8,128)S(1)}, f32[1,64,512]{2,1,0:T(8,128)S(1)}, u32[]{:S(2)}, u32[]{:S(2)}) %collective-permute-start.16) | collective-permute-done | bytes 131104 | tf_op jit(solution)/shard_map/ppermute | solution.py:21
  31.1 1.2 %collective-permute-done.17 = f32[1,64,512]{2,1,0:T(8,128)S(1)} collective-permute-done((f32[1,64,512]{2,1,0:T(8,128)S(1)}, f32[1,64,512]{2,1,0:T(8,128)S(1)}, u32[]{:S(2)}, u32[]{:S(2)}) %collective-permute-start.17) | collective-permute-done | bytes 131104 | tf_op jit(solution)/shard_map/ppermute | solution.py:21
  32.3 0.9 collective-permute-start.18
  33.3 2.6 %collective-permute-start.19 = (f32[2,64,512]{2,1,0:T(8,128)S(1)}, f32[2,64,512]{2,1,0:T(8,128)S(1)}, u32[]{:S(2)}, u32[]{:S(2)}) collective-permute-start(f32[2,64,512]{2,1,0:T(8,128)S(1)} %pad_maximum_fusion.5), channel_id=1, source_target_pairs={{0,8},{4,12},{8,0},{12,4},{16,24},{20,28},{24,16},{28,20},{1,9},{5... | collective-permute-start | bytes 786440 | tf_op jit(solution)/shard_map/ppermute | solution.py:21
  35.8 1.1 shard_map.102
  37.0 1.7 %collective-permute-done.18 = f32[2,64,512]{2,1,0:T(8,128)S(1)} collective-permute-done((f32[2,64,512]{2,1,0:T(8,128)S(1)}, f32[2,64,512]{2,1,0:T(8,128)S(1)}, u32[]{:S(2)}, u32[]{:S(2)}) %collective-permute-start.18) | collective-permute-done | bytes 262176 | tf_op jit(solution)/shard_map/ppermute | solution.py:21
  38.8 1.4 %collective-permute-done.19 = f32[2,64,512]{2,1,0:T(8,128)S(1)} collective-permute-done((f32[2,64,512]{2,1,0:T(8,128)S(1)}, f32[2,64,512]{2,1,0:T(8,128)S(1)}, u32[]{:S(2)}, u32[]{:S(2)}) %collective-permute-start.19) | collective-permute-done | bytes 262176 | tf_op jit(solution)/shard_map/ppermute | solution.py:21
  40.2 15.7 %conditional.2 = (f32[64,512]{1,0:T(8,128)S(1)}, bf16[1,512,512]{2,1,0:T(8,128)(2,1)S(1)}, bf16[1,512,512]{2,1,0:T(8,128)(2,1)}, bf16[2,512,512]{2,1,0:T(8,128)(...) conditional(s32[]{:T(128)} %bitcast.30, () %tuple.41, ...), branch_computations={%region_0.0_spmd, %region_1.0_spmd} | conditional | flops 3506177 | bytes 27656496 | solution.py:464
  40.8 0.5 collective-permute-start
  41.3 5.1 %collective-permute-done = f32[4,64,512]{2,1,0:T(8,128)S(1)} collective-permute-done((f32[4,64,512]{2,1,0:T(8,128)S(1)}, f32[4,64,512]{2,1,0:T(8,128)S(1)}, u32[]{:S(2)}, u32[]{:S(2)}) %collective-permute-start) | collective-permute-done | bytes 524320 | tf_op jit(solution)/shard_map/cond/branch_1_fun/ppermute | solution.py:21
  46.5 1.5 %collective-permute-start.4 = (f32[64,512]{1,0:T(8,128)S(1)}, f32[64,512]{1,0:T(8,128)S(1)}, u32[]{:S(2)}, u32[]{:S(2)}) collective-permute-start(f32[64,512]{1,0:T(8,128)S(1)} %get-tuple-element.293), channel_id=1, source_target_pairs={{0,24},{4,28},{8,16},{12,20},{16,8},{20,12},{24,0},{28,4},{1,25},{... | collective-permute-start | bytes 393224 | tf_op jit(solution)/shard_map/cond/branch_1_fun/ppermute | solution.py:21
  48.0 2.0 %collective-permute-start.3 = (f32[64,512]{1,0:T(8,128)S(1)}, f32[64,512]{1,0:T(8,128)S(1)}, u32[]{:S(2)}, u32[]{:S(2)}) collective-permute-start(f32[64,512]{1,0:T(8,128)S(1)} %get-tuple-element.294), channel_id=1, source_target_pairs={{0,16},{4,20},{8,24},{12,28},{16,0},{20,4},{24,8},{28,12},{1,17},{... | collective-permute-start | bytes 393224 | tf_op jit(solution)/shard_map/cond/branch_1_fun/ppermute | solution.py:21
  50.0 3.0 %branch_1_fun.3 = (bf16[1,512,512]{2,1,0:T(8,128)(2,1)S(1)}, bf16[1,512,512]{2,1,0:T(8,128)(2,1)}, bf16[2,512,512]{2,1,0:T(8,128)(2,1)S(1)}, bf16[2,512,512]{2,1...) custom-call(f32[4,320,512]{2,1,0:T(8,128)S(1)} %pad_maximum_fusion.r, ...), custom_call_target="tpu_custom_call" | custom-call | flops 1 | bytes 1 | tf_op jit(solution)/shard_map/cond/branch_1_fun/pallas_call | solution.py:103
  53.1 0.7 collective-permute-done.4
  53.8 2.0 %collective-permute-done.3 = f32[64,512]{1,0:T(8,128)S(1)} collective-permute-done((f32[64,512]{1,0:T(8,128)S(1)}, f32[64,512]{1,0:T(8,128)S(1)}, u32[]{:S(2)}, u32[]{:S(2)}) %collective-permute-start.3) | collective-permute-done | bytes 131104 | tf_op jit(solution)/shard_map/cond/branch_1_fun/ppermute | solution.py:21
  55.8 2.7 %collective-permute-start.22 = (f32[80,512]{1,0:T(8,128)S(1)}, f32[80,512]{1,0:T(8,128)S(1)}, u32[]{:S(2)}, u32[]{:S(2)}) collective-permute-start(f32[80,512]{1,0:T(8,128)S(1)} %get-tuple-element.267), channel_id=1, source_target_pairs={{0,2},{1,3},{2,0},{3,1},{4,6},{5,7},{6,4},{7,5},{8,10},{9,11},{10,... | collective-permute-start | bytes 491528 | tf_op jit(solution)/shard_map/ppermute | solution.py:21
  59.0 1.0 collective-permute-done.20.far_ref
  60.0 5.2 %shard_map.103 = (f32[432,256]{1,0:T(8,128)S(1)}, f32[432,256]{1,0:T(8,128)S(1)}, f32[432,512]{1,0:T(8,128)S(1)}, f32[432,512]{1,0:T(8,128)S(1)}) custom-call(f32[432,512]{1,0:T(8,128)S(1)} %slice.113.x_ref, f32[432,512]{1,0:T(8,128)S(1)} %slice.110.g_ref, f32[432,512]{1,0:T(8,128)} %collective-permute-done.20.far_ref, ...), custom_call_target="tpu_custom_call" | custom-call | flops 1 | bytes 1 | tf_op jit(solution)/shard_map/pallas_call | solution.py:103
  65.3 0.7 collective-permute-done.22
  66.0 1.8 %collective-permute-start.23 = (f32[432,512]{1,0:T(8,128)S(1)}, f32[432,512]{1,0:T(8,128)S(1)}, u32[]{:S(2)}, u32[]{:S(2)}) collective-permute-start(f32[432,512]{1,0:T(8,128)S(1)} %get-tuple-element.279), channel_id=1, source_target_pairs={{0,1},{1,0},{2,3},{3,2},{4,5},{5,4},{6,7},{7,6},{8,9},{9,8},{10,11... | collective-permute-start | bytes 2654216 | tf_op jit(solution)/shard_map/ppermute | solution.py:21
  67.8 2.3 %collective-permute-start.24 = (f32[432,512]{1,0:T(8,128)S(1)}, f32[432,512]{1,0:T(8,128)S(1)}, u32[]{:S(2)}, u32[]{:S(2)}) collective-permute-start(f32[432,512]{1,0:T(8,128)S(1)} %get-tuple-element.281), channel_id=1, source_target_pairs={{0,2},{1,3},{2,0},{3,1},{4,6},{5,7},{6,4},{7,5},{8,10},{9,11},{10,... | collective-permute-start | bytes 2654216 | tf_op jit(solution)/shard_map/ppermute | solution.py:21
  70.1 36.3 %conditional.3 = (f32[512,512]{1,0:T(8,128)S(1)}, f32[512,512]{1,0:T(8,128)S(1)}, f32[96,512]{1,0:T(8,128)S(1)}, f32[32,512]{1,0:T(8,128)S(1)}, f32[128,512]{1,0:T(8,128)S(1)}) conditional(s32[]{:T(128)} %bitcast.30, () %tuple.39, (f32[512,512]{1,0:T(8,128)S(1)}, f32[512,512]{1,0:T(8,128)S(1)}, f32[80,512]{1,0:T(8,128)S(1)}, f32[432,512]{1,0:T(8,128)}, ...), branch_computations={%region_2.0_spmd, %region_3.0_spmd} | conditional | flops 1179650 | bytes 53740068 | solution.py:544
  70.4 0.9 copy-done.5
  71.6 5.2 %branch_1_fun.4 = (f32[256,512]{1,0:T(8,128)S(1)}, f32[256,512]{1,0:T(8,128)S(1)}, f32[256,512]{1,0:T(8,128)S(1)}, f32[256,512]{1,0:T(8,128)S(1)}, f32[4,256,512]{2,1,0:T(8,128)S(1)}) custom-call(f32[512,512]{1,0:T(8,128)S(1)} %get-tuple-element.140.refs_0_, f32[512,512]{1,0:T(8,128)S(1)} %get-tuple-element.141.refs_1_, ...), custom_call_target="tpu_custom_call" | custom-call | flops 1 | bytes 1 | tf_op jit(solution)/shard_map/cond/branch_1_fun/pallas_call | solution.py:103
  77.0 4.1 %collective-permute-done.5 = f32[4,256,512]{2,1,0:T(8,128)S(1)} collective-permute-done((f32[4,256,512]{2,1,0:T(8,128)S(1)}, f32[4,256,512]{2,1,0:T(8,128)S(1)}, u32[]{:S(2)}, u32[]{:S(2)}) %collective-permute-start.5) | collective-permute-done | bytes 2097184 | tf_op jit(solution)/shard_map/cond/branch_1_fun/ppermute | solution.py:21
  81.9 3.3 %collective-permute-start.6 = (f32[2,128,512]{2,1,0:T(8,128)S(1)}, f32[2,128,512]{2,1,0:T(8,128)S(1)}, u32[]{:S(2)}, u32[]{:S(2)}) collective-permute-start(f32[2,128,512]{2,1,0:T(8,128)S(1)} %pad_maximum_fusion.1), channel_id=1, source_target_pairs={{0,8},{4,12},{8,0},{12,4},{16,24},{20,28},{24,16},{28,20},{1,9},{5... | collective-permute-start | bytes 1572872 | tf_op jit(solution)/shard_map/cond/branch_1_fun/ppermute | solution.py:21
  85.5 5.7 %branch_1_fun.5 = (f32[512,512]{1,0:T(8,128)S(1)}, f32[512,512]{1,0:T(8,128)S(1)}) custom-call(f32[512,512]{1,0:T(8,128)S(1)} %get-tuple-element.140.refs_0_, f32[512,512]{1,0:T(8,128)S(1)} %get-tuple-element.141.refs_1_, f32[80,512]{1,0:T(8,128)S(1)} %get-tuple-element.142.refs_2_, f32[432,512]{1,0:T(8,128)} %get-tuple-element.143.refs_3_, ...), custom_call_target="tpu_custom_call" | custom-call | flops 1 | bytes 1 | tf_op jit(solution)/shard_map/cond/branch_1_fun/pallas_call | solution.py:103
  91.2 6.2 %collective-permute-done.6 = f32[2,128,512]{2,1,0:T(8,128)S(1)} collective-permute-done((f32[2,128,512]{2,1,0:T(8,128)S(1)}, f32[2,128,512]{2,1,0:T(8,128)S(1)}, u32[]{:S(2)}, u32[]{:S(2)}) %collective-permute-start.6) | collective-permute-done | bytes 524320 | tf_op jit(solution)/shard_map/cond/branch_1_fun/ppermute | solution.py:21
  97.4 1.5 %collective-permute-done.7 = f32[2,128,512]{2,1,0:T(8,128)S(1)} collective-permute-done((f32[2,128,512]{2,1,0:T(8,128)S(1)}, f32[2,128,512]{2,1,0:T(8,128)S(1)}, u32[]{:S(2)}, u32[]{:S(2)}) %collective-permute-start.7) | collective-permute-done | bytes 524320 | tf_op jit(solution)/shard_map/cond/branch_1_fun/ppermute | solution.py:21
  99.7 6.6 %collective-permute-done.8 = f32[1,128,512]{2,1,0:T(8,128)S(1)} collective-permute-done((f32[1,128,512]{2,1,0:T(8,128)S(1)}, f32[1,128,512]{2,1,0:T(8,128)S(1)}, u32[]{:S(2)}, u32[]{:S(2)}) %collective-permute-start.8) | collective-permute-done | bytes 262176 | tf_op jit(solution)/shard_map/cond/branch_1_fun/ppermute | solution.py:21
  106.5 1.4 %collective-permute-start.25 = (f32[96,512]{1,0:T(8,128)S(1)}, f32[96,512]{1,0:T(8,128)S(1)}, u32[]{:S(2)}, u32[]{:S(2)}) collective-permute-start(f32[96,512]{1,0:T(8,128)S(1)} %get-tuple-element.287), channel_id=1, source_target_pairs={{0,1},{1,0},{2,3},{3,2},{4,5},{5,4},{6,7},{7,6},{8,9},{9,8},{10,11... | collective-permute-start | bytes 589832 | tf_op jit(solution)/shard_map/ppermute | solution.py:21
  108.3 1.1 shard_map.104
  109.4 1.1 shard_map.105
  110.5 3.3 %collective-permute-done.26.refs_4_ = f32[32,512]{1,0:T(8,128)S(1)} collective-permute-done((f32[32,512]{1,0:T(8,128)S(1)}, f32[32,512]{1,0:T(8,128)S(1)}, u32[]{:S(2)}, u32[]{:S(2)}) %collective-permute-start.26) | collective-permute-done | bytes 65568 | tf_op jit(solution)/shard_map/ppermute | solution.py:21
  113.8 1.4 %shard_map.106 = (f32[1,3,64,512]{3,2,1,0:T(8,128)}, f32[1,64,256]{2,1,0:T(8,128)}, f32[1,32,512]{2,1,0:T(8,128)}) custom-call(s32[1,2]{1,0:T(1,128)S(1)} %copy-done, f32[64,512]{1,0:T(8,128)S(1)} %copy-done.21, f32[128,512]{1,0:T(8,128)S(1)} %get-tuple-element.286.refs_2_, f32[96,512]{1,0:T(8,128)S(1)} %collective-permute-done.25.refs_3_, ...), custom_call_target="tpu_custom_call" | custom-call | flops 1 | bytes 1 | tf_op jit(solution)/shard_map/pallas_call | solution.py:103
  (88 shorter events, 4.2 us)
Async XLA Ops:
  0.6 12.5 %copy-start.1 = (f32[512,512]{1,0:T(8,128)S(1)}, f32[512,512]{1,0:T(8,128)}, u32[]{:S(2)}) copy-start(f32[512,512]{1,0:T(8,128)} %refs_0_.2) | copy-start | bytes 3145732
  2.8 19.3 %collective-permute-start.10 = (f32[176,512]{1,0:T(8,128)}, f32[176,512]{1,0:T(8,128)S(1)}, u32[]{:S(2)}, u32[]{:S(2)}) collective-permute-start(f32[176,512]{1,0:T(8,128)} %get-tuple-element.235), channel_id=1, source_target_pairs={{0,1},{1,0},{2,3},{3,2},{4,5},{5,4},{6,7},{7,6},{8,9},{9,8},{10,11... | collective-permute-start | bytes 1081352 | tf_op jit(solution)/shard_map/ppermute | solution.py:21
  5.8 18.9 %collective-permute-start.13 = (f32[192,512]{1,0:T(8,128)S(1)}, f32[192,512]{1,0:T(8,128)S(1)}, u32[]{:S(2)}, u32[]{:S(2)}) collective-permute-start(f32[192,512]{1,0:T(8,128)S(1)} %get-tuple-element.242), channel_id=1, source_target_pairs={{0,8},{4,12},{8,0},{12,4},{16,24},{20,28},{24,16},{28,20},{1,9},{5... | collective-permute-start | bytes 1179656 | tf_op jit(solution)/shard_map/ppermute | solution.py:21
  7.3 18.7 %collective-permute-start.14 = (f32[192,512]{1,0:T(8,128)S(1)}, f32[192,512]{1,0:T(8,128)S(1)}, u32[]{:S(2)}, u32[]{:S(2)}) collective-permute-start(f32[192,512]{1,0:T(8,128)S(1)} %get-tuple-element.242), channel_id=1, source_target_pairs={{0,16},{4,20},{8,24},{12,28},{16,0},{20,4},{24,8},{28,12},{1,17},{... | collective-permute-start | bytes 1179656 | tf_op jit(solution)/shard_map/ppermute | solution.py:21
  8.8 17.2 %collective-permute-start.15 = (f32[192,512]{1,0:T(8,128)S(1)}, f32[192,512]{1,0:T(8,128)S(1)}, u32[]{:S(2)}, u32[]{:S(2)}) collective-permute-start(f32[192,512]{1,0:T(8,128)S(1)} %get-tuple-element.242), channel_id=1, source_target_pairs={{0,24},{4,28},{8,16},{12,20},{16,8},{20,12},{24,0},{28,4},{1,25},{... | collective-permute-start | bytes 1179656 | tf_op jit(solution)/shard_map/ppermute | solution.py:21
  9.3 9.5 %collective-permute-start.12 = (f32[112,512]{1,0:T(8,128)}, f32[112,512]{1,0:T(8,128)S(1)}, u32[]{:S(2)}, u32[]{:S(2)}) collective-permute-start(f32[112,512]{1,0:T(8,128)} %get-tuple-element.239), channel_id=1, source_target_pairs={{0,2},{1,3},{2,0},{3,1},{4,6},{5,7},{6,4},{7,5},{8,10},{9,11},{10,... | collective-permute-start | bytes 688136 | tf_op jit(solution)/shard_map/ppermute | solution.py:21
  13.1 22.7 %copy-start.3 = (f32[512,512]{1,0:T(8,128)S(1)}, f32[512,512]{1,0:T(8,128)}, u32[]{:S(2)}) copy-start(f32[512,512]{1,0:T(8,128)} %refs_1_.1) | copy-start | bytes 3145732
  13.2 23.8 %copy-start = (s32[1,2]{1,0:T(1,128)S(1)}, s32[1,2]{1,0:T(1,128)}, u32[]{:S(2)}) copy-start(s32[1,2]{1,0:T(1,128)} %refs_0_.3) | copy-start | bytes 28
  18.7 41.3 %collective-permute-start.20 = (f32[432,512]{1,0:T(8,128)S(1)}, f32[432,512]{1,0:T(8,128)}, u32[]{:S(2)}, u32[]{:S(2)}) collective-permute-start(f32[432,512]{1,0:T(8,128)S(1)} %slice.113.x_ref), channel_id=1, source_target_pairs={{0,2},{1,3},{2,0},{3,1},{4,6},{5,7},{6,4},{7,5},{8,10},{9,11},{10,... | collective-permute-start | bytes 2654216 | tf_op jit(solution)/shard_map/ppermute | solution.py:21
  22.1 37.9 %collective-permute-start.11 = (f32[432,512]{1,0:T(8,128)S(1)}, f32[432,512]{1,0:T(8,128)}, u32[]{:S(2)}, u32[]{:S(2)}) collective-permute-start(f32[432,512]{1,0:T(8,128)S(1)} %slice.110.g_ref), channel_id=1, source_target_pairs={{0,1},{1,0},{2,3},{3,2},{4,5},{5,4},{6,7},{7,6},{8,9},{9,8},{10,11... | collective-permute-start | bytes 2654216 | tf_op jit(solution)/shard_map/ppermute | solution.py:21
  26.1 5.0 %collective-permute-start.16 = (f32[1,64,512]{2,1,0:T(8,128)S(1)}, f32[1,64,512]{2,1,0:T(8,128)S(1)}, u32[]{:S(2)}, u32[]{:S(2)}) collective-permute-start(f32[1,64,512]{2,1,0:T(8,128)S(1)} %get-tuple-element.314), channel_id=1, source_target_pairs={{0,8},{4,12},{8,0},{12,4},{16,24},{20,28},{24,16},{28,20},{1,9},{5... | collective-permute-start | bytes 393224 | tf_op jit(solution)/shard_map/ppermute | solution.py:21
  27.4 5.0 %collective-permute-start.17 = (f32[1,64,512]{2,1,0:T(8,128)S(1)}, f32[1,64,512]{2,1,0:T(8,128)S(1)}, u32[]{:S(2)}, u32[]{:S(2)}) collective-permute-start(f32[1,64,512]{2,1,0:T(8,128)S(1)} %get-tuple-element.313), channel_id=1, source_target_pairs={{0,16},{4,20},{8,24},{12,28},{16,0},{20,4},{24,8},{28,12},{1,17},{... | collective-permute-start | bytes 393224 | tf_op jit(solution)/shard_map/ppermute | solution.py:21
  32.3 6.4 %collective-permute-start.18 = (f32[2,64,512]{2,1,0:T(8,128)S(1)}, f32[2,64,512]{2,1,0:T(8,128)S(1)}, u32[]{:S(2)}, u32[]{:S(2)}) collective-permute-start(f32[2,64,512]{2,1,0:T(8,128)S(1)} %pad_maximum_fusion.4), channel_id=1, source_target_pairs={{0,16},{4,20},{8,24},{12,28},{16,0},{20,4},{24,8},{28,12},{1,17},{... | collective-permute-start | bytes 786440 | tf_op jit(solution)/shard_map/ppermute | solution.py:21
  33.3 6.9 %collective-permute-start.19 = (f32[2,64,512]{2,1,0:T(8,128)S(1)}, f32[2,64,512]{2,1,0:T(8,128)S(1)}, u32[]{:S(2)}, u32[]{:S(2)}) collective-permute-start(f32[2,64,512]{2,1,0:T(8,128)S(1)} %pad_maximum_fusion.5), channel_id=1, source_target_pairs={{0,8},{4,12},{8,0},{12,4},{16,24},{20,28},{24,16},{28,20},{1,9},{5... | collective-permute-start | bytes 786440 | tf_op jit(solution)/shard_map/ppermute | solution.py:21
  37.0 3.2 %copy-start.9 = (f32[80,512]{1,0:T(8,128)}, f32[80,512]{1,0:T(8,128)S(1)}, u32[]{:S(2)}) copy-start(f32[80,512]{1,0:T(8,128)S(1)} %slice.117) | copy-start | bytes 491524
  37.0 3.1 %copy-start.11 = (f32[80,512]{1,0:T(8,128)}, f32[80,512]{1,0:T(8,128)S(1)}, u32[]{:S(2)}) copy-start(f32[80,512]{1,0:T(8,128)S(1)} %slice.111) | copy-start | bytes 491524
  40.7 5.7 %collective-permute-start.1 = (f32[4,320,512]{2,1,0:T(8,128)S(1)}, f32[4,320,512]{2,1,0:T(8,128)S(1)}, u32[]{:S(2)}, u32[]{:S(2)}) collective-permute-start(f32[4,320,512]{2,1,0:T(8,128)S(1)} %pad_maximum_fusion.refs_0_), channel_id=1, source_target_pairs={{0,4},{4,0},{8,12},{12,8},{16,20},{20,16},{24,28},{28,24},{1,5},{5... | collective-permute-start | bytes 7864328 | tf_op jit(solution)/shard_map/cond/branch_1_fun/ppermute | solution.py:21
  40.8 5.6 %collective-permute-start = (f32[4,64,512]{2,1,0:T(8,128)S(1)}, f32[4,64,512]{2,1,0:T(8,128)S(1)}, u32[]{:S(2)}, u32[]{:S(2)}) collective-permute-start(f32[4,64,512]{2,1,0:T(8,128)S(1)} %get-tuple-element.91), channel_id=1, source_target_pairs={{0,4},{4,0},{8,12},{12,8},{16,20},{20,16},{24,28},{28,24},{1,5},{5... | collective-permute-start | bytes 1572872 | tf_op jit(solution)/shard_map/cond/branch_1_fun/ppermute | solution.py:21
  46.5 7.3 %collective-permute-start.4 = (f32[64,512]{1,0:T(8,128)S(1)}, f32[64,512]{1,0:T(8,128)S(1)}, u32[]{:S(2)}, u32[]{:S(2)}) collective-permute-start(f32[64,512]{1,0:T(8,128)S(1)} %get-tuple-element.293), channel_id=1, source_target_pairs={{0,24},{4,28},{8,16},{12,20},{16,8},{20,12},{24,0},{28,4},{1,25},{... | collective-permute-start | bytes 393224 | tf_op jit(solution)/shard_map/cond/branch_1_fun/ppermute | solution.py:21
  48.0 7.8 %collective-permute-start.3 = (f32[64,512]{1,0:T(8,128)S(1)}, f32[64,512]{1,0:T(8,128)S(1)}, u32[]{:S(2)}, u32[]{:S(2)}) collective-permute-start(f32[64,512]{1,0:T(8,128)S(1)} %get-tuple-element.294), channel_id=1, source_target_pairs={{0,16},{4,20},{8,24},{12,28},{16,0},{20,4},{24,8},{28,12},{1,17},{... | collective-permute-start | bytes 393224 | tf_op jit(solution)/shard_map/cond/branch_1_fun/ppermute | solution.py:21
  50.0 5.8 %collective-permute-start.2 = (f32[64,512]{1,0:T(8,128)S(1)}, f32[64,512]{1,0:T(8,128)S(1)}, u32[]{:S(2)}, u32[]{:S(2)}) collective-permute-start(f32[64,512]{1,0:T(8,128)S(1)} %get-tuple-element.292), channel_id=1, source_target_pairs={{0,8},{4,12},{8,0},{12,4},{16,24},{20,28},{24,16},{28,20},{1,9},{5... | collective-permute-start | bytes 393224 | tf_op jit(solution)/shard_map/cond/branch_1_fun/ppermute | solution.py:21
  55.8 9.4 %copy-start.20 = (f32[64,512]{1,0:T(8,128)}, f32[64,512]{1,0:T(8,128)S(1)}, u32[]{:S(2)}) copy-start(f32[64,512]{1,0:T(8,128)S(1)} %get-tuple-element.285.refs_1_) | copy-start | bytes 393220
  55.8 10.1 %collective-permute-start.22 = (f32[80,512]{1,0:T(8,128)S(1)}, f32[80,512]{1,0:T(8,128)S(1)}, u32[]{:S(2)}, u32[]{:S(2)}) collective-permute-start(f32[80,512]{1,0:T(8,128)S(1)} %get-tuple-element.267), channel_id=1, source_target_pairs={{0,2},{1,3},{2,0},{3,1},{4,6},{5,7},{6,4},{7,5},{8,10},{9,11},{10,... | collective-permute-start | bytes 491528 | tf_op jit(solution)/shard_map/ppermute | solution.py:21
  58.5 9.3 %collective-permute-start.21 = (f32[80,512]{1,0:T(8,128)S(1)}, f32[80,512]{1,0:T(8,128)S(1)}, u32[]{:S(2)}, u32[]{:S(2)}) collective-permute-start(f32[80,512]{1,0:T(8,128)S(1)} %get-tuple-element.264), channel_id=1, source_target_pairs={{0,1},{1,0},{2,3},{3,2},{4,5},{5,4},{6,7},{7,6},{8,9},{9,8},{10,11... | collective-permute-start | bytes 491528 | tf_op jit(solution)/shard_map/ppermute | solution.py:21
  60.0 10.1 %copy-start.2 = (f32[512,512]{1,0:T(8,128)S(1)}, f32[512,512]{1,0:T(8,128)}, u32[]{:S(2)}) copy-start(f32[512,512]{1,0:T(8,128)} %refs_0_.2) | copy-start | bytes 3145732
  60.0 10.1 %copy-start.4 = (f32[512,512]{1,0:T(8,128)S(1)}, f32[512,512]{1,0:T(8,128)}, u32[]{:S(2)}) copy-start(f32[512,512]{1,0:T(8,128)} %refs_1_.1) | copy-start | bytes 3145732
  60.0 10.1 %copy-start.10 = (f32[80,512]{1,0:T(8,128)S(1)}, f32[80,512]{1,0:T(8,128)}, u32[]{:S(2)}) copy-start(f32[80,512]{1,0:T(8,128)} %copy-done.9) | copy-start | bytes 491524
  60.0 10.1 %copy-start.12 = (f32[80,512]{1,0:T(8,128)S(1)}, f32[80,512]{1,0:T(8,128)}, u32[]{:S(2)}) copy-start(f32[80,512]{1,0:T(8,128)} %copy-done.11) | copy-start | bytes 491524
  66.0 42.3 %collective-permute-start.23 = (f32[432,512]{1,0:T(8,128)S(1)}, f32[432,512]{1,0:T(8,128)S(1)}, u32[]{:S(2)}, u32[]{:S(2)}) collective-permute-start(f32[432,512]{1,0:T(8,128)S(1)} %get-tuple-element.279), channel_id=1, source_target_pairs={{0,1},{1,0},{2,3},{3,2},{4,5},{5,4},{6,7},{7,6},{8,9},{9,8},{10,11... | collective-permute-start | bytes 2654216 | tf_op jit(solution)/shard_map/ppermute | solution.py:21
  67.8 41.6 %collective-permute-start.24 = (f32[432,512]{1,0:T(8,128)S(1)}, f32[432,512]{1,0:T(8,128)S(1)}, u32[]{:S(2)}, u32[]{:S(2)}) collective-permute-start(f32[432,512]{1,0:T(8,128)S(1)} %get-tuple-element.281), channel_id=1, source_target_pairs={{0,2},{1,3},{2,0},{3,1},{4,6},{5,7},{6,4},{7,5},{8,10},{9,11},{10,... | collective-permute-start | bytes 2654216 | tf_op jit(solution)/shard_map/ppermute | solution.py:21
  70.3 1.3 %copy-start.7 = (bf16[2,512,512]{2,1,0:T(8,128)(2,1)}, bf16[2,512,512]{2,1,0:T(8,128)(2,1)S(1)}, u32[]{:S(2)}) copy-start(bf16[2,512,512]{2,1,0:T(8,128)(2,1)S(1)} %get-tuple-element.153.refs_13_) | copy-start | bytes 3145732 | tf_op jit(solution)/shard_map/cond
  70.3 6.5 %copy-start.13 = (bf16[1,512,512]{2,1,0:T(8,128)(2,1)}, bf16[1,512,512]{2,1,0:T(8,128)(2,1)S(1)}, u32[]{:S(2)}) copy-start(bf16[1,512,512]{2,1,0:T(8,128)(2,1)S(1)} %get-tuple-element.150.refs_10_) | copy-start | bytes 1572868 | tf_op jit(solution)/shard_map/cond
  70.4 6.5 %copy-start.16 = (f32[80,256]{1,0:T(8,128)}, f32[80,256]{1,0:T(8,128)S(1)}, u32[]{:S(2)}) copy-start(f32[80,256]{1,0:T(8,128)S(1)} %get-tuple-element.144.refs_4_) | copy-start | bytes 245764 | tf_op jit(solution)/shard_map/cond
  70.4 6.5 %copy-start.18 = (f32[80,256]{1,0:T(8,128)}, f32[80,256]{1,0:T(8,128)S(1)}, u32[]{:S(2)}) copy-start(f32[80,256]{1,0:T(8,128)S(1)} %get-tuple-element.146.refs_6_) | copy-start | bytes 245764 | tf_op jit(solution)/shard_map/cond
  76.9 4.2 %collective-permute-start.5 = (f32[4,256,512]{2,1,0:T(8,128)S(1)}, f32[4,256,512]{2,1,0:T(8,128)S(1)}, u32[]{:S(2)}, u32[]{:S(2)}) collective-permute-start(f32[4,256,512]{2,1,0:T(8,128)S(1)} %get-tuple-element.135), channel_id=1, source_target_pairs={{0,4},{4,0},{8,12},{12,8},{16,20},{20,16},{24,28},{28,24},{1,5},{5... | collective-permute-start | bytes 6291464 | tf_op jit(solution)/shard_map/cond/branch_1_fun/ppermute | solution.py:21
  81.6 3.8 %copy-start.6 = (bf16[2,512,512]{2,1,0:T(8,128)(2,1)S(1)}, bf16[2,512,512]{2,1,0:T(8,128)(2,1)}, u32[]{:S(2)}) copy-start(bf16[2,512,512]{2,1,0:T(8,128)(2,1)} %copy-done.5) | copy-start | bytes 3145732 | tf_op jit(solution)/shard_map/cond
  81.6 3.8 %copy-start.8 = (bf16[2,512,512]{2,1,0:T(8,128)(2,1)S(1)}, bf16[2,512,512]{2,1,0:T(8,128)(2,1)}, u32[]{:S(2)}) copy-start(bf16[2,512,512]{2,1,0:T(8,128)(2,1)} %copy-done.7) | copy-start | bytes 3145732 | tf_op jit(solution)/shard_map/cond
  81.6 3.8 %copy-start.14 = (bf16[1,512,512]{2,1,0:T(8,128)(2,1)S(1)}, bf16[1,512,512]{2,1,0:T(8,128)(2,1)}, u32[]{:S(2)}) copy-start(bf16[1,512,512]{2,1,0:T(8,128)(2,1)} %copy-done.13) | copy-start | bytes 1572868 | tf_op jit(solution)/shard_map/cond
  81.7 3.8 %copy-start.15 = (bf16[1,512,512]{2,1,0:T(8,128)(2,1)S(1)}, bf16[1,512,512]{2,1,0:T(8,128)(2,1)}, u32[]{:S(2)}) copy-start(bf16[1,512,512]{2,1,0:T(8,128)(2,1)} %get-tuple-element.151.refs_11_) | copy-start | bytes 1572868 | tf_op jit(solution)/shard_map/cond
  81.7 3.8 %copy-start.17 = (f32[80,256]{1,0:T(8,128)S(1)}, f32[80,256]{1,0:T(8,128)}, u32[]{:S(2)}) copy-start(f32[80,256]{1,0:T(8,128)} %copy-done.16) | copy-start | bytes 245764 | tf_op jit(solution)/shard_map/cond
  81.7 3.8 %copy-start.19 = (f32[80,256]{1,0:T(8,128)S(1)}, f32[80,256]{1,0:T(8,128)}, u32[]{:S(2)}) copy-start(f32[80,256]{1,0:T(8,128)} %copy-done.18) | copy-start | bytes 245764 | tf_op jit(solution)/shard_map/cond
  81.9 15.5 %collective-permute-start.6 = (f32[2,128,512]{2,1,0:T(8,128)S(1)}, f32[2,128,512]{2,1,0:T(8,128)S(1)}, u32[]{:S(2)}, u32[]{:S(2)}) collective-permute-start(f32[2,128,512]{2,1,0:T(8,128)S(1)} %pad_maximum_fusion.1), channel_id=1, source_target_pairs={{0,8},{4,12},{8,0},{12,4},{16,24},{20,28},{24,16},{28,20},{1,9},{5... | collective-permute-start | bytes 1572872 | tf_op jit(solution)/shard_map/cond/branch_1_fun/ppermute | solution.py:21
  85.2 13.7 %collective-permute-start.7 = (f32[2,128,512]{2,1,0:T(8,128)S(1)}, f32[2,128,512]{2,1,0:T(8,128)S(1)}, u32[]{:S(2)}, u32[]{:S(2)}) collective-permute-start(f32[2,128,512]{2,1,0:T(8,128)S(1)} %pad_maximum_fusion.2), channel_id=1, source_target_pairs={{0,16},{4,20},{8,24},{12,28},{16,0},{20,4},{24,8},{28,12},{1,17},{... | collective-permute-start | bytes 1572872 | tf_op jit(solution)/shard_map/cond/branch_1_fun/ppermute | solution.py:21
  98.9 7.3 %collective-permute-start.8 = (f32[1,128,512]{2,1,0:T(8,128)S(1)}, f32[1,128,512]{2,1,0:T(8,128)S(1)}, u32[]{:S(2)}, u32[]{:S(2)}) collective-permute-start(f32[1,128,512]{2,1,0:T(8,128)S(1)} %get-tuple-element.164), channel_id=1, source_target_pairs={{0,16},{4,20},{8,24},{12,28},{16,0},{20,4},{24,8},{28,12},{1,17},{... | collective-permute-start | bytes 786440 | tf_op jit(solution)/shard_map/cond/branch_1_fun/ppermute | solution.py:21
  99.3 7.0 %collective-permute-start.9 = (f32[1,128,512]{2,1,0:T(8,128)S(1)}, f32[1,128,512]{2,1,0:T(8,128)S(1)}, u32[]{:S(2)}, u32[]{:S(2)}) collective-permute-start(f32[1,128,512]{2,1,0:T(8,128)S(1)} %get-tuple-element.165), channel_id=1, source_target_pairs={{0,8},{4,12},{8,0},{12,4},{16,24},{20,28},{24,16},{28,20},{1,9},{5... | collective-permute-start | bytes 786440 | tf_op jit(solution)/shard_map/cond/branch_1_fun/ppermute | solution.py:21
  106.5 7.3 %collective-permute-start.25 = (f32[96,512]{1,0:T(8,128)S(1)}, f32[96,512]{1,0:T(8,128)S(1)}, u32[]{:S(2)}, u32[]{:S(2)}) collective-permute-start(f32[96,512]{1,0:T(8,128)S(1)} %get-tuple-element.287), channel_id=1, source_target_pairs={{0,1},{1,0},{2,3},{3,2},{4,5},{5,4},{6,7},{7,6},{8,9},{9,8},{10,11... | collective-permute-start | bytes 589832 | tf_op jit(solution)/shard_map/ppermute | solution.py:21
  107.9 5.9 %collective-permute-start.26 = (f32[32,512]{1,0:T(8,128)S(1)}, f32[32,512]{1,0:T(8,128)S(1)}, u32[]{:S(2)}, u32[]{:S(2)}) collective-permute-start(f32[32,512]{1,0:T(8,128)S(1)} %get-tuple-element.288), channel_id=1, source_target_pairs={{0,2},{1,3},{2,0},{3,1},{4,6},{5,7},{6,4},{7,5},{8,10},{9,11},{10,... | collective-permute-start | bytes 196616 | tf_op jit(solution)/shard_map/ppermute | solution.py:21
  108.3 5.5 %copy-start.21 = (f32[64,512]{1,0:T(8,128)S(1)}, f32[64,512]{1,0:T(8,128)}, u32[]{:S(2)}) copy-start(f32[64,512]{1,0:T(8,128)} %copy-done.20) | copy-start | bytes 393220
  (1 other events, 1.0 us)

commit v4 on v3

--- a/solution.py
+++ b/solution.py
@@ -10,7 +10,7 @@
 
 F32 = jnp.float32
 BF16 = jnp.bfloat16
-EARLY = 80
+EARLY = 48
 VMEM_BYTES = 20 * 1024 * 1024
 JOIN_VMEM_BYTES = 8 * 1024 * 1024
 PACK_VMEM_BYTES = 60 * 1024 * 1024
@@ -143,7 +143,7 @@
         out_ref[:step, p * rank : (p + 1) * rank] = left[p * step : (p + 1) * step]
 
 
-def pack_kernel(bits_ref, w_ref, left_ref, right_ref, x_ref, g_ref, near_ref, far_ref, own_ref):
+def pack_kernel(bits_ref, w_ref, left_ref, right_ref, x_ref, g_ref, near_ref, far_ref, own_ref, self_ref):
     _, slots, rows, block = w_ref.shape
     sections = slots - 1
     rank_rows = right_ref.shape[1]
@@ -153,10 +153,10 @@
     near_ref[rows + rank_rows :] = g_ref[...]
     put_left(far_ref.at[:flat], left_ref[0], block)
     far_ref[flat:] = x_ref[...]
-    own_ref[:rows] = w_ref[0, 0]
+    self_ref[...] = w_ref[0, 0]
     for b in range(1, sections):
-        own_ref[b * rows : (b + 1) * rows] = slot_weights(bits_ref, w_ref, b, sections)
-    at = sections * rows
+        own_ref[(b - 1) * rows : b * rows] = slot_weights(bits_ref, w_ref, b, sections)
+    at = (sections - 1) * rows
     own_ref[at : at + rank_rows] = right_ref[0]
     put_left(own_ref.at[at + rank_rows :], left_ref[0], block)
 
@@ -225,7 +225,6 @@
                 move(lh, ll, i, owner * rows + p * flat, flat, value)
             return start + flat
 
-        at = move_wide(sh, sl, 0, at, rows)
         for i in range(sections - 1):
             at = move_wide(wh, wl, i, at, rows)
         at = move_wide(rh, rl, 0, at, rank_rows)
@@ -233,12 +232,27 @@
         at = move_wide(wh, wl, sections - 1, at, rows)
         at = move_wide(rh, rl, 1, at, rank_rows)
         at = move_left(1, at)
+        at = move_wide(sh, sl, 0, at, rows)
     if early:
         messages(*early, (wh, wl), (lh, ll, rh, rl), outs)
 
 
-def messages_kernel(x_ref, g_ref, far_ref, near_ref, wh, wl, lh, ll, rh, rl, *outs):
-    messages(x_ref, g_ref, far_ref, near_ref, (wh, wl), (lh, ll, rh, rl), outs)
+def begin_kernel(x_ref, g_ref, wh, wl, lh, ll, rh, rl, c_ref, cg_ref, ahead_ref, back_ref):
+    x, g = split(x_ref[...]), split(g_ref[...])
+    c_ref[...] = nn(x, (lh[0], ll[0]))
+    cg_ref[...] = nt(g, (rh[0], rl[0]))
+    ahead_ref[...] = nn(x, (wh[1], wl[1]))
+    back_ref[...] = nt(g, (wh[0], wl[0]))
+
+
+def messages_kernel(far_ref, near_ref, lh, ll, rh, rl, *refs):
+    c0_ref, cg0_ref, ahead0_ref, back0_ref, c_ref, cg_ref, ahead_ref, back_ref = refs
+    codes = c0_ref[...] + nn(split(far_ref[...]), (lh[1], ll[1]))
+    code_grads = cg0_ref[...] + nt(split(near_ref[...]), (rh[1], rl[1]))
+    c_ref[...] = codes
+    cg_ref[...] = code_grads
+    ahead_ref[...] = ahead0_ref[...] + nn(split(codes), (rh[1], rl[1]))
+    back_ref[...] = back0_ref[...] + nt(split(code_grads), (lh[1], ll[1]))
 
 
 def codes_kernel(x_ref, g_ref, far_ref, near_ref, lh, ll, rh, rl, c_ref, cg_ref):
@@ -393,8 +407,8 @@
     scale = 1.0 / math.sqrt(tokens * dp_count)
 
     by_slot = jnp.transpose(block_weights, (0, 2, 1, 3))
-    pack_shapes = [(lent_rows + early, block), (flat + early, block), (own_rows, block)]
-    out_near, out_far, own = call(
+    pack_shapes = [(lent_rows + early, block), (flat + early, block), (own_rows - rows, block), (rows, block)]
+    out_near, out_far, own, own_self = call(
         pack_kernel,
         [f32(*s) for s in pack_shapes],
         [partner_bits, by_slot, low_left, low_right, inputs, cotangent],
@@ -414,7 +428,7 @@
     late_g, got_near = lax.optimization_barrier((cotangent[early:], got_near))
     late_near = across(late_g, "feat", 1)
     early_far, early_near = got_far[flat:], got_near[lent_rows:]
-    lent = jnp.concatenate([got_near[:lent_rows], got_far[:flat]])
+    lent = jnp.concatenate([got_near[:lent_rows], got_far[:flat], own_self])
     lent, own = lax.optimization_barrier((lent, own))
     lent = gather_rows(lent, dp_count)
     *self_keep, self_give = call(
@@ -471,18 +485,27 @@
     far = [[early_far, late_far]]
     if folds:
         late_shapes = message_shapes(late)
+        step = late // 2 if late % 32 == 0 else late
+        late_specs = [by_tokens(step, width) for _, width in late_shapes]
+        begun = call(
+            begin_kernel,
+            [f32(*s) for s in late_shapes],
+            [late_x, late_g, *weights[2:]],
+            grid=(late // step,),
+            in_specs=[by_tokens(step, block)] * 2 + weight_specs[2:],
+            out_specs=late_specs,
+        )
         late_sent = call(
             messages_kernel,
             [f32(*s) for s in late_shapes],
-            [late_x, late_g, late_far, late_near, *weights[2:]],
-            grid=(1,),
-            in_specs=[whole((late, block))] * 4 + weight_specs[2:],
-            out_specs=[whole(s) for s in late_shapes],
+            [late_far, late_near, *weights[4:], *begun],
+            grid=(late // step,),
+            in_specs=[by_tokens(step, block)] * 2 + weight_specs[4:] + late_specs,
+            out_specs=late_specs,
         )
         first = [across(part, "feat", 1 << b) for b, part in enumerate(sent[2:])]
         rest = list(late_sent[2:])
-        rest[0], first[1] = lax.optimization_barrier((rest[0], first[1]))
-        rest[1], first[0] = lax.optimization_barrier((rest[1], first[0]))
+        rest[0], first = lax.optimization_barrier((rest[0], first))
         first, late_sent = lax.optimization_barrier((first, late_sent))
         rest = [across(part, "feat", 1 << b) for b, part in enumerate(rest)]
         codes, code_grads = ([sent[i], late_sent[i]] for i in range(2))

time: 115 us -> 115 us (level)
  starting transfers between devices: 38.1 us -> 34.1 us
  waiting for transfers between devices: 45.6 us -> 48.8 us
  local copies, waits for them, and re-layouts: 2.88 us -> 1.72 us
    ppermute x27, starting transfers between devices: 38.1 us -> 34.1 us  [across(): return lax.ppermute(block, axis, [(i, i ^ apart) for i in range(count)])]
    ppermute x27, waiting for transfers between devices: 45.6 us -> 48.8 us  [across(): return lax.ppermute(block, axis, [(i, i ^ apart) for i in range(count)])]
    cond x22 -> x4, local copies, waits for them, and re-layouts: 1.32 us -> 0.01 us
    pallas_call x9 -> x10, Pallas kernels: 25.9 us -> 27 us  [call(): pl.pallas_call(kernel, out_shape=out_shapes, in_specs=in_specs, out_specs...]
  transfers between devices with their start and end apart: 27 -> 27, of which waited for: 17 -> 19; matrix products, arithmetic and copies ran while one was open for 3% -> 3% of each run, Pallas kernels for 20% -> 21%
where the time goes in v4:
time: 115 us; the launch traced here: 114 us
  waiting for transfers between devices  48.8 us (42%)
  starting transfers between devices  34.1 us (30%)
  Pallas kernels  27 us (23%)
  local copies, waits for them, and re-layouts  1.72 us (1%)
  other arithmetic  1.39 us (1%)
    ppermute x27, waiting for transfers between devices, across(): return lax.ppermute(block, axis, [(i, i ^ apart) for i in range(count)])  48.8 us
    ppermute x27, starting transfers between devices, across(): return lax.ppermute(block, axis, [(i, i ^ apart) for i in range(count)])  34.1 us
    pallas_call x10, Pallas kernels, call(): pl.pallas_call(kernel, out_shape=out_shapes, in_specs=in_specs, out_specs...  27 us
  transfers between devices with their start and end apart: 27, of which 19 were waited for; matrix products, arithmetic and copies ran while one was open for 3% of the time, Pallas kernels for 21%

profile of v4, /device:TPU:0, one launch (start us, length us, event | category | flops | bytes accessed | tf_op | source)
XLA Modules:
  0.0 114.4 jit_solution(5284025164986682426)
XLA Ops:
  0.6 2.0 %shard_map.101 = (f32[144,512]{1,0:T(8,128)}, f32[80,512]{1,0:T(8,128)}, f32[128,512]{1,0:T(8,128)S(1)}, f32[64,512]{1,0:T(8,128)}) custom-call(s32[1,2]{1,0:T(1,128)} %refs_0_.3, f32[1,3,64,512]{3,2,1,0:T(8,128)} %bitcast.83, f32[1,64,256]{2,1,0:T(8,128)} %left_ref.1, f32[1,32,512]{2,1,0:T(8,128)} %right_ref.1, f32[512,512]{1,0:T(8,128)} %refs_0_.2, ...), custom_call_target="tpu_custom_call" | custom-call | flops 1 | bytes 1 | tf_op jit(solution)/shard_map/pallas_call | solution.py:103
  2.7 3.0 %collective-permute-start.10 = (f32[144,512]{1,0:T(8,128)}, f32[144,512]{1,0:T(8,128)S(1)}, u32[]{:S(2)}, u32[]{:S(2)}) collective-permute-start(f32[144,512]{1,0:T(8,128)} %get-tuple-element.239), channel_id=1, source_target_pairs={{0,1},{1,0},{2,3},{3,2},{4,5},{5,4},{6,7},{7,6},{8,9},{9,8},{10,11... | collective-permute-start | bytes 884744 | tf_op jit(solution)/shard_map/ppermute | solution.py:21
  5.7 2.6 %collective-permute-start.12 = (f32[80,512]{1,0:T(8,128)}, f32[80,512]{1,0:T(8,128)S(1)}, u32[]{:S(2)}, u32[]{:S(2)}) collective-permute-start(f32[80,512]{1,0:T(8,128)} %get-tuple-element.243), channel_id=1, source_target_pairs={{0,2},{1,3},{2,0},{3,1},{4,6},{5,7},{6,4},{7,5},{8,10},{9,11},{10,... | collective-permute-start | bytes 491528 | tf_op jit(solution)/shard_map/ppermute | solution.py:21
  8.3 1.5 %collective-permute-start.13 = (f32[128,512]{1,0:T(8,128)S(1)}, f32[128,512]{1,0:T(8,128)S(1)}, u32[]{:S(2)}, u32[]{:S(2)}) collective-permute-start(f32[128,512]{1,0:T(8,128)S(1)} %get-tuple-element.247), channel_id=1, source_target_pairs={{0,8},{4,12},{8,0},{12,4},{16,24},{20,28},{24,16},{28,20},{1,9},{5... | collective-permute-start | bytes 786440 | tf_op jit(solution)/shard_map/ppermute | solution.py:21
  9.8 1.5 %collective-permute-start.14 = (f32[128,512]{1,0:T(8,128)S(1)}, f32[128,512]{1,0:T(8,128)S(1)}, u32[]{:S(2)}, u32[]{:S(2)}) collective-permute-start(f32[128,512]{1,0:T(8,128)S(1)} %get-tuple-element.247), channel_id=1, source_target_pairs={{0,16},{4,20},{8,24},{12,28},{16,0},{20,4},{24,8},{28,12},{1,17},{... | collective-permute-start | bytes 786440 | tf_op jit(solution)/shard_map/ppermute | solution.py:21
  11.8 1.3 %slice.110.g_ref = f32[464,512]{1,0:T(8,128)S(1)} slice(f32[512,512]{1,0:T(8,128)} %refs_1_.1), slice={[48:512], [0:512]} | slice | bytes 1900544 | tf_op jit(solution)/shard_map/slice | solution.py:428
  13.1 2.7 %collective-permute-done.12 = f32[80,512]{1,0:T(8,128)S(1)} collective-permute-done((f32[80,512]{1,0:T(8,128)}, f32[80,512]{1,0:T(8,128)S(1)}, u32[]{:S(2)}, u32[]{:S(2)}) %collective-permute-start.12) | collective-permute-done | bytes 163872 | tf_op jit(solution)/shard_map/ppermute | solution.py:21
  15.8 3.3 %collective-permute-start.20 = (f32[464,512]{1,0:T(8,128)S(1)}, f32[464,512]{1,0:T(8,128)}, u32[]{:S(2)}, u32[]{:S(2)}) collective-permute-start(f32[464,512]{1,0:T(8,128)S(1)} %slice.113.x_ref), channel_id=1, source_target_pairs={{0,2},{1,3},{2,0},{3,1},{4,6},{5,7},{6,4},{7,5},{8,10},{9,11},{10,... | collective-permute-start | bytes 2850824 | tf_op jit(solution)/shard_map/ppermute | solution.py:21
  19.4 3.2 %collective-permute-done.14 = f32[128,512]{1,0:T(8,128)S(1)} collective-permute-done((f32[128,512]{1,0:T(8,128)S(1)}, f32[128,512]{1,0:T(8,128)S(1)}, u32[]{:S(2)}, u32[]{:S(2)}) %collective-permute-start.14) | collective-permute-done | bytes 262176 | tf_op jit(solution)/shard_map/ppermute | solution.py:21
  22.7 1.3 %collective-permute-start.16 = (f32[1,96,512]{2,1,0:T(8,128)S(1)}, f32[1,96,512]{2,1,0:T(8,128)S(1)}, u32[]{:S(2)}, u32[]{:S(2)}) collective-permute-start(f32[1,96,512]{2,1,0:T(8,128)S(1)} %get-tuple-element.322), channel_id=1, source_target_pairs={{0,8},{4,12},{8,0},{12,4},{16,24},{20,28},{24,16},{28,20},{1,9},{5... | collective-permute-start | bytes 589832 | tf_op jit(solution)/shard_map/ppermute | solution.py:21
  24.0 0.8 collective-permute-start.17
  24.8 3.6 %collective-permute-done.16 = f32[1,96,512]{2,1,0:T(8,128)S(1)} collective-permute-done((f32[1,96,512]{2,1,0:T(8,128)S(1)}, f32[1,96,512]{2,1,0:T(8,128)S(1)}, u32[]{:S(2)}, u32[]{:S(2)}) %collective-permute-start.16) | collective-permute-done | bytes 196640 | tf_op jit(solution)/shard_map/ppermute | solution.py:21
  28.4 1.2 %collective-permute-done.17 = f32[1,96,512]{2,1,0:T(8,128)S(1)} collective-permute-done((f32[1,96,512]{2,1,0:T(8,128)S(1)}, f32[1,96,512]{2,1,0:T(8,128)S(1)}, u32[]{:S(2)}, u32[]{:S(2)}) %collective-permute-start.17) | collective-permute-done | bytes 196640 | tf_op jit(solution)/shard_map/ppermute | solution.py:21
  29.7 1.1 collective-permute-start.18
  30.8 2.6 %collective-permute-start.19 = (f32[2,96,512]{2,1,0:T(8,128)S(1)}, f32[2,96,512]{2,1,0:T(8,128)S(1)}, u32[]{:S(2)}, u32[]{:S(2)}) collective-permute-start(f32[2,96,512]{2,1,0:T(8,128)S(1)} %pad_maximum_fusion.5), channel_id=1, source_target_pairs={{0,8},{4,12},{8,0},{12,4},{16,24},{20,28},{24,16},{28,20},{1,9},{5... | collective-permute-start | bytes 1179656 | tf_op jit(solution)/shard_map/ppermute | solution.py:21
  33.4 1.1 shard_map.102
  34.6 3.5 %collective-permute-done.18 = f32[2,96,512]{2,1,0:T(8,128)S(1)} collective-permute-done((f32[2,96,512]{2,1,0:T(8,128)S(1)}, f32[2,96,512]{2,1,0:T(8,128)S(1)}, u32[]{:S(2)}, u32[]{:S(2)}) %collective-permute-start.18) | collective-permute-done | bytes 393248 | tf_op jit(solution)/shard_map/ppermute | solution.py:21
  38.1 1.1 collective-permute-done.19
  39.2 15.7 %conditional.2 = (f32[64,512]{1,0:T(8,128)S(1)}, bf16[1,512,512]{2,1,0:T(8,128)(2,1)S(1)}, bf16[1,512,512]{2,1,0:T(8,128)(2,1)S(1)}, bf16[2,512,512]{2,1,0:T(8,1...) conditional(s32[]{:T(128)} %bitcast.30, () %tuple.40, ...), branch_computations={%region_0.0_spmd, %region_1.0_spmd} | conditional | flops 3506177 | bytes 28180784 | solution.py:478
  40.3 5.1 %collective-permute-done = f32[4,64,512]{2,1,0:T(8,128)S(1)} collective-permute-done((f32[4,64,512]{2,1,0:T(8,128)S(1)}, f32[4,64,512]{2,1,0:T(8,128)S(1)}, u32[]{:S(2)}, u32[]{:S(2)}) %collective-permute-start) | collective-permute-done | bytes 524320 | tf_op jit(solution)/shard_map/cond/branch_1_fun/ppermute | solution.py:21
  45.5 1.5 %collective-permute-start.4 = (f32[64,512]{1,0:T(8,128)S(1)}, f32[64,512]{1,0:T(8,128)S(1)}, u32[]{:S(2)}, u32[]{:S(2)}) collective-permute-start(f32[64,512]{1,0:T(8,128)S(1)} %get-tuple-element.301), channel_id=1, source_target_pairs={{0,24},{4,28},{8,16},{12,20},{16,8},{20,12},{24,0},{28,4},{1,25},{... | collective-permute-start | bytes 393224 | tf_op jit(solution)/shard_map/cond/branch_1_fun/ppermute | solution.py:21
  47.0 2.0 %collective-permute-start.3 = (f32[64,512]{1,0:T(8,128)S(1)}, f32[64,512]{1,0:T(8,128)S(1)}, u32[]{:S(2)}, u32[]{:S(2)}) collective-permute-start(f32[64,512]{1,0:T(8,128)S(1)} %get-tuple-element.302), channel_id=1, source_target_pairs={{0,16},{4,20},{8,24},{12,28},{16,0},{20,4},{24,8},{28,12},{1,17},{... | collective-permute-start | bytes 393224 | tf_op jit(solution)/shard_map/cond/branch_1_fun/ppermute | solution.py:21
  49.0 2.5 %branch_1_fun.3 = (bf16[1,512,512]{2,1,0:T(8,128)(2,1)S(1)}, bf16[1,512,512]{2,1,0:T(8,128)(2,1)S(1)}, bf16[2,512,512]{2,1,0:T(8,128)(2,1)S(1)}, bf16[2,512,512]...) custom-call(f32[4,320,512]{2,1,0:T(8,128)S(1)} %pad_maximum_fusion.r, ...), custom_call_target="tpu_custom_call" | custom-call | flops 1 | bytes 1 | tf_op jit(solution)/shard_map/cond/branch_1_fun/pallas_call | solution.py:103
  51.5 1.3 %collective-permute-done.4 = f32[64,512]{1,0:T(8,128)S(1)} collective-permute-done((f32[64,512]{1,0:T(8,128)S(1)}, f32[64,512]{1,0:T(8,128)S(1)}, u32[]{:S(2)}, u32[]{:S(2)}) %collective-permute-start.4) | collective-permute-done | bytes 131104 | tf_op jit(solution)/shard_map/cond/branch_1_fun/ppermute | solution.py:21
  52.8 2.0 %collective-permute-done.3 = f32[64,512]{1,0:T(8,128)S(1)} collective-permute-done((f32[64,512]{1,0:T(8,128)S(1)}, f32[64,512]{1,0:T(8,128)S(1)}, u32[]{:S(2)}, u32[]{:S(2)}) %collective-permute-start.3) | collective-permute-done | bytes 131104 | tf_op jit(solution)/shard_map/cond/branch_1_fun/ppermute | solution.py:21
  55.5 2.4 %shard_map.103 = (f32[464,256]{1,0:T(8,128)S(1)}, f32[464,256]{1,0:T(8,128)S(1)}, f32[464,512]{1,0:T(8,128)S(1)}, f32[464,512]{1,0:T(8,128)S(1)}) custom-call(f32[464,512]{1,0:T(8,128)S(1)} %slice.113.x_ref, f32[464,512]{1,0:T(8,128)S(1)} %slice.110.g_ref, bf16[2,512,512]{2,1,0:T(8,128)(2,1)S(1)} %get-tuple-element.266.wh, ...), custom_call_target="tpu_custom_call" | custom-call | flops 1 | bytes 1 | tf_op jit(solution)/shard_map/pallas_call | solution.py:103
  57.9 2.6 %collective-permute-done.20.far_ref = f32[464,512]{1,0:T(8,128)} collective-permute-done((f32[464,512]{1,0:T(8,128)S(1)}, f32[464,512]{1,0:T(8,128)}, u32[]{:S(2)}, u32[]{:S(2)}) %collective-permute-start.20) | collective-permute-done | bytes 950304 | tf_op jit(solution)/shard_map/ppermute | solution.py:21
  61.0 4.4 %shard_map.104 = (f32[464,256]{1,0:T(8,128)S(1)}, f32[464,256]{1,0:T(8,128)S(1)}, f32[464,512]{1,0:T(8,128)}, f32[464,512]{1,0:T(8,128)S(1)}) custom-call(f32[464,512]{1,0:T(8,128)} %collective-permute-done.20.far_ref, f32[464,512]{1,0:T(8,128)} %collective-permute-done.11.near_ref, bf16[2,512,256]{2,1,0:T(8,128)(2,1)S(1)} %get-tuple-element.262.lh, ...), custom_call_target="tpu_custom_call" | custom-call | flops 1 | bytes 1 | tf_op jit(solution)/shard_map/pallas_call | solution.py:103
  65.4 2.7 %collective-permute-start.23 = (f32[464,512]{1,0:T(8,128)}, f32[464,512]{1,0:T(8,128)S(1)}, u32[]{:S(2)}, u32[]{:S(2)}) collective-permute-start(f32[464,512]{1,0:T(8,128)} %get-tuple-element.288), channel_id=1, source_target_pairs={{0,1},{1,0},{2,3},{3,2},{4,5},{5,4},{6,7},{7,6},{8,9},{9,8},{10,11... | collective-permute-start | bytes 2850824 | tf_op jit(solution)/shard_map/ppermute | solution.py:21
  68.1 1.2 %collective-permute-start.24 = (f32[464,512]{1,0:T(8,128)S(1)}, f32[464,512]{1,0:T(8,128)S(1)}, u32[]{:S(2)}, u32[]{:S(2)}) collective-permute-start(f32[464,512]{1,0:T(8,128)S(1)} %get-tuple-element.279), channel_id=1, source_target_pairs={{0,2},{1,3},{2,0},{3,1},{4,6},{5,7},{6,4},{7,5},{8,10},{9,11},{10,... | collective-permute-start | bytes 2850824 | tf_op jit(solution)/shard_map/ppermute | solution.py:21
  69.3 34.5 %conditional.3 = (f32[512,512]{1,0:T(8,128)S(1)}, f32[512,512]{1,0:T(8,128)S(1)}, f32[96,512]{1,0:T(8,128)S(1)}, f32[32,512]{1,0:T(8,128)S(1)}, f32[128,512]{1,0:T(8,128)S(1)}) conditional(s32[]{:T(128)} %bitcast.30, () %tuple.38, (f32[512,512]{1,0:T(8,128)S(1)}, f32[512,512]{1,0:T(8,128)S(1)}, f32[48,512]{1,0:T(8,128)S(1)}, f32[464,512]{1,0:T(8,128)}, ...), branch_computations={%region_2.0_spmd, %region_3.0_spmd} | conditional | flops 1179650 | bytes 29753642 | solution.py:567
  69.6 5.3 %branch_1_fun.4 = (f32[256,512]{1,0:T(8,128)S(1)}, f32[256,512]{1,0:T(8,128)S(1)}, f32[256,512]{1,0:T(8,128)S(1)}, f32[256,512]{1,0:T(8,128)S(1)}, f32[4,256,512]{2,1,0:T(8,128)S(1)}) custom-call(f32[512,512]{1,0:T(8,128)S(1)} %get-tuple-element.140.refs_0_, f32[512,512]{1,0:T(8,128)S(1)} %get-tuple-element.141.refs_1_, ...), custom_call_target="tpu_custom_call" | custom-call | flops 1 | bytes 1 | tf_op jit(solution)/shard_map/cond/branch_1_fun/pallas_call | solution.py:103
  75.0 4.1 %collective-permute-done.5 = f32[4,256,512]{2,1,0:T(8,128)S(1)} collective-permute-done((f32[4,256,512]{2,1,0:T(8,128)S(1)}, f32[4,256,512]{2,1,0:T(8,128)S(1)}, u32[]{:S(2)}, u32[]{:S(2)}) %collective-permute-start.5) | collective-permute-done | bytes 2097184 | tf_op jit(solution)/shard_map/cond/branch_1_fun/ppermute | solution.py:21
  79.8 1.6 %collective-permute-start.6 = (f32[2,128,512]{2,1,0:T(8,128)S(1)}, f32[2,128,512]{2,1,0:T(8,128)S(1)}, u32[]{:S(2)}, u32[]{:S(2)}) collective-permute-start(f32[2,128,512]{2,1,0:T(8,128)S(1)} %pad_maximum_fusion.1), channel_id=1, source_target_pairs={{0,8},{4,12},{8,0},{12,4},{16,24},{20,28},{24,16},{28,20},{1,9},{5... | collective-permute-start | bytes 1572872 | tf_op jit(solution)/shard_map/cond/branch_1_fun/ppermute | solution.py:21
  81.3 1.5 %collective-permute-start.7 = (f32[2,128,512]{2,1,0:T(8,128)S(1)}, f32[2,128,512]{2,1,0:T(8,128)S(1)}, u32[]{:S(2)}, u32[]{:S(2)}) collective-permute-start(f32[2,128,512]{2,1,0:T(8,128)S(1)} %pad_maximum_fusion.2), channel_id=1, source_target_pairs={{0,16},{4,20},{8,24},{12,28},{16,0},{20,4},{24,8},{28,12},{1,17},{... | collective-permute-start | bytes 1572872 | tf_op jit(solution)/shard_map/cond/branch_1_fun/ppermute | solution.py:21
  82.9 5.7 %branch_1_fun.5 = (f32[512,512]{1,0:T(8,128)S(1)}, f32[512,512]{1,0:T(8,128)S(1)}) custom-call(f32[512,512]{1,0:T(8,128)S(1)} %get-tuple-element.140.refs_0_, f32[512,512]{1,0:T(8,128)S(1)} %get-tuple-element.141.refs_1_, f32[48,512]{1,0:T(8,128)S(1)} %get-tuple-element.142.refs_2_, f32[464,512]{1,0:T(8,128)} %get-tuple-element.143.refs_3_, ...), custom_call_target="tpu_custom_call" | custom-call | flops 1 | bytes 1 | tf_op jit(solution)/shard_map/cond/branch_1_fun/pallas_call | solution.py:103
  88.6 5.2 %collective-permute-done.6 = f32[2,128,512]{2,1,0:T(8,128)S(1)} collective-permute-done((f32[2,128,512]{2,1,0:T(8,128)S(1)}, f32[2,128,512]{2,1,0:T(8,128)S(1)}, u32[]{:S(2)}, u32[]{:S(2)}) %collective-permute-start.6) | collective-permute-done | bytes 524320 | tf_op jit(solution)/shard_map/cond/branch_1_fun/ppermute | solution.py:21
  93.8 1.2 %collective-permute-done.7 = f32[2,128,512]{2,1,0:T(8,128)S(1)} collective-permute-done((f32[2,128,512]{2,1,0:T(8,128)S(1)}, f32[2,128,512]{2,1,0:T(8,128)S(1)}, u32[]{:S(2)}, u32[]{:S(2)}) %collective-permute-start.7) | collective-permute-done | bytes 524320 | tf_op jit(solution)/shard_map/cond/branch_1_fun/ppermute | solution.py:21
  95.1 1.6 %collective-permute-start.8 = (f32[1,128,512]{2,1,0:T(8,128)S(1)}, f32[1,128,512]{2,1,0:T(8,128)S(1)}, u32[]{:S(2)}, u32[]{:S(2)}) collective-permute-start(f32[1,128,512]{2,1,0:T(8,128)S(1)} %get-tuple-element.164), channel_id=1, source_target_pairs={{0,16},{4,20},{8,24},{12,28},{16,0},{20,4},{24,8},{28,12},{1,17},{... | collective-permute-start | bytes 786440 | tf_op jit(solution)/shard_map/cond/branch_1_fun/ppermute | solution.py:21
  96.7 0.5 collective-permute-start.9
  97.2 5.1 %collective-permute-done.8 = f32[1,128,512]{2,1,0:T(8,128)S(1)} collective-permute-done((f32[1,128,512]{2,1,0:T(8,128)S(1)}, f32[1,128,512]{2,1,0:T(8,128)S(1)}, u32[]{:S(2)}, u32[]{:S(2)}) %collective-permute-start.8) | collective-permute-done | bytes 262176 | tf_op jit(solution)/shard_map/cond/branch_1_fun/ppermute | solution.py:21
  102.4 1.2 %collective-permute-done.9 = f32[1,128,512]{2,1,0:T(8,128)S(1)} collective-permute-done((f32[1,128,512]{2,1,0:T(8,128)S(1)}, f32[1,128,512]{2,1,0:T(8,128)S(1)}, u32[]{:S(2)}, u32[]{:S(2)}) %collective-permute-start.9) | collective-permute-done | bytes 262176 | tf_op jit(solution)/shard_map/cond/branch_1_fun/ppermute | solution.py:21
  103.8 1.9 %collective-permute-start.25 = (f32[96,512]{1,0:T(8,128)S(1)}, f32[96,512]{1,0:T(8,128)S(1)}, u32[]{:S(2)}, u32[]{:S(2)}) collective-permute-start(f32[96,512]{1,0:T(8,128)S(1)} %get-tuple-element.295), channel_id=1, source_target_pairs={{0,1},{1,0},{2,3},{3,2},{4,5},{5,4},{6,7},{7,6},{8,9},{9,8},{10,11... | collective-permute-start | bytes 589832 | tf_op jit(solution)/shard_map/ppermute | solution.py:21
  105.7 3.6 %collective-permute-done.23.late_ref = f32[464,512]{1,0:T(8,128)S(1)} collective-permute-done((f32[464,512]{1,0:T(8,128)}, f32[464,512]{1,0:T(8,128)S(1)}, u32[]{:S(2)}, u32[]{:S(2)}) %collective-permute-start.23) | collective-permute-done | bytes 950304 | tf_op jit(solution)/shard_map/ppermute | solution.py:21
  109.3 1.1 shard_map.105
  110.4 1.1 shard_map.106
  112.0 1.0 collective-permute-done.25.refs_3_
  113.0 1.4 %shard_map.107 = (f32[1,3,64,512]{3,2,1,0:T(8,128)}, f32[1,64,256]{2,1,0:T(8,128)}, f32[1,32,512]{2,1,0:T(8,128)}) custom-call(s32[1,2]{1,0:T(1,128)S(1)} %copy-done, f32[64,512]{1,0:T(8,128)S(1)} %copy-done.24, f32[128,512]{1,0:T(8,128)S(1)} %get-tuple-element.294.refs_2_, f32[96,512]{1,0:T(8,128)S(1)} %collective-permute-done.25.refs_3_, ...), custom_call_target="tpu_custom_call" | custom-call | flops 1 | bytes 1 | tf_op jit(solution)/shard_map/pallas_call | solution.py:103
  (101 shorter events, 4.7 us)
Async XLA Ops:
  0.6 12.4 %copy-start.1 = (f32[512,512]{1,0:T(8,128)S(1)}, f32[512,512]{1,0:T(8,128)}, u32[]{:S(2)}) copy-start(f32[512,512]{1,0:T(8,128)} %refs_0_.2) | copy-start | bytes 3145732
  2.7 16.6 %copy-start.27 = (f32[64,512]{1,0:T(8,128)S(1)}, f32[64,512]{1,0:T(8,128)}, u32[]{:S(2)}) copy-start(f32[64,512]{1,0:T(8,128)} %get-tuple-element.245) | copy-start | bytes 393220
  2.7 16.4 %collective-permute-start.10 = (f32[144,512]{1,0:T(8,128)}, f32[144,512]{1,0:T(8,128)S(1)}, u32[]{:S(2)}, u32[]{:S(2)}) collective-permute-start(f32[144,512]{1,0:T(8,128)} %get-tuple-element.239), channel_id=1, source_target_pairs={{0,1},{1,0},{2,3},{3,2},{4,5},{5,4},{6,7},{7,6},{8,9},{9,8},{10,11... | collective-permute-start | bytes 884744 | tf_op jit(solution)/shard_map/ppermute | solution.py:21
  5.7 10.1 %collective-permute-start.12 = (f32[80,512]{1,0:T(8,128)}, f32[80,512]{1,0:T(8,128)S(1)}, u32[]{:S(2)}, u32[]{:S(2)}) collective-permute-start(f32[80,512]{1,0:T(8,128)} %get-tuple-element.243), channel_id=1, source_target_pairs={{0,2},{1,3},{2,0},{3,1},{4,6},{5,7},{6,4},{7,5},{8,10},{9,11},{10,... | collective-permute-start | bytes 491528 | tf_op jit(solution)/shard_map/ppermute | solution.py:21
  8.3 11.1 %collective-permute-start.13 = (f32[128,512]{1,0:T(8,128)S(1)}, f32[128,512]{1,0:T(8,128)S(1)}, u32[]{:S(2)}, u32[]{:S(2)}) collective-permute-start(f32[128,512]{1,0:T(8,128)S(1)} %get-tuple-element.247), channel_id=1, source_target_pairs={{0,8},{4,12},{8,0},{12,4},{16,24},{20,28},{24,16},{28,20},{1,9},{5... | collective-permute-start | bytes 786440 | tf_op jit(solution)/shard_map/ppermute | solution.py:21
  9.8 12.8 %collective-permute-start.14 = (f32[128,512]{1,0:T(8,128)S(1)}, f32[128,512]{1,0:T(8,128)S(1)}, u32[]{:S(2)}, u32[]{:S(2)}) collective-permute-start(f32[128,512]{1,0:T(8,128)S(1)} %get-tuple-element.247), channel_id=1, source_target_pairs={{0,16},{4,20},{8,24},{12,28},{16,0},{20,4},{24,8},{28,12},{1,17},{... | collective-permute-start | bytes 786440 | tf_op jit(solution)/shard_map/ppermute | solution.py:21
  11.3 11.3 %collective-permute-start.15 = (f32[128,512]{1,0:T(8,128)S(1)}, f32[128,512]{1,0:T(8,128)S(1)}, u32[]{:S(2)}, u32[]{:S(2)}) collective-permute-start(f32[128,512]{1,0:T(8,128)S(1)} %get-tuple-element.247), channel_id=1, source_target_pairs={{0,24},{4,28},{8,16},{12,20},{16,8},{20,12},{24,0},{28,4},{1,25},{... | collective-permute-start | bytes 786440 | tf_op jit(solution)/shard_map/ppermute | solution.py:21
  13.0 20.4 %copy-start.3 = (f32[512,512]{1,0:T(8,128)S(1)}, f32[512,512]{1,0:T(8,128)}, u32[]{:S(2)}) copy-start(f32[512,512]{1,0:T(8,128)} %refs_1_.1) | copy-start | bytes 3145732
  15.8 44.8 %collective-permute-start.20 = (f32[464,512]{1,0:T(8,128)S(1)}, f32[464,512]{1,0:T(8,128)}, u32[]{:S(2)}, u32[]{:S(2)}) collective-permute-start(f32[464,512]{1,0:T(8,128)S(1)} %slice.113.x_ref), channel_id=1, source_target_pairs={{0,2},{1,3},{2,0},{3,1},{4,6},{5,7},{6,4},{7,5},{8,10},{9,11},{10,... | collective-permute-start | bytes 2850824 | tf_op jit(solution)/shard_map/ppermute | solution.py:21
  19.1 41.9 %collective-permute-start.11 = (f32[464,512]{1,0:T(8,128)S(1)}, f32[464,512]{1,0:T(8,128)}, u32[]{:S(2)}, u32[]{:S(2)}) collective-permute-start(f32[464,512]{1,0:T(8,128)S(1)} %slice.110.g_ref), channel_id=1, source_target_pairs={{0,1},{1,0},{2,3},{3,2},{4,5},{5,4},{6,7},{7,6},{8,9},{9,8},{10,11... | collective-permute-start | bytes 2850824 | tf_op jit(solution)/shard_map/ppermute | solution.py:21
  19.3 15.2 %copy-start = (s32[1,2]{1,0:T(1,128)S(1)}, s32[1,2]{1,0:T(1,128)}, u32[]{:S(2)}) copy-start(s32[1,2]{1,0:T(1,128)} %refs_0_.3) | copy-start | bytes 28
  22.7 5.7 %collective-permute-start.16 = (f32[1,96,512]{2,1,0:T(8,128)S(1)}, f32[1,96,512]{2,1,0:T(8,128)S(1)}, u32[]{:S(2)}, u32[]{:S(2)}) collective-permute-start(f32[1,96,512]{2,1,0:T(8,128)S(1)} %get-tuple-element.322), channel_id=1, source_target_pairs={{0,8},{4,12},{8,0},{12,4},{16,24},{20,28},{24,16},{28,20},{1,9},{5... | collective-permute-start | bytes 589832 | tf_op jit(solution)/shard_map/ppermute | solution.py:21
  24.0 5.7 %collective-permute-start.17 = (f32[1,96,512]{2,1,0:T(8,128)S(1)}, f32[1,96,512]{2,1,0:T(8,128)S(1)}, u32[]{:S(2)}, u32[]{:S(2)}) collective-permute-start(f32[1,96,512]{2,1,0:T(8,128)S(1)} %get-tuple-element.321), channel_id=1, source_target_pairs={{0,16},{4,20},{8,24},{12,28},{16,0},{20,4},{24,8},{28,12},{1,17},{... | collective-permute-start | bytes 589832 | tf_op jit(solution)/shard_map/ppermute | solution.py:21
  29.7 8.4 %collective-permute-start.18 = (f32[2,96,512]{2,1,0:T(8,128)S(1)}, f32[2,96,512]{2,1,0:T(8,128)S(1)}, u32[]{:S(2)}, u32[]{:S(2)}) collective-permute-start(f32[2,96,512]{2,1,0:T(8,128)S(1)} %pad_maximum_fusion.4), channel_id=1, source_target_pairs={{0,16},{4,20},{8,24},{12,28},{16,0},{20,4},{24,8},{28,12},{1,17},{... | collective-permute-start | bytes 1179656 | tf_op jit(solution)/shard_map/ppermute | solution.py:21
  30.8 8.4 %collective-permute-start.19 = (f32[2,96,512]{2,1,0:T(8,128)S(1)}, f32[2,96,512]{2,1,0:T(8,128)S(1)}, u32[]{:S(2)}, u32[]{:S(2)}) collective-permute-start(f32[2,96,512]{2,1,0:T(8,128)S(1)} %pad_maximum_fusion.5), channel_id=1, source_target_pairs={{0,8},{4,12},{8,0},{12,4},{16,24},{20,28},{24,16},{28,20},{1,9},{5... | collective-permute-start | bytes 1179656 | tf_op jit(solution)/shard_map/ppermute | solution.py:21
  34.6 4.6 %copy-start.19 = (f32[48,512]{1,0:T(8,128)}, f32[48,512]{1,0:T(8,128)S(1)}, u32[]{:S(2)}) copy-start(f32[48,512]{1,0:T(8,128)S(1)} %slice.117) | copy-start | bytes 294916
  34.6 4.5 %copy-start.21 = (f32[48,512]{1,0:T(8,128)}, f32[48,512]{1,0:T(8,128)S(1)}, u32[]{:S(2)}) copy-start(f32[48,512]{1,0:T(8,128)S(1)} %slice.111) | copy-start | bytes 294916
  39.7 5.7 %collective-permute-start.1 = (f32[4,320,512]{2,1,0:T(8,128)S(1)}, f32[4,320,512]{2,1,0:T(8,128)S(1)}, u32[]{:S(2)}, u32[]{:S(2)}) collective-permute-start(f32[4,320,512]{2,1,0:T(8,128)S(1)} %pad_maximum_fusion.refs_0_), channel_id=1, source_target_pairs={{0,4},{4,0},{8,12},{12,8},{16,20},{20,16},{24,28},{28,24},{1,5},{5... | collective-permute-start | bytes 7864328 | tf_op jit(solution)/shard_map/cond/branch_1_fun/ppermute | solution.py:21
  39.8 5.6 %collective-permute-start = (f32[4,64,512]{2,1,0:T(8,128)S(1)}, f32[4,64,512]{2,1,0:T(8,128)S(1)}, u32[]{:S(2)}, u32[]{:S(2)}) collective-permute-start(f32[4,64,512]{2,1,0:T(8,128)S(1)} %get-tuple-element.91), channel_id=1, source_target_pairs={{0,4},{4,0},{8,12},{12,8},{16,20},{20,16},{24,28},{28,24},{1,5},{5... | collective-permute-start | bytes 1572872 | tf_op jit(solution)/shard_map/cond/branch_1_fun/ppermute | solution.py:21
  45.5 7.3 %collective-permute-start.4 = (f32[64,512]{1,0:T(8,128)S(1)}, f32[64,512]{1,0:T(8,128)S(1)}, u32[]{:S(2)}, u32[]{:S(2)}) collective-permute-start(f32[64,512]{1,0:T(8,128)S(1)} %get-tuple-element.301), channel_id=1, source_target_pairs={{0,24},{4,28},{8,16},{12,20},{16,8},{20,12},{24,0},{28,4},{1,25},{... | collective-permute-start | bytes 393224 | tf_op jit(solution)/shard_map/cond/branch_1_fun/ppermute | solution.py:21
  47.0 7.8 %collective-permute-start.3 = (f32[64,512]{1,0:T(8,128)S(1)}, f32[64,512]{1,0:T(8,128)S(1)}, u32[]{:S(2)}, u32[]{:S(2)}) collective-permute-start(f32[64,512]{1,0:T(8,128)S(1)} %get-tuple-element.302), channel_id=1, source_target_pairs={{0,16},{4,20},{8,24},{12,28},{16,0},{20,4},{24,8},{28,12},{1,17},{... | collective-permute-start | bytes 393224 | tf_op jit(solution)/shard_map/cond/branch_1_fun/ppermute | solution.py:21
  49.0 5.8 %collective-permute-start.2 = (f32[64,512]{1,0:T(8,128)S(1)}, f32[64,512]{1,0:T(8,128)S(1)}, u32[]{:S(2)}, u32[]{:S(2)}) collective-permute-start(f32[64,512]{1,0:T(8,128)S(1)} %get-tuple-element.300), channel_id=1, source_target_pairs={{0,8},{4,12},{8,0},{12,4},{16,24},{20,28},{24,16},{28,20},{1,9},{5... | collective-permute-start | bytes 393224 | tf_op jit(solution)/shard_map/cond/branch_1_fun/ppermute | solution.py:21
  54.9 6.1 %copy-start.9 = (bf16[2,512,256]{2,1,0:T(8,128)(2,1)}, bf16[2,512,256]{2,1,0:T(8,128)(2,1)S(1)}, u32[]{:S(2)}) copy-start(bf16[2,512,256]{2,1,0:T(8,128)(2,1)S(1)} %get-tuple-element.263.ll) | copy-start | bytes 1572868
  54.9 6.0 %copy-start.11 = (bf16[2,256,512]{2,1,0:T(8,128)(2,1)}, bf16[2,256,512]{2,1,0:T(8,128)(2,1)S(1)}, u32[]{:S(2)}) copy-start(bf16[2,256,512]{2,1,0:T(8,128)(2,1)S(1)} %get-tuple-element.264.rh) | copy-start | bytes 1572868
  54.9 6.0 %copy-start.13 = (bf16[2,256,512]{2,1,0:T(8,128)(2,1)}, bf16[2,256,512]{2,1,0:T(8,128)(2,1)S(1)}, u32[]{:S(2)}) copy-start(bf16[2,256,512]{2,1,0:T(8,128)(2,1)S(1)} %get-tuple-element.265.rl) | copy-start | bytes 1572868
  54.9 10.5 %collective-permute-start.21 = (f32[48,512]{1,0:T(8,128)S(1)}, f32[48,512]{1,0:T(8,128)S(1)}, u32[]{:S(2)}, u32[]{:S(2)}) collective-permute-start(f32[48,512]{1,0:T(8,128)S(1)} %get-tuple-element.273), channel_id=1, source_target_pairs={{0,1},{1,0},{2,3},{3,2},{4,5},{5,4},{6,7},{7,6},{8,9},{9,8},{10,11... | collective-permute-start | bytes 294920 | tf_op jit(solution)/shard_map/ppermute | solution.py:21
  55.4 10.0 %collective-permute-start.22 = (f32[48,512]{1,0:T(8,128)S(1)}, f32[48,512]{1,0:T(8,128)S(1)}, u32[]{:S(2)}, u32[]{:S(2)}) collective-permute-start(f32[48,512]{1,0:T(8,128)S(1)} %get-tuple-element.274), channel_id=1, source_target_pairs={{0,2},{1,3},{2,0},{3,1},{4,6},{5,7},{6,4},{7,5},{8,10},{9,11},{10,... | collective-permute-start | bytes 294920 | tf_op jit(solution)/shard_map/ppermute | solution.py:21
  55.5 13.8 %copy-start.20 = (f32[48,512]{1,0:T(8,128)S(1)}, f32[48,512]{1,0:T(8,128)}, u32[]{:S(2)}) copy-start(f32[48,512]{1,0:T(8,128)} %copy-done.19) | copy-start | bytes 294916
  55.5 13.8 %copy-start.22 = (f32[48,512]{1,0:T(8,128)S(1)}, f32[48,512]{1,0:T(8,128)}, u32[]{:S(2)}) copy-start(f32[48,512]{1,0:T(8,128)} %copy-done.21) | copy-start | bytes 294916
  61.0 8.3 %copy-start.2 = (f32[512,512]{1,0:T(8,128)S(1)}, f32[512,512]{1,0:T(8,128)}, u32[]{:S(2)}) copy-start(f32[512,512]{1,0:T(8,128)} %refs_0_.2) | copy-start | bytes 3145732
  61.0 8.3 %copy-start.4 = (f32[512,512]{1,0:T(8,128)S(1)}, f32[512,512]{1,0:T(8,128)}, u32[]{:S(2)}) copy-start(f32[512,512]{1,0:T(8,128)} %refs_1_.1) | copy-start | bytes 3145732
  61.0 8.3 %copy-start.6 = (bf16[2,512,512]{2,1,0:T(8,128)(2,1)S(1)}, bf16[2,512,512]{2,1,0:T(8,128)(2,1)}, u32[]{:S(2)}) copy-start(bf16[2,512,512]{2,1,0:T(8,128)(2,1)} %copy-done.5) | copy-start | bytes 3145732
  61.0 8.3 %copy-start.8 = (bf16[2,512,512]{2,1,0:T(8,128)(2,1)S(1)}, bf16[2,512,512]{2,1,0:T(8,128)(2,1)}, u32[]{:S(2)}) copy-start(bf16[2,512,512]{2,1,0:T(8,128)(2,1)} %copy-done.7) | copy-start | bytes 3145732
  61.0 8.3 %copy-start.10 = (bf16[2,512,256]{2,1,0:T(8,128)(2,1)S(1)}, bf16[2,512,256]{2,1,0:T(8,128)(2,1)}, u32[]{:S(2)}) copy-start(bf16[2,512,256]{2,1,0:T(8,128)(2,1)} %copy-done.9) | copy-start | bytes 1572868
  61.0 8.3 %copy-start.12 = (bf16[2,256,512]{2,1,0:T(8,128)(2,1)S(1)}, bf16[2,256,512]{2,1,0:T(8,128)(2,1)}, u32[]{:S(2)}) copy-start(bf16[2,256,512]{2,1,0:T(8,128)(2,1)} %copy-done.11) | copy-start | bytes 1572868
  61.0 8.3 %copy-start.14 = (bf16[2,256,512]{2,1,0:T(8,128)(2,1)S(1)}, bf16[2,256,512]{2,1,0:T(8,128)(2,1)}, u32[]{:S(2)}) copy-start(bf16[2,256,512]{2,1,0:T(8,128)(2,1)} %copy-done.13) | copy-start | bytes 1572868
  61.0 8.3 %copy-start.16 = (bf16[1,512,512]{2,1,0:T(8,128)(2,1)S(1)}, bf16[1,512,512]{2,1,0:T(8,128)(2,1)}, u32[]{:S(2)}) copy-start(bf16[1,512,512]{2,1,0:T(8,128)(2,1)} %copy-done.15) | copy-start | bytes 1572868
  61.0 8.3 %copy-start.18 = (bf16[1,512,512]{2,1,0:T(8,128)(2,1)S(1)}, bf16[1,512,512]{2,1,0:T(8,128)(2,1)}, u32[]{:S(2)}) copy-start(bf16[1,512,512]{2,1,0:T(8,128)(2,1)} %copy-done.17) | copy-start | bytes 1572868
  65.4 43.9 %collective-permute-start.23 = (f32[464,512]{1,0:T(8,128)}, f32[464,512]{1,0:T(8,128)S(1)}, u32[]{:S(2)}, u32[]{:S(2)}) collective-permute-start(f32[464,512]{1,0:T(8,128)} %get-tuple-element.288), channel_id=1, source_target_pairs={{0,1},{1,0},{2,3},{3,2},{4,5},{5,4},{6,7},{7,6},{8,9},{9,8},{10,11... | collective-permute-start | bytes 2850824 | tf_op jit(solution)/shard_map/ppermute | solution.py:21
  68.1 42.3 %collective-permute-start.24 = (f32[464,512]{1,0:T(8,128)S(1)}, f32[464,512]{1,0:T(8,128)S(1)}, u32[]{:S(2)}, u32[]{:S(2)}) collective-permute-start(f32[464,512]{1,0:T(8,128)S(1)} %get-tuple-element.279), channel_id=1, source_target_pairs={{0,2},{1,3},{2,0},{3,1},{4,6},{5,7},{6,4},{7,5},{8,10},{9,11},{10,... | collective-permute-start | bytes 2850824 | tf_op jit(solution)/shard_map/ppermute | solution.py:21
  69.5 5.3 %copy-start.25 = (f32[48,256]{1,0:T(8,128)}, f32[48,256]{1,0:T(8,128)S(1)}, u32[]{:S(2)}) copy-start(f32[48,256]{1,0:T(8,128)S(1)} %get-tuple-element.146.refs_6_) | copy-start | bytes 147460 | tf_op jit(solution)/shard_map/cond
  74.9 4.2 %collective-permute-start.5 = (f32[4,256,512]{2,1,0:T(8,128)S(1)}, f32[4,256,512]{2,1,0:T(8,128)S(1)}, u32[]{:S(2)}, u32[]{:S(2)}) collective-permute-start(f32[4,256,512]{2,1,0:T(8,128)S(1)} %get-tuple-element.135), channel_id=1, source_target_pairs={{0,4},{4,0},{8,12},{12,8},{16,20},{20,16},{24,28},{28,24},{1,5},{5... | collective-permute-start | bytes 6291464 | tf_op jit(solution)/shard_map/cond/branch_1_fun/ppermute | solution.py:21
  79.8 14.0 %collective-permute-start.6 = (f32[2,128,512]{2,1,0:T(8,128)S(1)}, f32[2,128,512]{2,1,0:T(8,128)S(1)}, u32[]{:S(2)}, u32[]{:S(2)}) collective-permute-start(f32[2,128,512]{2,1,0:T(8,128)S(1)} %pad_maximum_fusion.1), channel_id=1, source_target_pairs={{0,8},{4,12},{8,0},{12,4},{16,24},{20,28},{24,16},{28,20},{1,9},{5... | collective-permute-start | bytes 1572872 | tf_op jit(solution)/shard_map/cond/branch_1_fun/ppermute | solution.py:21
  81.3 13.7 %collective-permute-start.7 = (f32[2,128,512]{2,1,0:T(8,128)S(1)}, f32[2,128,512]{2,1,0:T(8,128)S(1)}, u32[]{:S(2)}, u32[]{:S(2)}) collective-permute-start(f32[2,128,512]{2,1,0:T(8,128)S(1)} %pad_maximum_fusion.2), channel_id=1, source_target_pairs={{0,16},{4,20},{8,24},{12,28},{16,0},{20,4},{24,8},{28,12},{1,17},{... | collective-permute-start | bytes 1572872 | tf_op jit(solution)/shard_map/cond/branch_1_fun/ppermute | solution.py:21
  95.1 7.3 %collective-permute-start.8 = (f32[1,128,512]{2,1,0:T(8,128)S(1)}, f32[1,128,512]{2,1,0:T(8,128)S(1)}, u32[]{:S(2)}, u32[]{:S(2)}) collective-permute-start(f32[1,128,512]{2,1,0:T(8,128)S(1)} %get-tuple-element.164), channel_id=1, source_target_pairs={{0,16},{4,20},{8,24},{12,28},{16,0},{20,4},{24,8},{28,12},{1,17},{... | collective-permute-start | bytes 786440 | tf_op jit(solution)/shard_map/cond/branch_1_fun/ppermute | solution.py:21
  96.7 6.9 %collective-permute-start.9 = (f32[1,128,512]{2,1,0:T(8,128)S(1)}, f32[1,128,512]{2,1,0:T(8,128)S(1)}, u32[]{:S(2)}, u32[]{:S(2)}) collective-permute-start(f32[1,128,512]{2,1,0:T(8,128)S(1)} %get-tuple-element.165), channel_id=1, source_target_pairs={{0,8},{4,12},{8,0},{12,4},{16,24},{20,28},{24,16},{28,20},{1,9},{5... | collective-permute-start | bytes 786440 | tf_op jit(solution)/shard_map/cond/branch_1_fun/ppermute | solution.py:21
  103.8 9.2 %collective-permute-start.25 = (f32[96,512]{1,0:T(8,128)S(1)}, f32[96,512]{1,0:T(8,128)S(1)}, u32[]{:S(2)}, u32[]{:S(2)}) collective-permute-start(f32[96,512]{1,0:T(8,128)S(1)} %get-tuple-element.295), channel_id=1, source_target_pairs={{0,1},{1,0},{2,3},{3,2},{4,5},{5,4},{6,7},{7,6},{8,9},{9,8},{10,11... | collective-permute-start | bytes 589832 | tf_op jit(solution)/shard_map/ppermute | solution.py:21
  105.7 6.3 %collective-permute-start.26 = (f32[32,512]{1,0:T(8,128)S(1)}, f32[32,512]{1,0:T(8,128)S(1)}, u32[]{:S(2)}, u32[]{:S(2)}) collective-permute-start(f32[32,512]{1,0:T(8,128)S(1)} %get-tuple-element.296), channel_id=1, source_target_pairs={{0,2},{1,3},{2,0},{3,1},{4,6},{5,7},{6,4},{7,5},{8,10},{9,11},{10,... | collective-permute-start | bytes 196616 | tf_op jit(solution)/shard_map/ppermute | solution.py:21
  (7 other events, 22.2 us)

commit v5 on v4

--- a/solution.py
+++ b/solution.py
@@ -505,7 +505,7 @@
         )
         first = [across(part, "feat", 1 << b) for b, part in enumerate(sent[2:])]
         rest = list(late_sent[2:])
-        rest[0], first = lax.optimization_barrier((rest[0], first))
+        rest[1], first = lax.optimization_barrier((rest[1], first))
         first, late_sent = lax.optimization_barrier((first, late_sent))
         rest = [across(part, "feat", 1 << b) for b, part in enumerate(rest)]
         codes, code_grads = ([sent[i], late_sent[i]] for i in range(2))

time: 115 us -> 113 us (0.983)
  waiting for transfers between devices: 48.8 us -> 47.5 us
    ppermute x27, waiting for transfers between devices: 48.8 us -> 47.5 us  [across(): return lax.ppermute(block, axis, [(i, i ^ apart) for i in range(count)])]
  transfers between devices with their start and end apart: 27 -> 27, of which waited for: 19 -> 18; matrix products, arithmetic and copies ran while one was open for 3% -> 3% of each run, Pallas kernels for 21% -> 21%
where the time goes in v5:
time: 113 us
  waiting for transfers between devices  47.5 us (42%)
  starting transfers between devices  34 us (30%)
  Pallas kernels  27 us (24%)
  local copies, waits for them, and re-layouts  1.72 us (2%)
  other arithmetic  1.39 us (1%)
    ppermute x27, waiting for transfers between devices, across(): return lax.ppermute(block, axis, [(i, i ^ apart) for i in range(count)])  47.5 us
    ppermute x27, starting transfers between devices, across(): return lax.ppermute(block, axis, [(i, i ^ apart) for i in range(count)])  34 us
    pallas_call x10, Pallas kernels, call(): pl.pallas_call(kernel, out_shape=out_shapes, in_specs=in_specs, out_specs...  27 us
  transfers between devices with their start and end apart: 27, of which 18 were waited for; matrix products, arithmetic and copies ran while one was open for 3% of the time, Pallas kernels for 21%

profile of v5, /device:TPU:0, one launch (start us, length us, event | category | flops | bytes accessed | tf_op | source)
XLA Modules:
  0.0 113.0 jit_solution(6351437791530359850)
XLA Ops:
  0.6 2.0 %shard_map.101 = (f32[144,512]{1,0:T(8,128)}, f32[80,512]{1,0:T(8,128)}, f32[128,512]{1,0:T(8,128)S(1)}, f32[64,512]{1,0:T(8,128)}) custom-call(s32[1,2]{1,0:T(1,128)} %refs_0_.3, f32[1,3,64,512]{3,2,1,0:T(8,128)} %bitcast.83, f32[1,64,256]{2,1,0:T(8,128)} %left_ref.1, f32[1,32,512]{2,1,0:T(8,128)} %right_ref.1, f32[512,512]{1,0:T(8,128)} %refs_0_.2, ...), custom_call_target="tpu_custom_call" | custom-call | flops 1 | bytes 1 | tf_op jit(solution)/shard_map/pallas_call | solution.py:103
  2.7 3.0 %collective-permute-start.10 = (f32[144,512]{1,0:T(8,128)}, f32[144,512]{1,0:T(8,128)S(1)}, u32[]{:S(2)}, u32[]{:S(2)}) collective-permute-start(f32[144,512]{1,0:T(8,128)} %get-tuple-element.239), channel_id=1, source_target_pairs={{0,1},{1,0},{2,3},{3,2},{4,5},{5,4},{6,7},{7,6},{8,9},{9,8},{10,11... | collective-permute-start | bytes 884744 | tf_op jit(solution)/shard_map/ppermute | solution.py:21
  5.7 2.6 %collective-permute-start.12 = (f32[80,512]{1,0:T(8,128)}, f32[80,512]{1,0:T(8,128)S(1)}, u32[]{:S(2)}, u32[]{:S(2)}) collective-permute-start(f32[80,512]{1,0:T(8,128)} %get-tuple-element.243), channel_id=1, source_target_pairs={{0,2},{1,3},{2,0},{3,1},{4,6},{5,7},{6,4},{7,5},{8,10},{9,11},{10,... | collective-permute-start | bytes 491528 | tf_op jit(solution)/shard_map/ppermute | solution.py:21
  8.3 1.5 %collective-permute-start.13 = (f32[128,512]{1,0:T(8,128)S(1)}, f32[128,512]{1,0:T(8,128)S(1)}, u32[]{:S(2)}, u32[]{:S(2)}) collective-permute-start(f32[128,512]{1,0:T(8,128)S(1)} %get-tuple-element.247), channel_id=1, source_target_pairs={{0,8},{4,12},{8,0},{12,4},{16,24},{20,28},{24,16},{28,20},{1,9},{5... | collective-permute-start | bytes 786440 | tf_op jit(solution)/shard_map/ppermute | solution.py:21
  9.8 1.5 %collective-permute-start.14 = (f32[128,512]{1,0:T(8,128)S(1)}, f32[128,512]{1,0:T(8,128)S(1)}, u32[]{:S(2)}, u32[]{:S(2)}) collective-permute-start(f32[128,512]{1,0:T(8,128)S(1)} %get-tuple-element.247), channel_id=1, source_target_pairs={{0,16},{4,20},{8,24},{12,28},{16,0},{20,4},{24,8},{28,12},{1,17},{... | collective-permute-start | bytes 786440 | tf_op jit(solution)/shard_map/ppermute | solution.py:21
  11.8 1.3 %slice.110.g_ref = f32[464,512]{1,0:T(8,128)S(1)} slice(f32[512,512]{1,0:T(8,128)} %refs_1_.1), slice={[48:512], [0:512]} | slice | bytes 1900544 | tf_op jit(solution)/shard_map/slice | solution.py:428
  13.1 2.7 %collective-permute-done.12 = f32[80,512]{1,0:T(8,128)S(1)} collective-permute-done((f32[80,512]{1,0:T(8,128)}, f32[80,512]{1,0:T(8,128)S(1)}, u32[]{:S(2)}, u32[]{:S(2)}) %collective-permute-start.12) | collective-permute-done | bytes 163872 | tf_op jit(solution)/shard_map/ppermute | solution.py:21
  15.8 3.3 %collective-permute-start.20 = (f32[464,512]{1,0:T(8,128)S(1)}, f32[464,512]{1,0:T(8,128)}, u32[]{:S(2)}, u32[]{:S(2)}) collective-permute-start(f32[464,512]{1,0:T(8,128)S(1)} %slice.113.x_ref), channel_id=1, source_target_pairs={{0,2},{1,3},{2,0},{3,1},{4,6},{5,7},{6,4},{7,5},{8,10},{9,11},{10,... | collective-permute-start | bytes 2850824 | tf_op jit(solution)/shard_map/ppermute | solution.py:21
  19.4 3.2 %collective-permute-done.14 = f32[128,512]{1,0:T(8,128)S(1)} collective-permute-done((f32[128,512]{1,0:T(8,128)S(1)}, f32[128,512]{1,0:T(8,128)S(1)}, u32[]{:S(2)}, u32[]{:S(2)}) %collective-permute-start.14) | collective-permute-done | bytes 262176 | tf_op jit(solution)/shard_map/ppermute | solution.py:21
  22.7 1.3 %collective-permute-start.16 = (f32[1,96,512]{2,1,0:T(8,128)S(1)}, f32[1,96,512]{2,1,0:T(8,128)S(1)}, u32[]{:S(2)}, u32[]{:S(2)}) collective-permute-start(f32[1,96,512]{2,1,0:T(8,128)S(1)} %get-tuple-element.322), channel_id=1, source_target_pairs={{0,8},{4,12},{8,0},{12,4},{16,24},{20,28},{24,16},{28,20},{1,9},{5... | collective-permute-start | bytes 589832 | tf_op jit(solution)/shard_map/ppermute | solution.py:21
  24.0 0.8 collective-permute-start.17
  24.8 3.6 %collective-permute-done.16 = f32[1,96,512]{2,1,0:T(8,128)S(1)} collective-permute-done((f32[1,96,512]{2,1,0:T(8,128)S(1)}, f32[1,96,512]{2,1,0:T(8,128)S(1)}, u32[]{:S(2)}, u32[]{:S(2)}) %collective-permute-start.16) | collective-permute-done | bytes 196640 | tf_op jit(solution)/shard_map/ppermute | solution.py:21
  28.4 1.2 %collective-permute-done.17 = f32[1,96,512]{2,1,0:T(8,128)S(1)} collective-permute-done((f32[1,96,512]{2,1,0:T(8,128)S(1)}, f32[1,96,512]{2,1,0:T(8,128)S(1)}, u32[]{:S(2)}, u32[]{:S(2)}) %collective-permute-start.17) | collective-permute-done | bytes 196640 | tf_op jit(solution)/shard_map/ppermute | solution.py:21
  29.7 1.1 collective-permute-start.18
  30.8 2.6 %collective-permute-start.19 = (f32[2,96,512]{2,1,0:T(8,128)S(1)}, f32[2,96,512]{2,1,0:T(8,128)S(1)}, u32[]{:S(2)}, u32[]{:S(2)}) collective-permute-start(f32[2,96,512]{2,1,0:T(8,128)S(1)} %pad_maximum_fusion.5), channel_id=1, source_target_pairs={{0,8},{4,12},{8,0},{12,4},{16,24},{20,28},{24,16},{28,20},{1,9},{5... | collective-permute-start | bytes 1179656 | tf_op jit(solution)/shard_map/ppermute | solution.py:21
  33.4 1.1 shard_map.102
  34.6 3.5 %collective-permute-done.18 = f32[2,96,512]{2,1,0:T(8,128)S(1)} collective-permute-done((f32[2,96,512]{2,1,0:T(8,128)S(1)}, f32[2,96,512]{2,1,0:T(8,128)S(1)}, u32[]{:S(2)}, u32[]{:S(2)}) %collective-permute-start.18) | collective-permute-done | bytes 393248 | tf_op jit(solution)/shard_map/ppermute | solution.py:21
  38.1 1.1 collective-permute-done.19
  39.2 15.7 %conditional.2 = (f32[64,512]{1,0:T(8,128)S(1)}, bf16[1,512,512]{2,1,0:T(8,128)(2,1)S(1)}, bf16[1,512,512]{2,1,0:T(8,128)(2,1)S(1)}, bf16[2,512,512]{2,1,0:T(8,1...) conditional(s32[]{:T(128)} %bitcast.30, () %tuple.40, ...), branch_computations={%region_0.0_spmd, %region_1.0_spmd} | conditional | flops 3506177 | bytes 28180784 | solution.py:478
  40.3 5.1 %collective-permute-done = f32[4,64,512]{2,1,0:T(8,128)S(1)} collective-permute-done((f32[4,64,512]{2,1,0:T(8,128)S(1)}, f32[4,64,512]{2,1,0:T(8,128)S(1)}, u32[]{:S(2)}, u32[]{:S(2)}) %collective-permute-start) | collective-permute-done | bytes 524320 | tf_op jit(solution)/shard_map/cond/branch_1_fun/ppermute | solution.py:21
  45.5 1.5 %collective-permute-start.4 = (f32[64,512]{1,0:T(8,128)S(1)}, f32[64,512]{1,0:T(8,128)S(1)}, u32[]{:S(2)}, u32[]{:S(2)}) collective-permute-start(f32[64,512]{1,0:T(8,128)S(1)} %get-tuple-element.301), channel_id=1, source_target_pairs={{0,24},{4,28},{8,16},{12,20},{16,8},{20,12},{24,0},{28,4},{1,25},{... | collective-permute-start | bytes 393224 | tf_op jit(solution)/shard_map/cond/branch_1_fun/ppermute | solution.py:21
  47.0 2.0 %collective-permute-start.3 = (f32[64,512]{1,0:T(8,128)S(1)}, f32[64,512]{1,0:T(8,128)S(1)}, u32[]{:S(2)}, u32[]{:S(2)}) collective-permute-start(f32[64,512]{1,0:T(8,128)S(1)} %get-tuple-element.302), channel_id=1, source_target_pairs={{0,16},{4,20},{8,24},{12,28},{16,0},{20,4},{24,8},{28,12},{1,17},{... | collective-permute-start | bytes 393224 | tf_op jit(solution)/shard_map/cond/branch_1_fun/ppermute | solution.py:21
  49.0 2.5 %branch_1_fun.3 = (bf16[1,512,512]{2,1,0:T(8,128)(2,1)S(1)}, bf16[1,512,512]{2,1,0:T(8,128)(2,1)S(1)}, bf16[2,512,512]{2,1,0:T(8,128)(2,1)S(1)}, bf16[2,512,512]...) custom-call(f32[4,320,512]{2,1,0:T(8,128)S(1)} %pad_maximum_fusion.r, ...), custom_call_target="tpu_custom_call" | custom-call | flops 1 | bytes 1 | tf_op jit(solution)/shard_map/cond/branch_1_fun/pallas_call | solution.py:103
  51.5 1.3 %collective-permute-done.4 = f32[64,512]{1,0:T(8,128)S(1)} collective-permute-done((f32[64,512]{1,0:T(8,128)S(1)}, f32[64,512]{1,0:T(8,128)S(1)}, u32[]{:S(2)}, u32[]{:S(2)}) %collective-permute-start.4) | collective-permute-done | bytes 131104 | tf_op jit(solution)/shard_map/cond/branch_1_fun/ppermute | solution.py:21
  52.8 2.0 %collective-permute-done.3 = f32[64,512]{1,0:T(8,128)S(1)} collective-permute-done((f32[64,512]{1,0:T(8,128)S(1)}, f32[64,512]{1,0:T(8,128)S(1)}, u32[]{:S(2)}, u32[]{:S(2)}) %collective-permute-start.3) | collective-permute-done | bytes 131104 | tf_op jit(solution)/shard_map/cond/branch_1_fun/ppermute | solution.py:21
  55.5 2.4 %shard_map.103 = (f32[464,256]{1,0:T(8,128)S(1)}, f32[464,256]{1,0:T(8,128)S(1)}, f32[464,512]{1,0:T(8,128)S(1)}, f32[464,512]{1,0:T(8,128)S(1)}) custom-call(f32[464,512]{1,0:T(8,128)S(1)} %slice.113.x_ref, f32[464,512]{1,0:T(8,128)S(1)} %slice.110.g_ref, bf16[2,512,512]{2,1,0:T(8,128)(2,1)S(1)} %get-tuple-element.266.wh, ...), custom_call_target="tpu_custom_call" | custom-call | flops 1 | bytes 1 | tf_op jit(solution)/shard_map/pallas_call | solution.py:103
  57.9 2.6 %collective-permute-done.20.far_ref = f32[464,512]{1,0:T(8,128)} collective-permute-done((f32[464,512]{1,0:T(8,128)S(1)}, f32[464,512]{1,0:T(8,128)}, u32[]{:S(2)}, u32[]{:S(2)}) %collective-permute-start.20) | collective-permute-done | bytes 950304 | tf_op jit(solution)/shard_map/ppermute | solution.py:21
  61.0 4.4 %shard_map.104 = (f32[464,256]{1,0:T(8,128)S(1)}, f32[464,256]{1,0:T(8,128)S(1)}, f32[464,512]{1,0:T(8,128)}, f32[464,512]{1,0:T(8,128)S(1)}) custom-call(f32[464,512]{1,0:T(8,128)} %collective-permute-done.20.far_ref, f32[464,512]{1,0:T(8,128)} %collective-permute-done.11.near_ref, bf16[2,512,256]{2,1,0:T(8,128)(2,1)S(1)} %get-tuple-element.262.lh, ...), custom_call_target="tpu_custom_call" | custom-call | flops 1 | bytes 1 | tf_op jit(solution)/shard_map/pallas_call | solution.py:103
  65.4 2.6 %collective-permute-start.23 = (f32[464,512]{1,0:T(8,128)}, f32[464,512]{1,0:T(8,128)S(1)}, u32[]{:S(2)}, u32[]{:S(2)}) collective-permute-start(f32[464,512]{1,0:T(8,128)} %get-tuple-element.279), channel_id=1, source_target_pairs={{0,1},{1,0},{2,3},{3,2},{4,5},{5,4},{6,7},{7,6},{8,9},{9,8},{10,11... | collective-permute-start | bytes 2850824 | tf_op jit(solution)/shard_map/ppermute | solution.py:21
  68.0 1.2 %collective-permute-start.24 = (f32[464,512]{1,0:T(8,128)S(1)}, f32[464,512]{1,0:T(8,128)S(1)}, u32[]{:S(2)}, u32[]{:S(2)}) collective-permute-start(f32[464,512]{1,0:T(8,128)S(1)} %get-tuple-element.289), channel_id=1, source_target_pairs={{0,2},{1,3},{2,0},{3,1},{4,6},{5,7},{6,4},{7,5},{8,10},{9,11},{10,... | collective-permute-start | bytes 2850824 | tf_op jit(solution)/shard_map/ppermute | solution.py:21
  69.3 34.5 %conditional.3 = (f32[512,512]{1,0:T(8,128)S(1)}, f32[512,512]{1,0:T(8,128)S(1)}, f32[96,512]{1,0:T(8,128)S(1)}, f32[32,512]{1,0:T(8,128)S(1)}, f32[128,512]{1,0:T(8,128)S(1)}) conditional(s32[]{:T(128)} %bitcast.30, () %tuple.38, (f32[512,512]{1,0:T(8,128)S(1)}, f32[512,512]{1,0:T(8,128)S(1)}, f32[48,512]{1,0:T(8,128)S(1)}, f32[464,512]{1,0:T(8,128)}, ...), branch_computations={%region_2.0_spmd, %region_3.0_spmd} | conditional | flops 1179650 | bytes 29753642 | solution.py:567
  69.5 5.3 %branch_1_fun.4 = (f32[256,512]{1,0:T(8,128)S(1)}, f32[256,512]{1,0:T(8,128)S(1)}, f32[256,512]{1,0:T(8,128)S(1)}, f32[256,512]{1,0:T(8,128)S(1)}, f32[4,256,512]{2,1,0:T(8,128)S(1)}) custom-call(f32[512,512]{1,0:T(8,128)S(1)} %get-tuple-element.140.refs_0_, f32[512,512]{1,0:T(8,128)S(1)} %get-tuple-element.141.refs_1_, ...), custom_call_target="tpu_custom_call" | custom-call | flops 1 | bytes 1 | tf_op jit(solution)/shard_map/cond/branch_1_fun/pallas_call | solution.py:103
  74.9 4.1 %collective-permute-done.5 = f32[4,256,512]{2,1,0:T(8,128)S(1)} collective-permute-done((f32[4,256,512]{2,1,0:T(8,128)S(1)}, f32[4,256,512]{2,1,0:T(8,128)S(1)}, u32[]{:S(2)}, u32[]{:S(2)}) %collective-permute-start.5) | collective-permute-done | bytes 2097184 | tf_op jit(solution)/shard_map/cond/branch_1_fun/ppermute | solution.py:21
  79.7 1.6 %collective-permute-start.6 = (f32[2,128,512]{2,1,0:T(8,128)S(1)}, f32[2,128,512]{2,1,0:T(8,128)S(1)}, u32[]{:S(2)}, u32[]{:S(2)}) collective-permute-start(f32[2,128,512]{2,1,0:T(8,128)S(1)} %pad_maximum_fusion.1), channel_id=1, source_target_pairs={{0,8},{4,12},{8,0},{12,4},{16,24},{20,28},{24,16},{28,20},{1,9},{5... | collective-permute-start | bytes 1572872 | tf_op jit(solution)/shard_map/cond/branch_1_fun/ppermute | solution.py:21
  81.3 1.5 %collective-permute-start.7 = (f32[2,128,512]{2,1,0:T(8,128)S(1)}, f32[2,128,512]{2,1,0:T(8,128)S(1)}, u32[]{:S(2)}, u32[]{:S(2)}) collective-permute-start(f32[2,128,512]{2,1,0:T(8,128)S(1)} %pad_maximum_fusion.2), channel_id=1, source_target_pairs={{0,16},{4,20},{8,24},{12,28},{16,0},{20,4},{24,8},{28,12},{1,17},{... | collective-permute-start | bytes 1572872 | tf_op jit(solution)/shard_map/cond/branch_1_fun/ppermute | solution.py:21
  82.8 5.7 %branch_1_fun.5 = (f32[512,512]{1,0:T(8,128)S(1)}, f32[512,512]{1,0:T(8,128)S(1)}) custom-call(f32[512,512]{1,0:T(8,128)S(1)} %get-tuple-element.140.refs_0_, f32[512,512]{1,0:T(8,128)S(1)} %get-tuple-element.141.refs_1_, f32[48,512]{1,0:T(8,128)S(1)} %get-tuple-element.142.refs_2_, f32[464,512]{1,0:T(8,128)} %get-tuple-element.143.refs_3_, ...), custom_call_target="tpu_custom_call" | custom-call | flops 1 | bytes 1 | tf_op jit(solution)/shard_map/cond/branch_1_fun/pallas_call | solution.py:103
  88.5 5.2 %collective-permute-done.6 = f32[2,128,512]{2,1,0:T(8,128)S(1)} collective-permute-done((f32[2,128,512]{2,1,0:T(8,128)S(1)}, f32[2,128,512]{2,1,0:T(8,128)S(1)}, u32[]{:S(2)}, u32[]{:S(2)}) %collective-permute-start.6) | collective-permute-done | bytes 524320 | tf_op jit(solution)/shard_map/cond/branch_1_fun/ppermute | solution.py:21
  93.8 1.2 %collective-permute-done.7 = f32[2,128,512]{2,1,0:T(8,128)S(1)} collective-permute-done((f32[2,128,512]{2,1,0:T(8,128)S(1)}, f32[2,128,512]{2,1,0:T(8,128)S(1)}, u32[]{:S(2)}, u32[]{:S(2)}) %collective-permute-start.7) | collective-permute-done | bytes 524320 | tf_op jit(solution)/shard_map/cond/branch_1_fun/ppermute | solution.py:21
  95.1 1.6 %collective-permute-start.8 = (f32[1,128,512]{2,1,0:T(8,128)S(1)}, f32[1,128,512]{2,1,0:T(8,128)S(1)}, u32[]{:S(2)}, u32[]{:S(2)}) collective-permute-start(f32[1,128,512]{2,1,0:T(8,128)S(1)} %get-tuple-element.164), channel_id=1, source_target_pairs={{0,16},{4,20},{8,24},{12,28},{16,0},{20,4},{24,8},{28,12},{1,17},{... | collective-permute-start | bytes 786440 | tf_op jit(solution)/shard_map/cond/branch_1_fun/ppermute | solution.py:21
  96.6 0.5 collective-permute-start.9
  97.2 5.1 %collective-permute-done.8 = f32[1,128,512]{2,1,0:T(8,128)S(1)} collective-permute-done((f32[1,128,512]{2,1,0:T(8,128)S(1)}, f32[1,128,512]{2,1,0:T(8,128)S(1)}, u32[]{:S(2)}, u32[]{:S(2)}) %collective-permute-start.8) | collective-permute-done | bytes 262176 | tf_op jit(solution)/shard_map/cond/branch_1_fun/ppermute | solution.py:21
  102.3 1.2 %collective-permute-done.9 = f32[1,128,512]{2,1,0:T(8,128)S(1)} collective-permute-done((f32[1,128,512]{2,1,0:T(8,128)S(1)}, f32[1,128,512]{2,1,0:T(8,128)S(1)}, u32[]{:S(2)}, u32[]{:S(2)}) %collective-permute-start.9) | collective-permute-done | bytes 262176 | tf_op jit(solution)/shard_map/cond/branch_1_fun/ppermute | solution.py:21
  103.7 1.9 %collective-permute-start.25 = (f32[96,512]{1,0:T(8,128)S(1)}, f32[96,512]{1,0:T(8,128)S(1)}, u32[]{:S(2)}, u32[]{:S(2)}) collective-permute-start(f32[96,512]{1,0:T(8,128)S(1)} %get-tuple-element.295), channel_id=1, source_target_pairs={{0,1},{1,0},{2,3},{3,2},{4,5},{5,4},{6,7},{7,6},{8,9},{9,8},{10,11... | collective-permute-start | bytes 589832 | tf_op jit(solution)/shard_map/ppermute | solution.py:21
  105.7 2.7 %collective-permute-done.23.late_ref = f32[464,512]{1,0:T(8,128)S(1)} collective-permute-done((f32[464,512]{1,0:T(8,128)}, f32[464,512]{1,0:T(8,128)S(1)}, u32[]{:S(2)}, u32[]{:S(2)}) %collective-permute-start.23) | collective-permute-done | bytes 950304 | tf_op jit(solution)/shard_map/ppermute | solution.py:21
  108.4 1.1 shard_map.105
  109.5 1.1 shard_map.106
  110.7 1.0 collective-permute-done.26.refs_4_
  111.7 1.4 %shard_map.107 = (f32[1,3,64,512]{3,2,1,0:T(8,128)}, f32[1,64,256]{2,1,0:T(8,128)}, f32[1,32,512]{2,1,0:T(8,128)}) custom-call(s32[1,2]{1,0:T(1,128)S(1)} %copy-done, f32[64,512]{1,0:T(8,128)S(1)} %copy-done.24, f32[128,512]{1,0:T(8,128)S(1)} %get-tuple-element.294.refs_2_, f32[96,512]{1,0:T(8,128)S(1)} %collective-permute-done.25.refs_3_, ...), custom_call_target="tpu_custom_call" | custom-call | flops 1 | bytes 1 | tf_op jit(solution)/shard_map/pallas_call | solution.py:103
  (101 shorter events, 4.2 us)
Async XLA Ops:
  0.6 12.4 %copy-start.1 = (f32[512,512]{1,0:T(8,128)S(1)}, f32[512,512]{1,0:T(8,128)}, u32[]{:S(2)}) copy-start(f32[512,512]{1,0:T(8,128)} %refs_0_.2) | copy-start | bytes 3145732
  2.7 16.6 %copy-start.27 = (f32[64,512]{1,0:T(8,128)S(1)}, f32[64,512]{1,0:T(8,128)}, u32[]{:S(2)}) copy-start(f32[64,512]{1,0:T(8,128)} %get-tuple-element.245) | copy-start | bytes 393220
  2.7 16.4 %collective-permute-start.10 = (f32[144,512]{1,0:T(8,128)}, f32[144,512]{1,0:T(8,128)S(1)}, u32[]{:S(2)}, u32[]{:S(2)}) collective-permute-start(f32[144,512]{1,0:T(8,128)} %get-tuple-element.239), channel_id=1, source_target_pairs={{0,1},{1,0},{2,3},{3,2},{4,5},{5,4},{6,7},{7,6},{8,9},{9,8},{10,11... | collective-permute-start | bytes 884744 | tf_op jit(solution)/shard_map/ppermute | solution.py:21
  5.7 10.1 %collective-permute-start.12 = (f32[80,512]{1,0:T(8,128)}, f32[80,512]{1,0:T(8,128)S(1)}, u32[]{:S(2)}, u32[]{:S(2)}) collective-permute-start(f32[80,512]{1,0:T(8,128)} %get-tuple-element.243), channel_id=1, source_target_pairs={{0,2},{1,3},{2,0},{3,1},{4,6},{5,7},{6,4},{7,5},{8,10},{9,11},{10,... | collective-permute-start | bytes 491528 | tf_op jit(solution)/shard_map/ppermute | solution.py:21
  8.3 11.1 %collective-permute-start.13 = (f32[128,512]{1,0:T(8,128)S(1)}, f32[128,512]{1,0:T(8,128)S(1)}, u32[]{:S(2)}, u32[]{:S(2)}) collective-permute-start(f32[128,512]{1,0:T(8,128)S(1)} %get-tuple-element.247), channel_id=1, source_target_pairs={{0,8},{4,12},{8,0},{12,4},{16,24},{20,28},{24,16},{28,20},{1,9},{5... | collective-permute-start | bytes 786440 | tf_op jit(solution)/shard_map/ppermute | solution.py:21
  9.8 12.8 %collective-permute-start.14 = (f32[128,512]{1,0:T(8,128)S(1)}, f32[128,512]{1,0:T(8,128)S(1)}, u32[]{:S(2)}, u32[]{:S(2)}) collective-permute-start(f32[128,512]{1,0:T(8,128)S(1)} %get-tuple-element.247), channel_id=1, source_target_pairs={{0,16},{4,20},{8,24},{12,28},{16,0},{20,4},{24,8},{28,12},{1,17},{... | collective-permute-start | bytes 786440 | tf_op jit(solution)/shard_map/ppermute | solution.py:21
  11.3 11.3 %collective-permute-start.15 = (f32[128,512]{1,0:T(8,128)S(1)}, f32[128,512]{1,0:T(8,128)S(1)}, u32[]{:S(2)}, u32[]{:S(2)}) collective-permute-start(f32[128,512]{1,0:T(8,128)S(1)} %get-tuple-element.247), channel_id=1, source_target_pairs={{0,24},{4,28},{8,16},{12,20},{16,8},{20,12},{24,0},{28,4},{1,25},{... | collective-permute-start | bytes 786440 | tf_op jit(solution)/shard_map/ppermute | solution.py:21
  13.0 20.4 %copy-start.3 = (f32[512,512]{1,0:T(8,128)S(1)}, f32[512,512]{1,0:T(8,128)}, u32[]{:S(2)}) copy-start(f32[512,512]{1,0:T(8,128)} %refs_1_.1) | copy-start | bytes 3145732
  15.8 44.8 %collective-permute-start.20 = (f32[464,512]{1,0:T(8,128)S(1)}, f32[464,512]{1,0:T(8,128)}, u32[]{:S(2)}, u32[]{:S(2)}) collective-permute-start(f32[464,512]{1,0:T(8,128)S(1)} %slice.113.x_ref), channel_id=1, source_target_pairs={{0,2},{1,3},{2,0},{3,1},{4,6},{5,7},{6,4},{7,5},{8,10},{9,11},{10,... | collective-permute-start | bytes 2850824 | tf_op jit(solution)/shard_map/ppermute | solution.py:21
  19.1 41.9 %collective-permute-start.11 = (f32[464,512]{1,0:T(8,128)S(1)}, f32[464,512]{1,0:T(8,128)}, u32[]{:S(2)}, u32[]{:S(2)}) collective-permute-start(f32[464,512]{1,0:T(8,128)S(1)} %slice.110.g_ref), channel_id=1, source_target_pairs={{0,1},{1,0},{2,3},{3,2},{4,5},{5,4},{6,7},{7,6},{8,9},{9,8},{10,11... | collective-permute-start | bytes 2850824 | tf_op jit(solution)/shard_map/ppermute | solution.py:21
  19.3 15.2 %copy-start = (s32[1,2]{1,0:T(1,128)S(1)}, s32[1,2]{1,0:T(1,128)}, u32[]{:S(2)}) copy-start(s32[1,2]{1,0:T(1,128)} %refs_0_.3) | copy-start | bytes 28
  22.7 5.7 %collective-permute-start.16 = (f32[1,96,512]{2,1,0:T(8,128)S(1)}, f32[1,96,512]{2,1,0:T(8,128)S(1)}, u32[]{:S(2)}, u32[]{:S(2)}) collective-permute-start(f32[1,96,512]{2,1,0:T(8,128)S(1)} %get-tuple-element.322), channel_id=1, source_target_pairs={{0,8},{4,12},{8,0},{12,4},{16,24},{20,28},{24,16},{28,20},{1,9},{5... | collective-permute-start | bytes 589832 | tf_op jit(solution)/shard_map/ppermute | solution.py:21
  24.0 5.7 %collective-permute-start.17 = (f32[1,96,512]{2,1,0:T(8,128)S(1)}, f32[1,96,512]{2,1,0:T(8,128)S(1)}, u32[]{:S(2)}, u32[]{:S(2)}) collective-permute-start(f32[1,96,512]{2,1,0:T(8,128)S(1)} %get-tuple-element.321), channel_id=1, source_target_pairs={{0,16},{4,20},{8,24},{12,28},{16,0},{20,4},{24,8},{28,12},{1,17},{... | collective-permute-start | bytes 589832 | tf_op jit(solution)/shard_map/ppermute | solution.py:21
  29.7 8.4 %collective-permute-start.18 = (f32[2,96,512]{2,1,0:T(8,128)S(1)}, f32[2,96,512]{2,1,0:T(8,128)S(1)}, u32[]{:S(2)}, u32[]{:S(2)}) collective-permute-start(f32[2,96,512]{2,1,0:T(8,128)S(1)} %pad_maximum_fusion.4), channel_id=1, source_target_pairs={{0,16},{4,20},{8,24},{12,28},{16,0},{20,4},{24,8},{28,12},{1,17},{... | collective-permute-start | bytes 1179656 | tf_op jit(solution)/shard_map/ppermute | solution.py:21
  30.8 8.4 %collective-permute-start.19 = (f32[2,96,512]{2,1,0:T(8,128)S(1)}, f32[2,96,512]{2,1,0:T(8,128)S(1)}, u32[]{:S(2)}, u32[]{:S(2)}) collective-permute-start(f32[2,96,512]{2,1,0:T(8,128)S(1)} %pad_maximum_fusion.5), channel_id=1, source_target_pairs={{0,8},{4,12},{8,0},{12,4},{16,24},{20,28},{24,16},{28,20},{1,9},{5... | collective-permute-start | bytes 1179656 | tf_op jit(solution)/shard_map/ppermute | solution.py:21
  34.6 4.6 %copy-start.19 = (f32[48,512]{1,0:T(8,128)}, f32[48,512]{1,0:T(8,128)S(1)}, u32[]{:S(2)}) copy-start(f32[48,512]{1,0:T(8,128)S(1)} %slice.117) | copy-start | bytes 294916
  34.6 4.5 %copy-start.21 = (f32[48,512]{1,0:T(8,128)}, f32[48,512]{1,0:T(8,128)S(1)}, u32[]{:S(2)}) copy-start(f32[48,512]{1,0:T(8,128)S(1)} %slice.111) | copy-start | bytes 294916
  39.7 5.7 %collective-permute-start.1 = (f32[4,320,512]{2,1,0:T(8,128)S(1)}, f32[4,320,512]{2,1,0:T(8,128)S(1)}, u32[]{:S(2)}, u32[]{:S(2)}) collective-permute-start(f32[4,320,512]{2,1,0:T(8,128)S(1)} %pad_maximum_fusion.refs_0_), channel_id=1, source_target_pairs={{0,4},{4,0},{8,12},{12,8},{16,20},{20,16},{24,28},{28,24},{1,5},{5... | collective-permute-start | bytes 7864328 | tf_op jit(solution)/shard_map/cond/branch_1_fun/ppermute | solution.py:21
  39.8 5.6 %collective-permute-start = (f32[4,64,512]{2,1,0:T(8,128)S(1)}, f32[4,64,512]{2,1,0:T(8,128)S(1)}, u32[]{:S(2)}, u32[]{:S(2)}) collective-permute-start(f32[4,64,512]{2,1,0:T(8,128)S(1)} %get-tuple-element.91), channel_id=1, source_target_pairs={{0,4},{4,0},{8,12},{12,8},{16,20},{20,16},{24,28},{28,24},{1,5},{5... | collective-permute-start | bytes 1572872 | tf_op jit(solution)/shard_map/cond/branch_1_fun/ppermute | solution.py:21
  45.5 7.3 %collective-permute-start.4 = (f32[64,512]{1,0:T(8,128)S(1)}, f32[64,512]{1,0:T(8,128)S(1)}, u32[]{:S(2)}, u32[]{:S(2)}) collective-permute-start(f32[64,512]{1,0:T(8,128)S(1)} %get-tuple-element.301), channel_id=1, source_target_pairs={{0,24},{4,28},{8,16},{12,20},{16,8},{20,12},{24,0},{28,4},{1,25},{... | collective-permute-start | bytes 393224 | tf_op jit(solution)/shard_map/cond/branch_1_fun/ppermute | solution.py:21
  47.0 7.8 %collective-permute-start.3 = (f32[64,512]{1,0:T(8,128)S(1)}, f32[64,512]{1,0:T(8,128)S(1)}, u32[]{:S(2)}, u32[]{:S(2)}) collective-permute-start(f32[64,512]{1,0:T(8,128)S(1)} %get-tuple-element.302), channel_id=1, source_target_pairs={{0,16},{4,20},{8,24},{12,28},{16,0},{20,4},{24,8},{28,12},{1,17},{... | collective-permute-start | bytes 393224 | tf_op jit(solution)/shard_map/cond/branch_1_fun/ppermute | solution.py:21
  49.0 5.8 %collective-permute-start.2 = (f32[64,512]{1,0:T(8,128)S(1)}, f32[64,512]{1,0:T(8,128)S(1)}, u32[]{:S(2)}, u32[]{:S(2)}) collective-permute-start(f32[64,512]{1,0:T(8,128)S(1)} %get-tuple-element.300), channel_id=1, source_target_pairs={{0,8},{4,12},{8,0},{12,4},{16,24},{20,28},{24,16},{28,20},{1,9},{5... | collective-permute-start | bytes 393224 | tf_op jit(solution)/shard_map/cond/branch_1_fun/ppermute | solution.py:21
  54.9 6.1 %copy-start.9 = (bf16[2,512,256]{2,1,0:T(8,128)(2,1)}, bf16[2,512,256]{2,1,0:T(8,128)(2,1)S(1)}, u32[]{:S(2)}) copy-start(bf16[2,512,256]{2,1,0:T(8,128)(2,1)S(1)} %get-tuple-element.263.ll) | copy-start | bytes 1572868
  54.9 6.0 %copy-start.11 = (bf16[2,256,512]{2,1,0:T(8,128)(2,1)}, bf16[2,256,512]{2,1,0:T(8,128)(2,1)S(1)}, u32[]{:S(2)}) copy-start(bf16[2,256,512]{2,1,0:T(8,128)(2,1)S(1)} %get-tuple-element.264.rh) | copy-start | bytes 1572868
  54.9 6.0 %copy-start.13 = (bf16[2,256,512]{2,1,0:T(8,128)(2,1)}, bf16[2,256,512]{2,1,0:T(8,128)(2,1)S(1)}, u32[]{:S(2)}) copy-start(bf16[2,256,512]{2,1,0:T(8,128)(2,1)S(1)} %get-tuple-element.265.rl) | copy-start | bytes 1572868
  54.9 13.1 %collective-permute-start.21 = (f32[48,512]{1,0:T(8,128)S(1)}, f32[48,512]{1,0:T(8,128)S(1)}, u32[]{:S(2)}, u32[]{:S(2)}) collective-permute-start(f32[48,512]{1,0:T(8,128)S(1)} %get-tuple-element.273), channel_id=1, source_target_pairs={{0,1},{1,0},{2,3},{3,2},{4,5},{5,4},{6,7},{7,6},{8,9},{9,8},{10,11... | collective-permute-start | bytes 294920 | tf_op jit(solution)/shard_map/ppermute | solution.py:21
  55.4 12.6 %collective-permute-start.22 = (f32[48,512]{1,0:T(8,128)S(1)}, f32[48,512]{1,0:T(8,128)S(1)}, u32[]{:S(2)}, u32[]{:S(2)}) collective-permute-start(f32[48,512]{1,0:T(8,128)S(1)} %get-tuple-element.274), channel_id=1, source_target_pairs={{0,2},{1,3},{2,0},{3,1},{4,6},{5,7},{6,4},{7,5},{8,10},{9,11},{10,... | collective-permute-start | bytes 294920 | tf_op jit(solution)/shard_map/ppermute | solution.py:21
  55.5 13.7 %copy-start.20 = (f32[48,512]{1,0:T(8,128)S(1)}, f32[48,512]{1,0:T(8,128)}, u32[]{:S(2)}) copy-start(f32[48,512]{1,0:T(8,128)} %copy-done.19) | copy-start | bytes 294916
  55.5 13.7 %copy-start.22 = (f32[48,512]{1,0:T(8,128)S(1)}, f32[48,512]{1,0:T(8,128)}, u32[]{:S(2)}) copy-start(f32[48,512]{1,0:T(8,128)} %copy-done.21) | copy-start | bytes 294916
  61.0 8.3 %copy-start.2 = (f32[512,512]{1,0:T(8,128)S(1)}, f32[512,512]{1,0:T(8,128)}, u32[]{:S(2)}) copy-start(f32[512,512]{1,0:T(8,128)} %refs_0_.2) | copy-start | bytes 3145732
  61.0 8.3 %copy-start.4 = (f32[512,512]{1,0:T(8,128)S(1)}, f32[512,512]{1,0:T(8,128)}, u32[]{:S(2)}) copy-start(f32[512,512]{1,0:T(8,128)} %refs_1_.1) | copy-start | bytes 3145732
  61.0 8.2 %copy-start.6 = (bf16[2,512,512]{2,1,0:T(8,128)(2,1)S(1)}, bf16[2,512,512]{2,1,0:T(8,128)(2,1)}, u32[]{:S(2)}) copy-start(bf16[2,512,512]{2,1,0:T(8,128)(2,1)} %copy-done.5) | copy-start | bytes 3145732
  61.0 8.2 %copy-start.8 = (bf16[2,512,512]{2,1,0:T(8,128)(2,1)S(1)}, bf16[2,512,512]{2,1,0:T(8,128)(2,1)}, u32[]{:S(2)}) copy-start(bf16[2,512,512]{2,1,0:T(8,128)(2,1)} %copy-done.7) | copy-start | bytes 3145732
  61.0 8.2 %copy-start.10 = (bf16[2,512,256]{2,1,0:T(8,128)(2,1)S(1)}, bf16[2,512,256]{2,1,0:T(8,128)(2,1)}, u32[]{:S(2)}) copy-start(bf16[2,512,256]{2,1,0:T(8,128)(2,1)} %copy-done.9) | copy-start | bytes 1572868
  61.0 8.2 %copy-start.12 = (bf16[2,256,512]{2,1,0:T(8,128)(2,1)S(1)}, bf16[2,256,512]{2,1,0:T(8,128)(2,1)}, u32[]{:S(2)}) copy-start(bf16[2,256,512]{2,1,0:T(8,128)(2,1)} %copy-done.11) | copy-start | bytes 1572868
  61.0 8.2 %copy-start.14 = (bf16[2,256,512]{2,1,0:T(8,128)(2,1)S(1)}, bf16[2,256,512]{2,1,0:T(8,128)(2,1)}, u32[]{:S(2)}) copy-start(bf16[2,256,512]{2,1,0:T(8,128)(2,1)} %copy-done.13) | copy-start | bytes 1572868
  61.0 8.2 %copy-start.16 = (bf16[1,512,512]{2,1,0:T(8,128)(2,1)S(1)}, bf16[1,512,512]{2,1,0:T(8,128)(2,1)}, u32[]{:S(2)}) copy-start(bf16[1,512,512]{2,1,0:T(8,128)(2,1)} %copy-done.15) | copy-start | bytes 1572868
  61.0 8.2 %copy-start.18 = (bf16[1,512,512]{2,1,0:T(8,128)(2,1)S(1)}, bf16[1,512,512]{2,1,0:T(8,128)(2,1)}, u32[]{:S(2)}) copy-start(bf16[1,512,512]{2,1,0:T(8,128)(2,1)} %copy-done.17) | copy-start | bytes 1572868
  65.4 43.0 %collective-permute-start.23 = (f32[464,512]{1,0:T(8,128)}, f32[464,512]{1,0:T(8,128)S(1)}, u32[]{:S(2)}, u32[]{:S(2)}) collective-permute-start(f32[464,512]{1,0:T(8,128)} %get-tuple-element.279), channel_id=1, source_target_pairs={{0,1},{1,0},{2,3},{3,2},{4,5},{5,4},{6,7},{7,6},{8,9},{9,8},{10,11... | collective-permute-start | bytes 2850824 | tf_op jit(solution)/shard_map/ppermute | solution.py:21
  68.0 41.5 %collective-permute-start.24 = (f32[464,512]{1,0:T(8,128)S(1)}, f32[464,512]{1,0:T(8,128)S(1)}, u32[]{:S(2)}, u32[]{:S(2)}) collective-permute-start(f32[464,512]{1,0:T(8,128)S(1)} %get-tuple-element.289), channel_id=1, source_target_pairs={{0,2},{1,3},{2,0},{3,1},{4,6},{5,7},{6,4},{7,5},{8,10},{9,11},{10,... | collective-permute-start | bytes 2850824 | tf_op jit(solution)/shard_map/ppermute | solution.py:21
  69.5 5.3 %copy-start.25 = (f32[48,256]{1,0:T(8,128)}, f32[48,256]{1,0:T(8,128)S(1)}, u32[]{:S(2)}) copy-start(f32[48,256]{1,0:T(8,128)S(1)} %get-tuple-element.146.refs_6_) | copy-start | bytes 147460 | tf_op jit(solution)/shard_map/cond
  74.8 4.2 %collective-permute-start.5 = (f32[4,256,512]{2,1,0:T(8,128)S(1)}, f32[4,256,512]{2,1,0:T(8,128)S(1)}, u32[]{:S(2)}, u32[]{:S(2)}) collective-permute-start(f32[4,256,512]{2,1,0:T(8,128)S(1)} %get-tuple-element.135), channel_id=1, source_target_pairs={{0,4},{4,0},{8,12},{12,8},{16,20},{20,16},{24,28},{28,24},{1,5},{5... | collective-permute-start | bytes 6291464 | tf_op jit(solution)/shard_map/cond/branch_1_fun/ppermute | solution.py:21
  79.7 14.0 %collective-permute-start.6 = (f32[2,128,512]{2,1,0:T(8,128)S(1)}, f32[2,128,512]{2,1,0:T(8,128)S(1)}, u32[]{:S(2)}, u32[]{:S(2)}) collective-permute-start(f32[2,128,512]{2,1,0:T(8,128)S(1)} %pad_maximum_fusion.1), channel_id=1, source_target_pairs={{0,8},{4,12},{8,0},{12,4},{16,24},{20,28},{24,16},{28,20},{1,9},{5... | collective-permute-start | bytes 1572872 | tf_op jit(solution)/shard_map/cond/branch_1_fun/ppermute | solution.py:21
  81.3 13.7 %collective-permute-start.7 = (f32[2,128,512]{2,1,0:T(8,128)S(1)}, f32[2,128,512]{2,1,0:T(8,128)S(1)}, u32[]{:S(2)}, u32[]{:S(2)}) collective-permute-start(f32[2,128,512]{2,1,0:T(8,128)S(1)} %pad_maximum_fusion.2), channel_id=1, source_target_pairs={{0,16},{4,20},{8,24},{12,28},{16,0},{20,4},{24,8},{28,12},{1,17},{... | collective-permute-start | bytes 1572872 | tf_op jit(solution)/shard_map/cond/branch_1_fun/ppermute | solution.py:21
  95.1 7.3 %collective-permute-start.8 = (f32[1,128,512]{2,1,0:T(8,128)S(1)}, f32[1,128,512]{2,1,0:T(8,128)S(1)}, u32[]{:S(2)}, u32[]{:S(2)}) collective-permute-start(f32[1,128,512]{2,1,0:T(8,128)S(1)} %get-tuple-element.164), channel_id=1, source_target_pairs={{0,16},{4,20},{8,24},{12,28},{16,0},{20,4},{24,8},{28,12},{1,17},{... | collective-permute-start | bytes 786440 | tf_op jit(solution)/shard_map/cond/branch_1_fun/ppermute | solution.py:21
  96.6 6.9 %collective-permute-start.9 = (f32[1,128,512]{2,1,0:T(8,128)S(1)}, f32[1,128,512]{2,1,0:T(8,128)S(1)}, u32[]{:S(2)}, u32[]{:S(2)}) collective-permute-start(f32[1,128,512]{2,1,0:T(8,128)S(1)} %get-tuple-element.165), channel_id=1, source_target_pairs={{0,8},{4,12},{8,0},{12,4},{16,24},{20,28},{24,16},{28,20},{1,9},{5... | collective-permute-start | bytes 786440 | tf_op jit(solution)/shard_map/cond/branch_1_fun/ppermute | solution.py:21
  103.7 7.9 %collective-permute-start.25 = (f32[96,512]{1,0:T(8,128)S(1)}, f32[96,512]{1,0:T(8,128)S(1)}, u32[]{:S(2)}, u32[]{:S(2)}) collective-permute-start(f32[96,512]{1,0:T(8,128)S(1)} %get-tuple-element.295), channel_id=1, source_target_pairs={{0,1},{1,0},{2,3},{3,2},{4,5},{5,4},{6,7},{7,6},{8,9},{9,8},{10,11... | collective-permute-start | bytes 589832 | tf_op jit(solution)/shard_map/ppermute | solution.py:21
  105.7 6.0 %collective-permute-start.26 = (f32[32,512]{1,0:T(8,128)S(1)}, f32[32,512]{1,0:T(8,128)S(1)}, u32[]{:S(2)}, u32[]{:S(2)}) collective-permute-start(f32[32,512]{1,0:T(8,128)S(1)} %get-tuple-element.296), channel_id=1, source_target_pairs={{0,2},{1,3},{2,0},{3,1},{4,6},{5,7},{6,4},{7,5},{8,10},{9,11},{10,... | collective-permute-start | bytes 196616 | tf_op jit(solution)/shard_map/ppermute | solution.py:21
  (7 other events, 21.8 us)

commit v6 on v5

--- a/solution.py
+++ b/solution.py
@@ -583,7 +583,9 @@
         functools.partial(place_kernel, sizes),
         [f32(*by_slot.shape), f32(*low_left.shape), f32(*low_right.shape)],
         [partner_bits, self_grads, kept, near_back, far_back],
-        in_specs=[smem] + [vmem] * 4,
+        grid=(1,),
+        in_specs=[smem] + [whole(p.shape) for p in (self_grads, kept, near_back, far_back)],
+        out_specs=[whole(by_slot.shape), whole(low_left.shape), whole(low_right.shape)],
     )
     block_grads = jnp.transpose(block_grads, (0, 2, 1, 3))
     return (outputs, grad, block_grads, left_grads, right_grads)

time: 113 us -> 113 us (level)
  no operation moved by 1% of the time
where the time goes in v6:
time: 113 us
  waiting for transfers between devices  47.5 us (42%)
  starting transfers between devices  34 us (30%)
  Pallas kernels  27 us (24%)
  local copies, waits for them, and re-layouts  1.72 us (2%)
  other arithmetic  1.39 us (1%)
    ppermute x27, waiting for transfers between devices, across(): return lax.ppermute(block, axis, [(i, i ^ apart) for i in range(count)])  47.5 us
    ppermute x27, starting transfers between devices, across(): return lax.ppermute(block, axis, [(i, i ^ apart) for i in range(count)])  34 us
    pallas_call x10, Pallas kernels, call(): pl.pallas_call(kernel, out_shape=out_shapes, in_specs=in_specs, out_specs...  27 us
  transfers between devices with their start and end apart: 27, of which 18 were waited for; matrix products, arithmetic and copies ran while one was open for 3% of the time, Pallas kernels for 21%

profile of v6, /device:TPU:0, one launch (start us, length us, event | category | flops | bytes accessed | tf_op | source)
XLA Modules:
  0.0 113.0 jit_solution(6351437791530359850)
XLA Ops:
  0.6 2.0 %shard_map.101 = (f32[144,512]{1,0:T(8,128)}, f32[80,512]{1,0:T(8,128)}, f32[128,512]{1,0:T(8,128)S(1)}, f32[64,512]{1,0:T(8,128)}) custom-call(s32[1,2]{1,0:T(1,128)} %refs_0_.3, f32[1,3,64,512]{3,2,1,0:T(8,128)} %bitcast.83, f32[1,64,256]{2,1,0:T(8,128)} %left_ref.1, f32[1,32,512]{2,1,0:T(8,128)} %right_ref.1, f32[512,512]{1,0:T(8,128)} %refs_0_.2, ...), custom_call_target="tpu_custom_call" | custom-call | flops 1 | bytes 1 | tf_op jit(solution)/shard_map/pallas_call | solution.py:103
  2.7 3.0 %collective-permute-start.10 = (f32[144,512]{1,0:T(8,128)}, f32[144,512]{1,0:T(8,128)S(1)}, u32[]{:S(2)}, u32[]{:S(2)}) collective-permute-start(f32[144,512]{1,0:T(8,128)} %get-tuple-element.239), channel_id=1, source_target_pairs={{0,1},{1,0},{2,3},{3,2},{4,5},{5,4},{6,7},{7,6},{8,9},{9,8},{10,11... | collective-permute-start | bytes 884744 | tf_op jit(solution)/shard_map/ppermute | solution.py:21
  5.7 2.6 %collective-permute-start.12 = (f32[80,512]{1,0:T(8,128)}, f32[80,512]{1,0:T(8,128)S(1)}, u32[]{:S(2)}, u32[]{:S(2)}) collective-permute-start(f32[80,512]{1,0:T(8,128)} %get-tuple-element.243), channel_id=1, source_target_pairs={{0,2},{1,3},{2,0},{3,1},{4,6},{5,7},{6,4},{7,5},{8,10},{9,11},{10,... | collective-permute-start | bytes 491528 | tf_op jit(solution)/shard_map/ppermute | solution.py:21
  8.3 1.5 %collective-permute-start.13 = (f32[128,512]{1,0:T(8,128)S(1)}, f32[128,512]{1,0:T(8,128)S(1)}, u32[]{:S(2)}, u32[]{:S(2)}) collective-permute-start(f32[128,512]{1,0:T(8,128)S(1)} %get-tuple-element.247), channel_id=1, source_target_pairs={{0,8},{4,12},{8,0},{12,4},{16,24},{20,28},{24,16},{28,20},{1,9},{5... | collective-permute-start | bytes 786440 | tf_op jit(solution)/shard_map/ppermute | solution.py:21
  9.8 1.5 %collective-permute-start.14 = (f32[128,512]{1,0:T(8,128)S(1)}, f32[128,512]{1,0:T(8,128)S(1)}, u32[]{:S(2)}, u32[]{:S(2)}) collective-permute-start(f32[128,512]{1,0:T(8,128)S(1)} %get-tuple-element.247), channel_id=1, source_target_pairs={{0,16},{4,20},{8,24},{12,28},{16,0},{20,4},{24,8},{28,12},{1,17},{... | collective-permute-start | bytes 786440 | tf_op jit(solution)/shard_map/ppermute | solution.py:21
  11.8 1.3 %slice.110.g_ref = f32[464,512]{1,0:T(8,128)S(1)} slice(f32[512,512]{1,0:T(8,128)} %refs_1_.1), slice={[48:512], [0:512]} | slice | bytes 1900544 | tf_op jit(solution)/shard_map/slice | solution.py:428
  13.1 2.7 %collective-permute-done.12 = f32[80,512]{1,0:T(8,128)S(1)} collective-permute-done((f32[80,512]{1,0:T(8,128)}, f32[80,512]{1,0:T(8,128)S(1)}, u32[]{:S(2)}, u32[]{:S(2)}) %collective-permute-start.12) | collective-permute-done | bytes 163872 | tf_op jit(solution)/shard_map/ppermute | solution.py:21
  15.8 3.3 %collective-permute-start.20 = (f32[464,512]{1,0:T(8,128)S(1)}, f32[464,512]{1,0:T(8,128)}, u32[]{:S(2)}, u32[]{:S(2)}) collective-permute-start(f32[464,512]{1,0:T(8,128)S(1)} %slice.113.x_ref), channel_id=1, source_target_pairs={{0,2},{1,3},{2,0},{3,1},{4,6},{5,7},{6,4},{7,5},{8,10},{9,11},{10,... | collective-permute-start | bytes 2850824 | tf_op jit(solution)/shard_map/ppermute | solution.py:21
  19.4 3.2 %collective-permute-done.14 = f32[128,512]{1,0:T(8,128)S(1)} collective-permute-done((f32[128,512]{1,0:T(8,128)S(1)}, f32[128,512]{1,0:T(8,128)S(1)}, u32[]{:S(2)}, u32[]{:S(2)}) %collective-permute-start.14) | collective-permute-done | bytes 262176 | tf_op jit(solution)/shard_map/ppermute | solution.py:21
  22.7 1.3 %collective-permute-start.16 = (f32[1,96,512]{2,1,0:T(8,128)S(1)}, f32[1,96,512]{2,1,0:T(8,128)S(1)}, u32[]{:S(2)}, u32[]{:S(2)}) collective-permute-start(f32[1,96,512]{2,1,0:T(8,128)S(1)} %get-tuple-element.322), channel_id=1, source_target_pairs={{0,8},{4,12},{8,0},{12,4},{16,24},{20,28},{24,16},{28,20},{1,9},{5... | collective-permute-start | bytes 589832 | tf_op jit(solution)/shard_map/ppermute | solution.py:21
  24.0 0.8 collective-permute-start.17
  24.8 3.6 %collective-permute-done.16 = f32[1,96,512]{2,1,0:T(8,128)S(1)} collective-permute-done((f32[1,96,512]{2,1,0:T(8,128)S(1)}, f32[1,96,512]{2,1,0:T(8,128)S(1)}, u32[]{:S(2)}, u32[]{:S(2)}) %collective-permute-start.16) | collective-permute-done | bytes 196640 | tf_op jit(solution)/shard_map/ppermute | solution.py:21
  28.4 1.2 %collective-permute-done.17 = f32[1,96,512]{2,1,0:T(8,128)S(1)} collective-permute-done((f32[1,96,512]{2,1,0:T(8,128)S(1)}, f32[1,96,512]{2,1,0:T(8,128)S(1)}, u32[]{:S(2)}, u32[]{:S(2)}) %collective-permute-start.17) | collective-permute-done | bytes 196640 | tf_op jit(solution)/shard_map/ppermute | solution.py:21
  29.7 1.1 collective-permute-start.18
  30.8 2.6 %collective-permute-start.19 = (f32[2,96,512]{2,1,0:T(8,128)S(1)}, f32[2,96,512]{2,1,0:T(8,128)S(1)}, u32[]{:S(2)}, u32[]{:S(2)}) collective-permute-start(f32[2,96,512]{2,1,0:T(8,128)S(1)} %pad_maximum_fusion.5), channel_id=1, source_target_pairs={{0,8},{4,12},{8,0},{12,4},{16,24},{20,28},{24,16},{28,20},{1,9},{5... | collective-permute-start | bytes 1179656 | tf_op jit(solution)/shard_map/ppermute | solution.py:21
  33.4 1.1 shard_map.102
  34.6 3.5 %collective-permute-done.18 = f32[2,96,512]{2,1,0:T(8,128)S(1)} collective-permute-done((f32[2,96,512]{2,1,0:T(8,128)S(1)}, f32[2,96,512]{2,1,0:T(8,128)S(1)}, u32[]{:S(2)}, u32[]{:S(2)}) %collective-permute-start.18) | collective-permute-done | bytes 393248 | tf_op jit(solution)/shard_map/ppermute | solution.py:21
  38.1 1.1 collective-permute-done.19
  39.2 15.7 %conditional.2 = (f32[64,512]{1,0:T(8,128)S(1)}, bf16[1,512,512]{2,1,0:T(8,128)(2,1)S(1)}, bf16[1,512,512]{2,1,0:T(8,128)(2,1)S(1)}, bf16[2,512,512]{2,1,0:T(8,1...) conditional(s32[]{:T(128)} %bitcast.30, () %tuple.40, ...), branch_computations={%region_0.0_spmd, %region_1.0_spmd} | conditional | flops 3506177 | bytes 28180784 | solution.py:478
  40.3 5.1 %collective-permute-done = f32[4,64,512]{2,1,0:T(8,128)S(1)} collective-permute-done((f32[4,64,512]{2,1,0:T(8,128)S(1)}, f32[4,64,512]{2,1,0:T(8,128)S(1)}, u32[]{:S(2)}, u32[]{:S(2)}) %collective-permute-start) | collective-permute-done | bytes 524320 | tf_op jit(solution)/shard_map/cond/branch_1_fun/ppermute | solution.py:21
  45.5 1.5 %collective-permute-start.4 = (f32[64,512]{1,0:T(8,128)S(1)}, f32[64,512]{1,0:T(8,128)S(1)}, u32[]{:S(2)}, u32[]{:S(2)}) collective-permute-start(f32[64,512]{1,0:T(8,128)S(1)} %get-tuple-element.301), channel_id=1, source_target_pairs={{0,24},{4,28},{8,16},{12,20},{16,8},{20,12},{24,0},{28,4},{1,25},{... | collective-permute-start | bytes 393224 | tf_op jit(solution)/shard_map/cond/branch_1_fun/ppermute | solution.py:21
  47.0 2.0 %collective-permute-start.3 = (f32[64,512]{1,0:T(8,128)S(1)}, f32[64,512]{1,0:T(8,128)S(1)}, u32[]{:S(2)}, u32[]{:S(2)}) collective-permute-start(f32[64,512]{1,0:T(8,128)S(1)} %get-tuple-element.302), channel_id=1, source_target_pairs={{0,16},{4,20},{8,24},{12,28},{16,0},{20,4},{24,8},{28,12},{1,17},{... | collective-permute-start | bytes 393224 | tf_op jit(solution)/shard_map/cond/branch_1_fun/ppermute | solution.py:21
  49.0 2.5 %branch_1_fun.3 = (bf16[1,512,512]{2,1,0:T(8,128)(2,1)S(1)}, bf16[1,512,512]{2,1,0:T(8,128)(2,1)S(1)}, bf16[2,512,512]{2,1,0:T(8,128)(2,1)S(1)}, bf16[2,512,512]...) custom-call(f32[4,320,512]{2,1,0:T(8,128)S(1)} %pad_maximum_fusion.r, ...), custom_call_target="tpu_custom_call" | custom-call | flops 1 | bytes 1 | tf_op jit(solution)/shard_map/cond/branch_1_fun/pallas_call | solution.py:103
  51.5 1.3 %collective-permute-done.4 = f32[64,512]{1,0:T(8,128)S(1)} collective-permute-done((f32[64,512]{1,0:T(8,128)S(1)}, f32[64,512]{1,0:T(8,128)S(1)}, u32[]{:S(2)}, u32[]{:S(2)}) %collective-permute-start.4) | collective-permute-done | bytes 131104 | tf_op jit(solution)/shard_map/cond/branch_1_fun/ppermute | solution.py:21
  52.8 2.0 %collective-permute-done.3 = f32[64,512]{1,0:T(8,128)S(1)} collective-permute-done((f32[64,512]{1,0:T(8,128)S(1)}, f32[64,512]{1,0:T(8,128)S(1)}, u32[]{:S(2)}, u32[]{:S(2)}) %collective-permute-start.3) | collective-permute-done | bytes 131104 | tf_op jit(solution)/shard_map/cond/branch_1_fun/ppermute | solution.py:21
  55.5 2.4 %shard_map.103 = (f32[464,256]{1,0:T(8,128)S(1)}, f32[464,256]{1,0:T(8,128)S(1)}, f32[464,512]{1,0:T(8,128)S(1)}, f32[464,512]{1,0:T(8,128)S(1)}) custom-call(f32[464,512]{1,0:T(8,128)S(1)} %slice.113.x_ref, f32[464,512]{1,0:T(8,128)S(1)} %slice.110.g_ref, bf16[2,512,512]{2,1,0:T(8,128)(2,1)S(1)} %get-tuple-element.266.wh, ...), custom_call_target="tpu_custom_call" | custom-call | flops 1 | bytes 1 | tf_op jit(solution)/shard_map/pallas_call | solution.py:103
  57.9 2.6 %collective-permute-done.20.far_ref = f32[464,512]{1,0:T(8,128)} collective-permute-done((f32[464,512]{1,0:T(8,128)S(1)}, f32[464,512]{1,0:T(8,128)}, u32[]{:S(2)}, u32[]{:S(2)}) %collective-permute-start.20) | collective-permute-done | bytes 950304 | tf_op jit(solution)/shard_map/ppermute | solution.py:21
  61.0 4.4 %shard_map.104 = (f32[464,256]{1,0:T(8,128)S(1)}, f32[464,256]{1,0:T(8,128)S(1)}, f32[464,512]{1,0:T(8,128)}, f32[464,512]{1,0:T(8,128)S(1)}) custom-call(f32[464,512]{1,0:T(8,128)} %collective-permute-done.20.far_ref, f32[464,512]{1,0:T(8,128)} %collective-permute-done.11.near_ref, bf16[2,512,256]{2,1,0:T(8,128)(2,1)S(1)} %get-tuple-element.262.lh, ...), custom_call_target="tpu_custom_call" | custom-call | flops 1 | bytes 1 | tf_op jit(solution)/shard_map/pallas_call | solution.py:103
  65.4 2.6 %collective-permute-start.23 = (f32[464,512]{1,0:T(8,128)}, f32[464,512]{1,0:T(8,128)S(1)}, u32[]{:S(2)}, u32[]{:S(2)}) collective-permute-start(f32[464,512]{1,0:T(8,128)} %get-tuple-element.279), channel_id=1, source_target_pairs={{0,1},{1,0},{2,3},{3,2},{4,5},{5,4},{6,7},{7,6},{8,9},{9,8},{10,11... | collective-permute-start | bytes 2850824 | tf_op jit(solution)/shard_map/ppermute | solution.py:21
  68.0 1.2 %collective-permute-start.24 = (f32[464,512]{1,0:T(8,128)S(1)}, f32[464,512]{1,0:T(8,128)S(1)}, u32[]{:S(2)}, u32[]{:S(2)}) collective-permute-start(f32[464,512]{1,0:T(8,128)S(1)} %get-tuple-element.289), channel_id=1, source_target_pairs={{0,2},{1,3},{2,0},{3,1},{4,6},{5,7},{6,4},{7,5},{8,10},{9,11},{10,... | collective-permute-start | bytes 2850824 | tf_op jit(solution)/shard_map/ppermute | solution.py:21
  69.3 34.5 %conditional.3 = (f32[512,512]{1,0:T(8,128)S(1)}, f32[512,512]{1,0:T(8,128)S(1)}, f32[96,512]{1,0:T(8,128)S(1)}, f32[32,512]{1,0:T(8,128)S(1)}, f32[128,512]{1,0:T(8,128)S(1)}) conditional(s32[]{:T(128)} %bitcast.30, () %tuple.38, (f32[512,512]{1,0:T(8,128)S(1)}, f32[512,512]{1,0:T(8,128)S(1)}, f32[48,512]{1,0:T(8,128)S(1)}, f32[464,512]{1,0:T(8,128)}, ...), branch_computations={%region_2.0_spmd, %region_3.0_spmd} | conditional | flops 1179650 | bytes 29753642 | solution.py:567
  69.5 5.3 %branch_1_fun.4 = (f32[256,512]{1,0:T(8,128)S(1)}, f32[256,512]{1,0:T(8,128)S(1)}, f32[256,512]{1,0:T(8,128)S(1)}, f32[256,512]{1,0:T(8,128)S(1)}, f32[4,256,512]{2,1,0:T(8,128)S(1)}) custom-call(f32[512,512]{1,0:T(8,128)S(1)} %get-tuple-element.140.refs_0_, f32[512,512]{1,0:T(8,128)S(1)} %get-tuple-element.141.refs_1_, ...), custom_call_target="tpu_custom_call" | custom-call | flops 1 | bytes 1 | tf_op jit(solution)/shard_map/cond/branch_1_fun/pallas_call | solution.py:103
  74.9 4.1 %collective-permute-done.5 = f32[4,256,512]{2,1,0:T(8,128)S(1)} collective-permute-done((f32[4,256,512]{2,1,0:T(8,128)S(1)}, f32[4,256,512]{2,1,0:T(8,128)S(1)}, u32[]{:S(2)}, u32[]{:S(2)}) %collective-permute-start.5) | collective-permute-done | bytes 2097184 | tf_op jit(solution)/shard_map/cond/branch_1_fun/ppermute | solution.py:21
  79.7 1.6 %collective-permute-start.6 = (f32[2,128,512]{2,1,0:T(8,128)S(1)}, f32[2,128,512]{2,1,0:T(8,128)S(1)}, u32[]{:S(2)}, u32[]{:S(2)}) collective-permute-start(f32[2,128,512]{2,1,0:T(8,128)S(1)} %pad_maximum_fusion.1), channel_id=1, source_target_pairs={{0,8},{4,12},{8,0},{12,4},{16,24},{20,28},{24,16},{28,20},{1,9},{5... | collective-permute-start | bytes 1572872 | tf_op jit(solution)/shard_map/cond/branch_1_fun/ppermute | solution.py:21
  81.3 1.5 %collective-permute-start.7 = (f32[2,128,512]{2,1,0:T(8,128)S(1)}, f32[2,128,512]{2,1,0:T(8,128)S(1)}, u32[]{:S(2)}, u32[]{:S(2)}) collective-permute-start(f32[2,128,512]{2,1,0:T(8,128)S(1)} %pad_maximum_fusion.2), channel_id=1, source_target_pairs={{0,16},{4,20},{8,24},{12,28},{16,0},{20,4},{24,8},{28,12},{1,17},{... | collective-permute-start | bytes 1572872 | tf_op jit(solution)/shard_map/cond/branch_1_fun/ppermute | solution.py:21
  82.8 5.7 %branch_1_fun.5 = (f32[512,512]{1,0:T(8,128)S(1)}, f32[512,512]{1,0:T(8,128)S(1)}) custom-call(f32[512,512]{1,0:T(8,128)S(1)} %get-tuple-element.140.refs_0_, f32[512,512]{1,0:T(8,128)S(1)} %get-tuple-element.141.refs_1_, f32[48,512]{1,0:T(8,128)S(1)} %get-tuple-element.142.refs_2_, f32[464,512]{1,0:T(8,128)} %get-tuple-element.143.refs_3_, ...), custom_call_target="tpu_custom_call" | custom-call | flops 1 | bytes 1 | tf_op jit(solution)/shard_map/cond/branch_1_fun/pallas_call | solution.py:103
  88.5 5.2 %collective-permute-done.6 = f32[2,128,512]{2,1,0:T(8,128)S(1)} collective-permute-done((f32[2,128,512]{2,1,0:T(8,128)S(1)}, f32[2,128,512]{2,1,0:T(8,128)S(1)}, u32[]{:S(2)}, u32[]{:S(2)}) %collective-permute-start.6) | collective-permute-done | bytes 524320 | tf_op jit(solution)/shard_map/cond/branch_1_fun/ppermute | solution.py:21
  93.8 1.2 %collective-permute-done.7 = f32[2,128,512]{2,1,0:T(8,128)S(1)} collective-permute-done((f32[2,128,512]{2,1,0:T(8,128)S(1)}, f32[2,128,512]{2,1,0:T(8,128)S(1)}, u32[]{:S(2)}, u32[]{:S(2)}) %collective-permute-start.7) | collective-permute-done | bytes 524320 | tf_op jit(solution)/shard_map/cond/branch_1_fun/ppermute | solution.py:21
  95.1 1.6 %collective-permute-start.8 = (f32[1,128,512]{2,1,0:T(8,128)S(1)}, f32[1,128,512]{2,1,0:T(8,128)S(1)}, u32[]{:S(2)}, u32[]{:S(2)}) collective-permute-start(f32[1,128,512]{2,1,0:T(8,128)S(1)} %get-tuple-element.164), channel_id=1, source_target_pairs={{0,16},{4,20},{8,24},{12,28},{16,0},{20,4},{24,8},{28,12},{1,17},{... | collective-permute-start | bytes 786440 | tf_op jit(solution)/shard_map/cond/branch_1_fun/ppermute | solution.py:21
  96.6 0.5 collective-permute-start.9
  97.2 5.1 %collective-permute-done.8 = f32[1,128,512]{2,1,0:T(8,128)S(1)} collective-permute-done((f32[1,128,512]{2,1,0:T(8,128)S(1)}, f32[1,128,512]{2,1,0:T(8,128)S(1)}, u32[]{:S(2)}, u32[]{:S(2)}) %collective-permute-start.8) | collective-permute-done | bytes 262176 | tf_op jit(solution)/shard_map/cond/branch_1_fun/ppermute | solution.py:21
  102.3 1.2 %collective-permute-done.9 = f32[1,128,512]{2,1,0:T(8,128)S(1)} collective-permute-done((f32[1,128,512]{2,1,0:T(8,128)S(1)}, f32[1,128,512]{2,1,0:T(8,128)S(1)}, u32[]{:S(2)}, u32[]{:S(2)}) %collective-permute-start.9) | collective-permute-done | bytes 262176 | tf_op jit(solution)/shard_map/cond/branch_1_fun/ppermute | solution.py:21
  103.7 1.9 %collective-permute-start.25 = (f32[96,512]{1,0:T(8,128)S(1)}, f32[96,512]{1,0:T(8,128)S(1)}, u32[]{:S(2)}, u32[]{:S(2)}) collective-permute-start(f32[96,512]{1,0:T(8,128)S(1)} %get-tuple-element.295), channel_id=1, source_target_pairs={{0,1},{1,0},{2,3},{3,2},{4,5},{5,4},{6,7},{7,6},{8,9},{9,8},{10,11... | collective-permute-start | bytes 589832 | tf_op jit(solution)/shard_map/ppermute | solution.py:21
  105.7 2.7 %collective-permute-done.23.late_ref = f32[464,512]{1,0:T(8,128)S(1)} collective-permute-done((f32[464,512]{1,0:T(8,128)}, f32[464,512]{1,0:T(8,128)S(1)}, u32[]{:S(2)}, u32[]{:S(2)}) %collective-permute-start.23) | collective-permute-done | bytes 950304 | tf_op jit(solution)/shard_map/ppermute | solution.py:21
  108.4 1.1 shard_map.105
  109.5 1.1 shard_map.106
  110.7 1.0 collective-permute-done.26.refs_4_
  111.7 1.4 %shard_map.107 = (f32[1,3,64,512]{3,2,1,0:T(8,128)}, f32[1,64,256]{2,1,0:T(8,128)}, f32[1,32,512]{2,1,0:T(8,128)}) custom-call(s32[1,2]{1,0:T(1,128)S(1)} %copy-done, f32[64,512]{1,0:T(8,128)S(1)} %copy-done.24, f32[128,512]{1,0:T(8,128)S(1)} %get-tuple-element.294.refs_2_, f32[96,512]{1,0:T(8,128)S(1)} %collective-permute-done.25.refs_3_, ...), custom_call_target="tpu_custom_call" | custom-call | flops 1 | bytes 1 | tf_op jit(solution)/shard_map/pallas_call | solution.py:103
  (101 shorter events, 4.2 us)
Async XLA Ops:
  0.6 12.4 %copy-start.1 = (f32[512,512]{1,0:T(8,128)S(1)}, f32[512,512]{1,0:T(8,128)}, u32[]{:S(2)}) copy-start(f32[512,512]{1,0:T(8,128)} %refs_0_.2) | copy-start | bytes 3145732
  2.7 16.6 %copy-start.27 = (f32[64,512]{1,0:T(8,128)S(1)}, f32[64,512]{1,0:T(8,128)}, u32[]{:S(2)}) copy-start(f32[64,512]{1,0:T(8,128)} %get-tuple-element.245) | copy-start | bytes 393220
  2.7 16.4 %collective-permute-start.10 = (f32[144,512]{1,0:T(8,128)}, f32[144,512]{1,0:T(8,128)S(1)}, u32[]{:S(2)}, u32[]{:S(2)}) collective-permute-start(f32[144,512]{1,0:T(8,128)} %get-tuple-element.239), channel_id=1, source_target_pairs={{0,1},{1,0},{2,3},{3,2},{4,5},{5,4},{6,7},{7,6},{8,9},{9,8},{10,11... | collective-permute-start | bytes 884744 | tf_op jit(solution)/shard_map/ppermute | solution.py:21
  5.7 10.1 %collective-permute-start.12 = (f32[80,512]{1,0:T(8,128)}, f32[80,512]{1,0:T(8,128)S(1)}, u32[]{:S(2)}, u32[]{:S(2)}) collective-permute-start(f32[80,512]{1,0:T(8,128)} %get-tuple-element.243), channel_id=1, source_target_pairs={{0,2},{1,3},{2,0},{3,1},{4,6},{5,7},{6,4},{7,5},{8,10},{9,11},{10,... | collective-permute-start | bytes 491528 | tf_op jit(solution)/shard_map/ppermute | solution.py:21
  8.3 11.1 %collective-permute-start.13 = (f32[128,512]{1,0:T(8,128)S(1)}, f32[128,512]{1,0:T(8,128)S(1)}, u32[]{:S(2)}, u32[]{:S(2)}) collective-permute-start(f32[128,512]{1,0:T(8,128)S(1)} %get-tuple-element.247), channel_id=1, source_target_pairs={{0,8},{4,12},{8,0},{12,4},{16,24},{20,28},{24,16},{28,20},{1,9},{5... | collective-permute-start | bytes 786440 | tf_op jit(solution)/shard_map/ppermute | solution.py:21
  9.8 12.8 %collective-permute-start.14 = (f32[128,512]{1,0:T(8,128)S(1)}, f32[128,512]{1,0:T(8,128)S(1)}, u32[]{:S(2)}, u32[]{:S(2)}) collective-permute-start(f32[128,512]{1,0:T(8,128)S(1)} %get-tuple-element.247), channel_id=1, source_target_pairs={{0,16},{4,20},{8,24},{12,28},{16,0},{20,4},{24,8},{28,12},{1,17},{... | collective-permute-start | bytes 786440 | tf_op jit(solution)/shard_map/ppermute | solution.py:21
  11.3 11.3 %collective-permute-start.15 = (f32[128,512]{1,0:T(8,128)S(1)}, f32[128,512]{1,0:T(8,128)S(1)}, u32[]{:S(2)}, u32[]{:S(2)}) collective-permute-start(f32[128,512]{1,0:T(8,128)S(1)} %get-tuple-element.247), channel_id=1, source_target_pairs={{0,24},{4,28},{8,16},{12,20},{16,8},{20,12},{24,0},{28,4},{1,25},{... | collective-permute-start | bytes 786440 | tf_op jit(solution)/shard_map/ppermute | solution.py:21
  13.0 20.4 %copy-start.3 = (f32[512,512]{1,0:T(8,128)S(1)}, f32[512,512]{1,0:T(8,128)}, u32[]{:S(2)}) copy-start(f32[512,512]{1,0:T(8,128)} %refs_1_.1) | copy-start | bytes 3145732
  15.8 44.8 %collective-permute-start.20 = (f32[464,512]{1,0:T(8,128)S(1)}, f32[464,512]{1,0:T(8,128)}, u32[]{:S(2)}, u32[]{:S(2)}) collective-permute-start(f32[464,512]{1,0:T(8,128)S(1)} %slice.113.x_ref), channel_id=1, source_target_pairs={{0,2},{1,3},{2,0},{3,1},{4,6},{5,7},{6,4},{7,5},{8,10},{9,11},{10,... | collective-permute-start | bytes 2850824 | tf_op jit(solution)/shard_map/ppermute | solution.py:21
  19.1 41.9 %collective-permute-start.11 = (f32[464,512]{1,0:T(8,128)S(1)}, f32[464,512]{1,0:T(8,128)}, u32[]{:S(2)}, u32[]{:S(2)}) collective-permute-start(f32[464,512]{1,0:T(8,128)S(1)} %slice.110.g_ref), channel_id=1, source_target_pairs={{0,1},{1,0},{2,3},{3,2},{4,5},{5,4},{6,7},{7,6},{8,9},{9,8},{10,11... | collective-permute-start | bytes 2850824 | tf_op jit(solution)/shard_map/ppermute | solution.py:21
  19.3 15.2 %copy-start = (s32[1,2]{1,0:T(1,128)S(1)}, s32[1,2]{1,0:T(1,128)}, u32[]{:S(2)}) copy-start(s32[1,2]{1,0:T(1,128)} %refs_0_.3) | copy-start | bytes 28
  22.7 5.7 %collective-permute-start.16 = (f32[1,96,512]{2,1,0:T(8,128)S(1)}, f32[1,96,512]{2,1,0:T(8,128)S(1)}, u32[]{:S(2)}, u32[]{:S(2)}) collective-permute-start(f32[1,96,512]{2,1,0:T(8,128)S(1)} %get-tuple-element.322), channel_id=1, source_target_pairs={{0,8},{4,12},{8,0},{12,4},{16,24},{20,28},{24,16},{28,20},{1,9},{5... | collective-permute-start | bytes 589832 | tf_op jit(solution)/shard_map/ppermute | solution.py:21
  24.0 5.7 %collective-permute-start.17 = (f32[1,96,512]{2,1,0:T(8,128)S(1)}, f32[1,96,512]{2,1,0:T(8,128)S(1)}, u32[]{:S(2)}, u32[]{:S(2)}) collective-permute-start(f32[1,96,512]{2,1,0:T(8,128)S(1)} %get-tuple-element.321), channel_id=1, source_target_pairs={{0,16},{4,20},{8,24},{12,28},{16,0},{20,4},{24,8},{28,12},{1,17},{... | collective-permute-start | bytes 589832 | tf_op jit(solution)/shard_map/ppermute | solution.py:21
  29.7 8.4 %collective-permute-start.18 = (f32[2,96,512]{2,1,0:T(8,128)S(1)}, f32[2,96,512]{2,1,0:T(8,128)S(1)}, u32[]{:S(2)}, u32[]{:S(2)}) collective-permute-start(f32[2,96,512]{2,1,0:T(8,128)S(1)} %pad_maximum_fusion.4), channel_id=1, source_target_pairs={{0,16},{4,20},{8,24},{12,28},{16,0},{20,4},{24,8},{28,12},{1,17},{... | collective-permute-start | bytes 1179656 | tf_op jit(solution)/shard_map/ppermute | solution.py:21
  30.8 8.4 %collective-permute-start.19 = (f32[2,96,512]{2,1,0:T(8,128)S(1)}, f32[2,96,512]{2,1,0:T(8,128)S(1)}, u32[]{:S(2)}, u32[]{:S(2)}) collective-permute-start(f32[2,96,512]{2,1,0:T(8,128)S(1)} %pad_maximum_fusion.5), channel_id=1, source_target_pairs={{0,8},{4,12},{8,0},{12,4},{16,24},{20,28},{24,16},{28,20},{1,9},{5... | collective-permute-start | bytes 1179656 | tf_op jit(solution)/shard_map/ppermute | solution.py:21
  34.6 4.6 %copy-start.19 = (f32[48,512]{1,0:T(8,128)}, f32[48,512]{1,0:T(8,128)S(1)}, u32[]{:S(2)}) copy-start(f32[48,512]{1,0:T(8,128)S(1)} %slice.117) | copy-start | bytes 294916
  34.6 4.5 %copy-start.21 = (f32[48,512]{1,0:T(8,128)}, f32[48,512]{1,0:T(8,128)S(1)}, u32[]{:S(2)}) copy-start(f32[48,512]{1,0:T(8,128)S(1)} %slice.111) | copy-start | bytes 294916
  39.7 5.7 %collective-permute-start.1 = (f32[4,320,512]{2,1,0:T(8,128)S(1)}, f32[4,320,512]{2,1,0:T(8,128)S(1)}, u32[]{:S(2)}, u32[]{:S(2)}) collective-permute-start(f32[4,320,512]{2,1,0:T(8,128)S(1)} %pad_maximum_fusion.refs_0_), channel_id=1, source_target_pairs={{0,4},{4,0},{8,12},{12,8},{16,20},{20,16},{24,28},{28,24},{1,5},{5... | collective-permute-start | bytes 7864328 | tf_op jit(solution)/shard_map/cond/branch_1_fun/ppermute | solution.py:21
  39.8 5.6 %collective-permute-start = (f32[4,64,512]{2,1,0:T(8,128)S(1)}, f32[4,64,512]{2,1,0:T(8,128)S(1)}, u32[]{:S(2)}, u32[]{:S(2)}) collective-permute-start(f32[4,64,512]{2,1,0:T(8,128)S(1)} %get-tuple-element.91), channel_id=1, source_target_pairs={{0,4},{4,0},{8,12},{12,8},{16,20},{20,16},{24,28},{28,24},{1,5},{5... | collective-permute-start | bytes 1572872 | tf_op jit(solution)/shard_map/cond/branch_1_fun/ppermute | solution.py:21
  45.5 7.3 %collective-permute-start.4 = (f32[64,512]{1,0:T(8,128)S(1)}, f32[64,512]{1,0:T(8,128)S(1)}, u32[]{:S(2)}, u32[]{:S(2)}) collective-permute-start(f32[64,512]{1,0:T(8,128)S(1)} %get-tuple-element.301), channel_id=1, source_target_pairs={{0,24},{4,28},{8,16},{12,20},{16,8},{20,12},{24,0},{28,4},{1,25},{... | collective-permute-start | bytes 393224 | tf_op jit(solution)/shard_map/cond/branch_1_fun/ppermute | solution.py:21
  47.0 7.8 %collective-permute-start.3 = (f32[64,512]{1,0:T(8,128)S(1)}, f32[64,512]{1,0:T(8,128)S(1)}, u32[]{:S(2)}, u32[]{:S(2)}) collective-permute-start(f32[64,512]{1,0:T(8,128)S(1)} %get-tuple-element.302), channel_id=1, source_target_pairs={{0,16},{4,20},{8,24},{12,28},{16,0},{20,4},{24,8},{28,12},{1,17},{... | collective-permute-start | bytes 393224 | tf_op jit(solution)/shard_map/cond/branch_1_fun/ppermute | solution.py:21
  49.0 5.8 %collective-permute-start.2 = (f32[64,512]{1,0:T(8,128)S(1)}, f32[64,512]{1,0:T(8,128)S(1)}, u32[]{:S(2)}, u32[]{:S(2)}) collective-permute-start(f32[64,512]{1,0:T(8,128)S(1)} %get-tuple-element.300), channel_id=1, source_target_pairs={{0,8},{4,12},{8,0},{12,4},{16,24},{20,28},{24,16},{28,20},{1,9},{5... | collective-permute-start | bytes 393224 | tf_op jit(solution)/shard_map/cond/branch_1_fun/ppermute | solution.py:21
  54.9 6.1 %copy-start.9 = (bf16[2,512,256]{2,1,0:T(8,128)(2,1)}, bf16[2,512,256]{2,1,0:T(8,128)(2,1)S(1)}, u32[]{:S(2)}) copy-start(bf16[2,512,256]{2,1,0:T(8,128)(2,1)S(1)} %get-tuple-element.263.ll) | copy-start | bytes 1572868
  54.9 6.0 %copy-start.11 = (bf16[2,256,512]{2,1,0:T(8,128)(2,1)}, bf16[2,256,512]{2,1,0:T(8,128)(2,1)S(1)}, u32[]{:S(2)}) copy-start(bf16[2,256,512]{2,1,0:T(8,128)(2,1)S(1)} %get-tuple-element.264.rh) | copy-start | bytes 1572868
  54.9 6.0 %copy-start.13 = (bf16[2,256,512]{2,1,0:T(8,128)(2,1)}, bf16[2,256,512]{2,1,0:T(8,128)(2,1)S(1)}, u32[]{:S(2)}) copy-start(bf16[2,256,512]{2,1,0:T(8,128)(2,1)S(1)} %get-tuple-element.265.rl) | copy-start | bytes 1572868
  54.9 13.1 %collective-permute-start.21 = (f32[48,512]{1,0:T(8,128)S(1)}, f32[48,512]{1,0:T(8,128)S(1)}, u32[]{:S(2)}, u32[]{:S(2)}) collective-permute-start(f32[48,512]{1,0:T(8,128)S(1)} %get-tuple-element.273), channel_id=1, source_target_pairs={{0,1},{1,0},{2,3},{3,2},{4,5},{5,4},{6,7},{7,6},{8,9},{9,8},{10,11... | collective-permute-start | bytes 294920 | tf_op jit(solution)/shard_map/ppermute | solution.py:21
  55.4 12.6 %collective-permute-start.22 = (f32[48,512]{1,0:T(8,128)S(1)}, f32[48,512]{1,0:T(8,128)S(1)}, u32[]{:S(2)}, u32[]{:S(2)}) collective-permute-start(f32[48,512]{1,0:T(8,128)S(1)} %get-tuple-element.274), channel_id=1, source_target_pairs={{0,2},{1,3},{2,0},{3,1},{4,6},{5,7},{6,4},{7,5},{8,10},{9,11},{10,... | collective-permute-start | bytes 294920 | tf_op jit(solution)/shard_map/ppermute | solution.py:21
  55.5 13.7 %copy-start.20 = (f32[48,512]{1,0:T(8,128)S(1)}, f32[48,512]{1,0:T(8,128)}, u32[]{:S(2)}) copy-start(f32[48,512]{1,0:T(8,128)} %copy-done.19) | copy-start | bytes 294916
  55.5 13.7 %copy-start.22 = (f32[48,512]{1,0:T(8,128)S(1)}, f32[48,512]{1,0:T(8,128)}, u32[]{:S(2)}) copy-start(f32[48,512]{1,0:T(8,128)} %copy-done.21) | copy-start | bytes 294916
  61.0 8.3 %copy-start.2 = (f32[512,512]{1,0:T(8,128)S(1)}, f32[512,512]{1,0:T(8,128)}, u32[]{:S(2)}) copy-start(f32[512,512]{1,0:T(8,128)} %refs_0_.2) | copy-start | bytes 3145732
  61.0 8.3 %copy-start.4 = (f32[512,512]{1,0:T(8,128)S(1)}, f32[512,512]{1,0:T(8,128)}, u32[]{:S(2)}) copy-start(f32[512,512]{1,0:T(8,128)} %refs_1_.1) | copy-start | bytes 3145732
  61.0 8.2 %copy-start.6 = (bf16[2,512,512]{2,1,0:T(8,128)(2,1)S(1)}, bf16[2,512,512]{2,1,0:T(8,128)(2,1)}, u32[]{:S(2)}) copy-start(bf16[2,512,512]{2,1,0:T(8,128)(2,1)} %copy-done.5) | copy-start | bytes 3145732
  61.0 8.2 %copy-start.8 = (bf16[2,512,512]{2,1,0:T(8,128)(2,1)S(1)}, bf16[2,512,512]{2,1,0:T(8,128)(2,1)}, u32[]{:S(2)}) copy-start(bf16[2,512,512]{2,1,0:T(8,128)(2,1)} %copy-done.7) | copy-start | bytes 3145732
  61.0 8.2 %copy-start.10 = (bf16[2,512,256]{2,1,0:T(8,128)(2,1)S(1)}, bf16[2,512,256]{2,1,0:T(8,128)(2,1)}, u32[]{:S(2)}) copy-start(bf16[2,512,256]{2,1,0:T(8,128)(2,1)} %copy-done.9) | copy-start | bytes 1572868
  61.0 8.2 %copy-start.12 = (bf16[2,256,512]{2,1,0:T(8,128)(2,1)S(1)}, bf16[2,256,512]{2,1,0:T(8,128)(2,1)}, u32[]{:S(2)}) copy-start(bf16[2,256,512]{2,1,0:T(8,128)(2,1)} %copy-done.11) | copy-start | bytes 1572868
  61.0 8.2 %copy-start.14 = (bf16[2,256,512]{2,1,0:T(8,128)(2,1)S(1)}, bf16[2,256,512]{2,1,0:T(8,128)(2,1)}, u32[]{:S(2)}) copy-start(bf16[2,256,512]{2,1,0:T(8,128)(2,1)} %copy-done.13) | copy-start | bytes 1572868
  61.0 8.2 %copy-start.16 = (bf16[1,512,512]{2,1,0:T(8,128)(2,1)S(1)}, bf16[1,512,512]{2,1,0:T(8,128)(2,1)}, u32[]{:S(2)}) copy-start(bf16[1,512,512]{2,1,0:T(8,128)(2,1)} %copy-done.15) | copy-start | bytes 1572868
  61.0 8.2 %copy-start.18 = (bf16[1,512,512]{2,1,0:T(8,128)(2,1)S(1)}, bf16[1,512,512]{2,1,0:T(8,128)(2,1)}, u32[]{:S(2)}) copy-start(bf16[1,512,512]{2,1,0:T(8,128)(2,1)} %copy-done.17) | copy-start | bytes 1572868
  65.4 43.0 %collective-permute-start.23 = (f32[464,512]{1,0:T(8,128)}, f32[464,512]{1,0:T(8,128)S(1)}, u32[]{:S(2)}, u32[]{:S(2)}) collective-permute-start(f32[464,512]{1,0:T(8,128)} %get-tuple-element.279), channel_id=1, source_target_pairs={{0,1},{1,0},{2,3},{3,2},{4,5},{5,4},{6,7},{7,6},{8,9},{9,8},{10,11... | collective-permute-start | bytes 2850824 | tf_op jit(solution)/shard_map/ppermute | solution.py:21
  68.0 41.5 %collective-permute-start.24 = (f32[464,512]{1,0:T(8,128)S(1)}, f32[464,512]{1,0:T(8,128)S(1)}, u32[]{:S(2)}, u32[]{:S(2)}) collective-permute-start(f32[464,512]{1,0:T(8,128)S(1)} %get-tuple-element.289), channel_id=1, source_target_pairs={{0,2},{1,3},{2,0},{3,1},{4,6},{5,7},{6,4},{7,5},{8,10},{9,11},{10,... | collective-permute-start | bytes 2850824 | tf_op jit(solution)/shard_map/ppermute | solution.py:21
  69.5 5.3 %copy-start.25 = (f32[48,256]{1,0:T(8,128)}, f32[48,256]{1,0:T(8,128)S(1)}, u32[]{:S(2)}) copy-start(f32[48,256]{1,0:T(8,128)S(1)} %get-tuple-element.146.refs_6_) | copy-start | bytes 147460 | tf_op jit(solution)/shard_map/cond
  74.8 4.2 %collective-permute-start.5 = (f32[4,256,512]{2,1,0:T(8,128)S(1)}, f32[4,256,512]{2,1,0:T(8,128)S(1)}, u32[]{:S(2)}, u32[]{:S(2)}) collective-permute-start(f32[4,256,512]{2,1,0:T(8,128)S(1)} %get-tuple-element.135), channel_id=1, source_target_pairs={{0,4},{4,0},{8,12},{12,8},{16,20},{20,16},{24,28},{28,24},{1,5},{5... | collective-permute-start | bytes 6291464 | tf_op jit(solution)/shard_map/cond/branch_1_fun/ppermute | solution.py:21
  79.7 14.0 %collective-permute-start.6 = (f32[2,128,512]{2,1,0:T(8,128)S(1)}, f32[2,128,512]{2,1,0:T(8,128)S(1)}, u32[]{:S(2)}, u32[]{:S(2)}) collective-permute-start(f32[2,128,512]{2,1,0:T(8,128)S(1)} %pad_maximum_fusion.1), channel_id=1, source_target_pairs={{0,8},{4,12},{8,0},{12,4},{16,24},{20,28},{24,16},{28,20},{1,9},{5... | collective-permute-start | bytes 1572872 | tf_op jit(solution)/shard_map/cond/branch_1_fun/ppermute | solution.py:21
  81.3 13.7 %collective-permute-start.7 = (f32[2,128,512]{2,1,0:T(8,128)S(1)}, f32[2,128,512]{2,1,0:T(8,128)S(1)}, u32[]{:S(2)}, u32[]{:S(2)}) collective-permute-start(f32[2,128,512]{2,1,0:T(8,128)S(1)} %pad_maximum_fusion.2), channel_id=1, source_target_pairs={{0,16},{4,20},{8,24},{12,28},{16,0},{20,4},{24,8},{28,12},{1,17},{... | collective-permute-start | bytes 1572872 | tf_op jit(solution)/shard_map/cond/branch_1_fun/ppermute | solution.py:21
  95.1 7.3 %collective-permute-start.8 = (f32[1,128,512]{2,1,0:T(8,128)S(1)}, f32[1,128,512]{2,1,0:T(8,128)S(1)}, u32[]{:S(2)}, u32[]{:S(2)}) collective-permute-start(f32[1,128,512]{2,1,0:T(8,128)S(1)} %get-tuple-element.164), channel_id=1, source_target_pairs={{0,16},{4,20},{8,24},{12,28},{16,0},{20,4},{24,8},{28,12},{1,17},{... | collective-permute-start | bytes 786440 | tf_op jit(solution)/shard_map/cond/branch_1_fun/ppermute | solution.py:21
  96.6 6.9 %collective-permute-start.9 = (f32[1,128,512]{2,1,0:T(8,128)S(1)}, f32[1,128,512]{2,1,0:T(8,128)S(1)}, u32[]{:S(2)}, u32[]{:S(2)}) collective-permute-start(f32[1,128,512]{2,1,0:T(8,128)S(1)} %get-tuple-element.165), channel_id=1, source_target_pairs={{0,8},{4,12},{8,0},{12,4},{16,24},{20,28},{24,16},{28,20},{1,9},{5... | collective-permute-start | bytes 786440 | tf_op jit(solution)/shard_map/cond/branch_1_fun/ppermute | solution.py:21
  103.7 7.9 %collective-permute-start.25 = (f32[96,512]{1,0:T(8,128)S(1)}, f32[96,512]{1,0:T(8,128)S(1)}, u32[]{:S(2)}, u32[]{:S(2)}) collective-permute-start(f32[96,512]{1,0:T(8,128)S(1)} %get-tuple-element.295), channel_id=1, source_target_pairs={{0,1},{1,0},{2,3},{3,2},{4,5},{5,4},{6,7},{7,6},{8,9},{9,8},{10,11... | collective-permute-start | bytes 589832 | tf_op jit(solution)/shard_map/ppermute | solution.py:21
  105.7 6.0 %collective-permute-start.26 = (f32[32,512]{1,0:T(8,128)S(1)}, f32[32,512]{1,0:T(8,128)S(1)}, u32[]{:S(2)}, u32[]{:S(2)}) collective-permute-start(f32[32,512]{1,0:T(8,128)S(1)} %get-tuple-element.296), channel_id=1, source_target_pairs={{0,2},{1,3},{2,0},{3,1},{4,6},{5,7},{6,4},{7,5},{8,10},{9,11},{10,... | collective-permute-start | bytes 196616 | tf_op jit(solution)/shard_map/ppermute | solution.py:21
  (7 other events, 21.8 us)
